TPU v7x, 32 devices: a whole 2x2x4 slice. The times are simulated.
32 devices in a mesh: pipe: 2 (over x), dp: 4 (over z), tensor: 4 (over y, core).
Axes of the slice: x: 2, y: 2, z: 4, core: 2. Of those that a mesh axis runs over, the one named last changes fastest.
Arguments:
- layer_inputs: bfloat16 [2, 480, 8, 768], P('pipe', 'tensor', 'dp'), may hold values from -6 to 6
- segment_ids: int32 [2, 8, 480], P(None, 'dp'), may hold values from 0 to 23, never falling along the last dimension, each value on 1 to 40 neighbouring positions
- slot_ids: int32 [480, 8], P('tensor', 'dp'), may hold values from 0 to 4095
- memory_table: bfloat16 [4096, 768], replicated, may hold values from -6 to 6
- buckets: int32 [960], replicated, may hold values from 0 to 31, as said below
- self_qkv: bfloat16 [2, 768, 3, 768], P('pipe', 'dp', None, 'tensor'), may hold values from -0.21875 to 0.21875
- self_out: bfloat16 [2, 768, 768], P('pipe', 'tensor', 'dp'), may hold values from -0.875 to 0.875
- source_kv: bfloat16 [2, 768, 2, 768], P('pipe', 'dp', None, 'tensor'), may hold values from -0.21875 to 0.21875
- ff_in: bfloat16 [2, 768, 3072], P('pipe', 'dp', 'tensor'), may hold values from -0.21875 to 0.21875
- ff_out: bfloat16 [2, 3072, 768], P('pipe', 'tensor', 'dp'), may hold values from -0.109375 to 0.109375
- rel_bias: bfloat16 [2, 32, 12], P('pipe', 'dp', 'tensor'), may hold values from -4 to 4
- gains: bfloat16 [2, 3, 768], P('pipe', None, 'dp'), may hold values from 0.5 to 1.5
- cross_query: bfloat16 [768, 768], P(('pipe', 'dp'), 'tensor'), may hold values from -0.21875 to 0.21875
- cross_out: bfloat16 [768, 768], P('tensor', ('pipe', 'dp')), may hold values from -0.875 to 0.875
- cross_gain: bfloat16 [768], P(('pipe', 'dp')), may hold values from 0.5 to 1.5
- cotangents: bfloat16 [2, 480, 8, 768], P('pipe', 'tensor', 'dp'), may hold values from -6 to 6
Outputs:
- section_outputs: bfloat16 [2, 480, 8, 768], P('pipe', 'tensor', 'dp')
- input_grads: float32 [2, 480, 8, 768], P('pipe', 'tensor', 'dp')
- grad_self_qkv: float32 [2, 768, 3, 768], P('pipe', 'dp', None, 'tensor')
- grad_self_out: float32 [2, 768, 768], P('pipe', 'tensor', 'dp')
- grad_source_kv: float32 [2, 768, 2, 768], P('pipe', 'dp', None, 'tensor')
- grad_ff_in: float32 [2, 768, 3072], P('pipe', 'dp', 'tensor')
- grad_ff_out: float32 [2, 3072, 768], P('pipe', 'tensor', 'dp')
- grad_rel_bias: float32 [2, 32, 12], P('pipe', 'dp', 'tensor')
- grad_gains: float32 [2, 3, 768], P('pipe', None, 'dp')
- grad_cross_query: float32 [768, 768], P(('pipe', 'dp'), 'tensor')
- grad_cross_out: float32 [768, 768], P('tensor', ('pipe', 'dp'))
- grad_cross_gain: float32 [768], P(('pipe', 'dp'))
Inputs may be any that keep to these rules, and one draw needn't show every extreme that they name: Entry o + 480 is the bucket of the offset o (key position minus query position) for -480 < o < 480; entry 0 is not read. Offsets below zero take buckets under 32/2, the others 32/2 and up; the bucket never falls as |o| grows.
All inputs are finite; a program needn't handle non-finite values.
Results may differ from a plain program's by a relative error of at most 0.025.
Values may be sent and summed in bfloat16 or wider, within the bound.
A program may use at most 192 MiB of HBM per device.

v0:
```python
import jax
import jax.numpy as jnp
from jax import lax
from jax.sharding import PartitionSpec as P

HD = 64
NB = 32
MEM = 20
MICRO = 2


EPSILON = 1e-06
HIGHEST = lax.Precision.HIGHEST


def from_behind(array, axis, by):
    count = lax.axis_size(axis)
    pairs = [(i, i + by) for i in range(count) if 0 <= i + by < count]
    return lax.ppermute(array, axis, pairs)


def norm_apply(values, gain):
    return values * lax.rsqrt(jnp.mean(values * values, axis=-1, keepdims=True) + EPSILON) * gain


def norm_back(values, gain, grad_normed):
    _, pullback = jax.vjp(norm_apply, values, gain)
    return pullback(grad_normed)


def offset_index(first_row, row_count, seq_width):
    query_pos = first_row + jnp.arange(row_count, dtype=jnp.int32)[:, None]
    key_pos = jnp.arange(seq_width, dtype=jnp.int32)[None, :]
    return key_pos - query_pos + seq_width


def project(left, weight):
    return jnp.einsum("qre,ed->qrd", left, weight, preferred_element_type=jnp.float32)


def project_back(left, weight):
    return jnp.einsum("qrd,ed->qre", left, weight, preferred_element_type=jnp.float32)


def contract(left, right):
    return jnp.einsum("qre,qrd->ed", left, right, preferred_element_type=jnp.float32)


def diagonal_sums(block_grads, first_row, seq_width):
    head_count, query_count, key_count = block_grads.shape
    flipped = block_grads[:, ::-1, :]
    padded_width = key_count + query_count
    padded = jnp.pad(flipped, ((0, 0), (0, 0), (0, query_count)))
    skewed = padded.reshape(head_count, query_count * padded_width)[
        :, : query_count * (padded_width - 1)
    ]
    skewed = skewed.reshape(head_count, query_count, padded_width - 1)
    column_sums = jnp.sum(skewed, axis=1)
    lead_pad = seq_width - first_row - (query_count - 1)
    tail_pad = 2 * seq_width - lead_pad - (padded_width - 1)
    return jnp.pad(column_sums, ((0, 0), (lead_pad, tail_pad)))


def block_scores(query_blk, key_rows, offset_bias, allowed, first_row, seq_width):
    row_count, key_len = (query_blk.shape[0], key_rows.shape[0])
    scale = query_blk.shape[3] ** (-0.5)
    scores = (
        jnp.einsum("qrhd,krhd->rhqk", query_blk, key_rows, preferred_element_type=jnp.float32)
        * scale
    )
    if offset_bias is not None:
        own_part = offset_bias[:, offset_index(first_row, row_count, seq_width)]
        lead_part = jnp.zeros((own_part.shape[0], row_count, key_len - seq_width), jnp.float32)
        scores = scores + jnp.concatenate([lead_part, own_part], -1)[None]
    return jnp.where(allowed(first_row, row_count)[:, None], scores, -1000000000.0)


def attend(queries, key_rows, values, offset_bias, allowed):
    seq_width = queries.shape[0]
    half = seq_width // 2
    results = []
    logsums = []
    for part_no in range(2):
        first_row = part_no * half
        scores = block_scores(
            queries[first_row : first_row + half],
            key_rows,
            offset_bias,
            allowed,
            first_row,
            seq_width,
        )
        maximum = jnp.max(scores, axis=-1, keepdims=True)
        expscores = jnp.exp(scores - maximum)
        denominator = jnp.sum(expscores, axis=-1, keepdims=True)
        weights = (expscores / denominator).astype(jnp.bfloat16)
        results.append(
            jnp.einsum("rhqk,krhd->qrhd", weights, values, preferred_element_type=jnp.float32)
        )
        logsums.append((maximum + jnp.log(denominator))[..., 0])
    mixed = jnp.concatenate(results, 0)
    return (
        mixed.reshape(mixed.shape[0], mixed.shape[1], -1).astype(jnp.bfloat16),
        jnp.concatenate(logsums, -1),
    )


def attend_back(queries, key_rows, values, grad_mixed, logsums, offset_bias, allowed):
    seq_width = queries.shape[0]
    key_len = key_rows.shape[0]
    half = seq_width // 2
    scale = queries.shape[3] ** (-0.5)
    grad_heads = grad_mixed.reshape(queries.shape)
    grad_query = []
    grad_key = jnp.zeros(key_rows.shape, jnp.float32)
    grad_value = jnp.zeros(values.shape, jnp.float32)
    grad_bias = None
    if offset_bias is not None:
        grad_bias = jnp.zeros(offset_bias.shape, jnp.float32)
    for part_no in range(2):
        first_row = part_no * half
        query_blk = queries[first_row : first_row + half]
        grad_blk = grad_heads[first_row : first_row + half]
        scores = block_scores(query_blk, key_rows, offset_bias, allowed, first_row, seq_width)
        probability = jnp.exp(scores - logsums[:, :, first_row : first_row + half, None])
        grad_probs = jnp.einsum(
            "qrhd,krhd->rhqk", grad_blk, values, preferred_element_type=jnp.float32
        )
        row_inner = jnp.sum(probability * grad_probs, axis=-1, keepdims=True)
        grad_scores = (probability * (grad_probs - row_inner)).astype(jnp.bfloat16)
        grad_query.append(
            jnp.einsum("rhqk,krhd->qrhd", grad_scores, key_rows, preferred_element_type=jnp.float32)
            * scale
        )
        grad_key = (
            grad_key
            + jnp.einsum(
                "rhqk,qrhd->krhd", grad_scores, query_blk, preferred_element_type=jnp.float32
            )
            * scale
        )
        grad_value = grad_value + jnp.einsum(
            "rhqk,qrhd->krhd",
            probability.astype(jnp.bfloat16),
            grad_blk,
            preferred_element_type=jnp.float32,
        )
        if offset_bias is not None:
            own_grads = jnp.sum(grad_scores.astype(jnp.float32), axis=0)[..., key_len - seq_width :]
            grad_bias = grad_bias + diagonal_sums(own_grads, first_row, seq_width)
    return (jnp.concatenate(grad_query, 0), grad_key, grad_value, grad_bias)


def body(
    layer_inputs,
    segment_ids,
    slot_ids,
    memory_table,
    buckets,
    self_qkv,
    self_out,
    source_kv,
    ff_in,
    ff_out,
    rel_bias,
    gains,
    cross_query,
    cross_out,
    cross_gain,
    cotangents,
):
    section = lax.axis_index("pipe")
    encoder = section == 0
    shard_len = layer_inputs.shape[1]
    seq_width = segment_ids.shape[2]
    micro_rows = layer_inputs.shape[2] // MICRO
    model_width = layer_inputs.shape[3]
    positions = jnp.arange(seq_width, dtype=jnp.int32)
    bucket_hot = (buckets[:, None] == jnp.arange(NB, dtype=jnp.int32)[None, :]).astype(jnp.float32)

    def fetch_weights():
        fetched = (
            lax.all_gather(self_qkv, "dp", axis=1, tiled=True),
            lax.all_gather(self_out, "dp", axis=2, tiled=True),
            lax.all_gather(source_kv, "dp", axis=1, tiled=True),
            lax.all_gather(ff_in, "dp", axis=1, tiled=True),
            lax.all_gather(ff_out, "dp", axis=2, tiled=True),
            lax.all_gather(rel_bias, "dp", axis=1, tiled=True),
            lax.all_gather(gains, "dp", axis=2, tiled=True),
        )
        extra = (
            lax.all_gather(cross_query, ("pipe", "dp"), axis=0, tiled=True),
            lax.all_gather(cross_out, ("pipe", "dp"), axis=1, tiled=True),
            lax.all_gather(cross_gain, ("pipe", "dp"), axis=0, tiled=True),
        )
        return tuple((member[0] for member in fetched)) + tuple(extra)

    def spread(rows_part):
        return lax.all_gather(rows_part, "tensor", axis=0, tiled=True)

    def spread_grad(rows_part):
        return lax.all_gather(rows_part, "tensor", axis=0, tiled=True)

    def collect(left, weight):

        def term_rows(first_row, row_count):
            return project(left, weight)

        return lax.psum_scatter(
            term_rows(jnp.int32(0), lax.axis_size("tensor") * shard_len),
            "tensor",
            scatter_dimension=0,
            tiled=True,
        )

    def collect_grad(left, weight):

        def term_rows(first_row, row_count):
            return project_back(left, weight)

        return lax.psum_scatter(
            term_rows(jnp.int32(0), lax.axis_size("tensor") * shard_len),
            "tensor",
            scatter_dimension=0,
            tiled=True,
        )

    def masks(batch_no):
        seg_rows = lax.dynamic_slice_in_dim(segment_ids, batch_no * micro_rows, micro_rows, 1)
        own_seg = lax.dynamic_index_in_dim(seg_rows, section, 0, keepdims=False)
        source_seg = jnp.where(encoder, (positions // MEM)[None, :], seg_rows[0])

        def allow_self(first_row, row_count):
            query_seg = lax.dynamic_slice_in_dim(own_seg, first_row, row_count, 1)
            query_pos = first_row + jnp.arange(row_count, dtype=jnp.int32)
            ordered = encoder | (positions[None, :] <= query_pos[:, None])
            prefix = encoder & (query_seg[:, :, None] == source_seg[:, None, :])
            own_keys = (query_seg[:, :, None] == own_seg[:, None, :]) & ordered[None]
            return jnp.concatenate([prefix, own_keys], 2)

        def allow_cross(first_row, row_count):
            query_seg = lax.dynamic_slice_in_dim(own_seg, first_row, row_count, 1)
            return query_seg[:, :, None] == source_seg[:, None, :]

        return (allow_self, allow_cross)

    received = jnp.zeros((shard_len, micro_rows, model_width), jnp.bfloat16)
    section_out = jnp.zeros(layer_inputs.shape[1:], jnp.bfloat16)
    saved = []
    for step_no in range(MICRO + 1):
        batch_no = jnp.clip(step_no - section, 0, MICRO - 1)
        valid = (step_no - section >= 0) & (step_no - section < MICRO)
        weights = fetch_weights()
        row_first = batch_no * micro_rows
        x_in = lax.dynamic_slice_in_dim(layer_inputs[0], row_first, micro_rows, 1).astype(
            jnp.float32
        )
        slot_rows = lax.dynamic_slice_in_dim(slot_ids, row_first, micro_rows, 1)
        src_raw = jnp.where(encoder, memory_table[slot_rows], received).astype(jnp.float32)
        allow_self, allow_cross = masks(batch_no)
        (
            forward_w_qkv,
            forward_w_out,
            forward_w_kv,
            forward_w_in,
            forward_w_ffo,
            forward_rel_rows,
            forward_gain_rows,
            forward_w_query,
            forward_w_cross,
            forward_gain_cross,
        ) = weights
        forward_gain_all = forward_gain_rows.astype(jnp.float32)
        forward_gain_x = forward_gain_cross.astype(jnp.float32)
        forward_offset_bias = jnp.dot(
            bucket_hot,
            forward_rel_rows.astype(jnp.float32),
            precision=HIGHEST,
            preferred_element_type=jnp.float32,
        ).T
        forward_flat_qkv = forward_w_qkv.reshape(model_width, -1)
        head_count = forward_flat_qkv.shape[1] // 3 // HD
        forward_rows_a = spread(norm_apply(x_in, forward_gain_all[0]).astype(jnp.bfloat16))
        forward_split_qkv = (
            project(forward_rows_a, forward_flat_qkv)
            .astype(jnp.bfloat16)
            .reshape(seq_width, micro_rows, 3, head_count, HD)
        )
        forward_rows_s = lax.all_gather(
            norm_apply(src_raw, forward_gain_all[2]).astype(jnp.bfloat16),
            "tensor",
            axis=0,
            tiled=True,
        )
        forward_kv_src = (
            project(forward_rows_s, forward_w_kv.reshape(model_width, -1))
            .astype(jnp.bfloat16)
            .reshape(seq_width, micro_rows, 2, head_count, HD)
        )
        forward_keys_a = jnp.concatenate([forward_kv_src[:, :, 0], forward_split_qkv[:, :, 1]], 0)
        forward_values_a = jnp.concatenate([forward_kv_src[:, :, 1], forward_split_qkv[:, :, 2]], 0)
        forward_mixed_a, forward_logsums_a = attend(
            forward_split_qkv[:, :, 0],
            forward_keys_a,
            forward_values_a,
            forward_offset_bias,
            allow_self,
        )
        forward_x_mid = x_in + collect(forward_mixed_a, forward_w_out)
        forward_rows_b = spread(norm_apply(forward_x_mid, forward_gain_x).astype(jnp.bfloat16))
        forward_query_b = (
            project(forward_rows_b, forward_w_query)
            .astype(jnp.bfloat16)
            .reshape(seq_width, micro_rows, head_count, HD)
        )
        forward_mixed_b, forward_logsums_b = attend(
            forward_query_b, forward_kv_src[:, :, 0], forward_kv_src[:, :, 1], None, allow_cross
        )
        forward_x_late = forward_x_mid + jnp.where(
            encoder, 0.0, collect(forward_mixed_b, forward_w_cross)
        )
        forward_rows_c = spread(
            norm_apply(forward_x_late, forward_gain_all[1]).astype(jnp.bfloat16)
        )
        forward_pre_act = project(forward_rows_c, forward_w_in)
        forward_hidden = jax.nn.gelu(forward_pre_act).astype(jnp.bfloat16)
        result = forward_x_late + collect(forward_hidden, forward_w_ffo)
        forward_kept = (
            x_in,
            src_raw,
            forward_x_mid,
            forward_x_late,
            forward_rows_a,
            forward_split_qkv,
            forward_keys_a,
            forward_values_a,
            forward_mixed_a,
            forward_logsums_a,
            forward_rows_b,
            forward_rows_s,
            forward_query_b,
            forward_kv_src,
            forward_mixed_b,
            forward_logsums_b,
            forward_rows_c,
            forward_pre_act,
            forward_hidden,
            forward_offset_bias,
        )
        result, kept = (result, forward_kept)
        sent = result.astype(jnp.bfloat16)
        section_out = jnp.where(
            valid, lax.dynamic_update_slice_in_dim(section_out, sent, row_first, 1), section_out
        )
        received = from_behind(sent, "pipe", 1)
        saved.append((kept, batch_no, valid))
    grad_back = jnp.zeros((shard_len, micro_rows, model_width), jnp.bfloat16)
    input_grads = jnp.zeros(layer_inputs.shape[1:], jnp.float32)
    offset_total = None
    totals = None
    cross_totals = None
    for back_no in range(MICRO + 1):
        kept, batch_no, valid = saved[MICRO - back_no]
        weights = fetch_weights()
        row_first = batch_no * micro_rows
        cotangent = lax.dynamic_slice_in_dim(cotangents[0], row_first, micro_rows, 1).astype(
            jnp.float32
        )
        grad_out = cotangent + grad_back.astype(jnp.float32)
        allow_self, allow_cross = masks(batch_no)
        w_qkv, w_out, w_kv, w_in, w_ffo, rel_rows, gain_rows, w_query, w_cross, gain_cross = weights
        gain_all = gain_rows.astype(jnp.float32)
        gain_x = gain_cross.astype(jnp.float32)
        (
            backward_x_in,
            backward_src_raw,
            x_mid,
            x_late,
            rows_a,
            split_qkv,
            keys_a,
            values_a,
            mixed_a,
            logsums_a,
            rows_b,
            rows_s,
            query_b,
            kv_src,
            mixed_b,
            logsums_b,
            rows_c,
            pre_act,
            hidden,
            offset_bias,
        ) = kept
        grad_c = spread_grad(grad_out.astype(jnp.bfloat16))
        grad_ffo = contract(hidden, grad_c)
        grad_hidden = project_back(grad_c, w_ffo)
        _, gelu_pull = jax.vjp(jax.nn.gelu, pre_act)
        grad_pre = gelu_pull(grad_hidden)[0].astype(jnp.bfloat16)
        grad_in_w = contract(rows_c, grad_pre)
        dx_late, dgain_c = norm_back(x_late, gain_all[1], collect_grad(grad_pre, w_in))
        grad_late = grad_out + dx_late
        grad_b = spread_grad(jnp.where(encoder, 0.0, grad_late).astype(jnp.bfloat16))
        grad_cross = contract(mixed_b, grad_b)
        grad_mixed_b = project_back(grad_b, w_cross).astype(jnp.bfloat16)
        dq_b, dk_b, dv_b, _ = attend_back(
            query_b, kv_src[:, :, 0], kv_src[:, :, 1], grad_mixed_b, logsums_b, None, allow_cross
        )
        grad_query_b = dq_b.reshape(seq_width, micro_rows, -1).astype(jnp.bfloat16)
        grad_query_w = contract(rows_b, grad_query_b)
        dx_mid, dgain_x = norm_back(x_mid, gain_x, collect_grad(grad_query_b, w_query))
        grad_mid = grad_late + dx_mid
        grad_a = spread_grad(grad_mid.astype(jnp.bfloat16))
        grad_out_w = contract(mixed_a, grad_a)
        grad_mixed_a = project_back(grad_a, w_out).astype(jnp.bfloat16)
        dq_a, dk_a, dv_a, grad_offsets = attend_back(
            split_qkv[:, :, 0], keys_a, values_a, grad_mixed_a, logsums_a, offset_bias, allow_self
        )
        grad_qkv = (
            jnp.stack([dq_a, dk_a[seq_width:], dv_a[seq_width:]], 2)
            .reshape(seq_width, micro_rows, -1)
            .astype(jnp.bfloat16)
        )
        grad_kv_src = (
            jnp.stack([dk_a[:seq_width] + dk_b, dv_a[:seq_width] + dv_b], 2)
            .reshape(seq_width, micro_rows, -1)
            .astype(jnp.bfloat16)
        )
        grad_kv_w = contract(rows_s, grad_kv_src).reshape(w_kv.shape)
        flat_kv = w_kv.reshape(model_width, -1)
        grad_normed_s = lax.psum_scatter(
            project_back(grad_kv_src, flat_kv), "tensor", scatter_dimension=0, tiled=True
        )
        dsource, dgain_s = norm_back(backward_src_raw, gain_all[2], grad_normed_s)
        flat_qkv = w_qkv.reshape(model_width, -1)
        grad_qkv_w = contract(rows_a, grad_qkv).reshape(w_qkv.shape)
        dx_in, dgain_a = norm_back(backward_x_in, gain_all[0], collect_grad(grad_qkv, flat_qkv))
        grad_in = grad_mid + dx_in
        grads = (
            grad_qkv_w,
            grad_out_w,
            grad_kv_w,
            grad_in_w,
            grad_ffo,
            jnp.stack([dgain_a, dgain_c, dgain_s]),
        )
        cross_parts = (grad_query_w, grad_cross, dgain_x)
        grad_in, dsource, grads, cross_parts, grad_offsets = (
            grad_in,
            dsource,
            grads,
            cross_parts,
            grad_offsets,
        )
        input_grads = jnp.where(
            valid, lax.dynamic_update_slice_in_dim(input_grads, grad_in, row_first, 1), input_grads
        )
        grad_back = from_behind(dsource.astype(jnp.bfloat16), "pipe", -1)
        grads = tuple((jnp.where(valid, member, 0.0) for member in grads))
        cross_parts = tuple((jnp.where(valid, member, 0.0) for member in cross_parts))
        grad_offsets = jnp.where(valid, grad_offsets, 0.0)
        if totals is None:
            totals, cross_totals, offset_total = (grads, cross_parts, grad_offsets)
        else:
            totals = tuple((older + newer for older, newer in zip(totals, grads)))
            cross_totals = tuple((older + newer for older, newer in zip(cross_totals, cross_parts)))
            offset_total = offset_total + grad_offsets
    bucket_grads = jnp.dot(
        bucket_hot.T, offset_total.T, precision=HIGHEST, preferred_element_type=jnp.float32
    )
    section_totals = (
        totals[0][None],
        totals[1][None],
        totals[2][None],
        totals[3][None],
        totals[4][None],
        bucket_grads[None],
        totals[5][None],
    )
    final = (
        lax.psum_scatter(
            section_totals[0].astype(jnp.bfloat16), "dp", scatter_dimension=1, tiled=True
        ).astype(jnp.float32),
        lax.psum_scatter(
            section_totals[1].astype(jnp.bfloat16), "dp", scatter_dimension=2, tiled=True
        ).astype(jnp.float32),
        lax.psum_scatter(
            section_totals[2].astype(jnp.bfloat16), "dp", scatter_dimension=1, tiled=True
        ).astype(jnp.float32),
        lax.psum_scatter(
            section_totals[3].astype(jnp.bfloat16), "dp", scatter_dimension=1, tiled=True
        ).astype(jnp.float32),
        lax.psum_scatter(
            section_totals[4].astype(jnp.bfloat16), "dp", scatter_dimension=2, tiled=True
        ).astype(jnp.float32),
        lax.psum_scatter(
            section_totals[5].astype(jnp.bfloat16), "dp", scatter_dimension=1, tiled=True
        ).astype(jnp.float32),
        lax.psum_scatter(
            section_totals[6].astype(jnp.bfloat16), "dp", scatter_dimension=2, tiled=True
        ).astype(jnp.float32),
    )
    cross_final = (
        lax.psum_scatter(cross_totals[0], ("pipe", "dp"), scatter_dimension=0, tiled=True),
        lax.psum_scatter(cross_totals[1], ("pipe", "dp"), scatter_dimension=1, tiled=True),
        lax.psum_scatter(cross_totals[2], ("pipe", "dp"), scatter_dimension=0, tiled=True),
    )
    gain_grads, cross_gain_grads = lax.psum((final[6], cross_final[2]), "tensor")
    return (
        section_out[None],
        input_grads[None],
        final[0],
        final[1],
        final[2],
        final[3],
        final[4],
        final[5],
        gain_grads,
        cross_final[0],
        cross_final[1],
        cross_gain_grads,
    )


def solution(mesh):
    placed = (
        P("pipe", "tensor", "dp", None),
        P(None, "dp", None),
        P("tensor", "dp"),
        P(),
        P(),
        P("pipe", "dp", None, "tensor"),
        P("pipe", "tensor", "dp"),
        P("pipe", "dp", None, "tensor"),
        P("pipe", "dp", "tensor"),
        P("pipe", "tensor", "dp"),
        P("pipe", "dp", "tensor"),
        P("pipe", None, "dp"),
        P(("pipe", "dp"), "tensor"),
        P("tensor", ("pipe", "dp")),
        P(("pipe", "dp")),
        P("pipe", "tensor", "dp", None),
    )
    return jax.shard_map(
        body,
        mesh=mesh,
        in_specs=placed,
        out_specs=(
            P("pipe", "tensor", "dp", None),
            P("pipe", "tensor", "dp", None),
            P("pipe", "dp", None, "tensor"),
            P("pipe", "tensor", "dp"),
            P("pipe", "dp", None, "tensor"),
            P("pipe", "dp", "tensor"),
            P("pipe", "tensor", "dp"),
            P("pipe", "dp", "tensor"),
            P("pipe", None, "dp"),
            P(("pipe", "dp"), "tensor"),
            P("tensor", ("pipe", "dp")),
            P(("pipe", "dp")),
        ),
        check_vma=False,
    )
```

profile of v0, /device:TPU:9, one launch (start us, length us, event | category | flops | bytes accessed | tf_op | source)
XLA Modules:
  0.0 1945.9 jit_solution(10538258342866057455)
XLA Ops:
  15.2 11.8 all_gather.62
  27.5 6.9 slice_reduce_fusion
  35.3 12.9 all_gather.65
  48.4 29.3 %all_gather.66 = bf16[1,768,3,192]{3,2,0,1:T(4,128)(2,1)S(1)} all-gather(bf16[1,192,3,192]{3,2,0,1:T(4,128)(2,1)S(1)} %copy.104), channel_id=1, replica_groups=mesh['pipe'=2,'dp'=4,'tensor'=4] {'dp'}, dimensions={1}, use_global_device_ids=true | all-gather | bytes 1105920 | tf_op jit(solution)/shard_map/all_gather | solution.py:183
  87.0 8.9 all_gather.63
  95.9 17.3 all_gather.64
  116.9 10.8 all_gather.67
  128.8 211.6 %gather_fusion.1 = f32[115200,3]{1,0:T(8,128)} fusion(f32[3,960]{0,1:T(8,128)S(1)} %copy.108, s32[115712]{0:T(1024)S(1)} %pad_clamp_fusion.1), kind=kCustom, calls=%fused_computation.1 | custom fusion | bytes 3225600 | tf_op jit(solution)/shard_map/gather | solution.py:72
  340.4 32.8 %copy.128 = f32[240,480,3]{1,0,2:T(8,128)} copy(f32[240,480,3]{2,1,0:T(8,128)} %bitcast.931) | data formatting | bytes 2764800 | tf_op jit(solution)/shard_map/gather | solution.py:72
  373.9 211.6 %gather_fusion.2 = f32[115200,3]{1,0:T(8,128)} fusion(f32[3,960]{0,1:T(8,128)S(1)} %copy.108, s32[115712]{0:T(1024)S(1)} %pad_clamp_fusion), kind=kCustom, calls=%fused_computation.2 | custom fusion | bytes 3225600 | tf_op jit(solution)/shard_map/gather | solution.py:72
  585.5 32.8 %copy.129 = f32[240,480,3]{1,0,2:T(8,128)} copy(f32[240,480,3]{2,1,0:T(8,128)} %bitcast.930) | data formatting | bytes 2764800 | tf_op jit(solution)/shard_map/gather | solution.py:72
  630.1 14.2 all_gather.68
  648.2 16.1 all-reduce.14
  664.4 23.4 %all_gather.71 = bf16[768,192]{1,0:T(8,128)(2,1)S(1)} all-gather(bf16[96,192]{1,0:T(8,128)(2,1)S(1)} %copy-done.272), channel_id=1, replica_groups=mesh['pipe'=2,'dp'=4,'tensor'=4] {'pipe','dp'}, dimensions={0}, use_global_device_ids=true | all-gather | bytes 331776 | tf_op jit(solution)/shard_map/all_gather | solution.py:192
  687.8 26.3 %all_gather.72 = bf16[192,768]{0,1:T(8,128)(2,1)S(1)} all-gather(bf16[192,96]{0,1:T(8,128)(2,1)S(1)} %copy.114), channel_id=1, replica_groups=mesh['pipe'=2,'dp'=4,'tensor'=4] {'pipe','dp'}, dimensions={1}, use_global_device_ids=true | all-gather | bytes 331776 | tf_op jit(solution)/shard_map/all_gather | solution.py:193
  716.4 30.4 %all_gather.70 = bf16[480,1,768]{2,0,1:T(8,128)(2,1)S(1)} all-gather(bf16[120,1,768]{2,0,1:T(8,128)(2,1)S(1)} %multiply_convert_fusion.20), channel_id=1, replica_groups=mesh['pipe'=2,'dp'=4,'tensor'=4] {'tensor'}, dimensions={0}, use_global_device_ids=true | all-gather | bytes 921600 | tf_op jit(solution)/shard_map/all_gather | solution.py:199
  754.0 26.5 %reduce-scatter.45.cloned.1.call-done = f32[120,1,768]{2,0,1:T(8,128)} async-done(((f32[480,1,768]{2,0,1:T(8,128)}), f32[120,1,768]{2,0,1:T(8,128)}) %reduce-scatter.45.cloned.1.call-update) | async-done | bytes 368656 | tf_op jit(solution)/shard_map/reduce_scatter | solution.py:209
  780.8 8.9 all_gather.73
  793.0 22.1 %all-gather.6.cloned.1.call-done = bf16[1,768,768]{1,2,0:T(8,128)(2,1)} async-done(((bf16[1,768,192]{1,2,0:T(8,128)(2,1)}), bf16[1,768,768]{1,2,0:T(8,128)(2,1)}) %all-gather.6.cloned.1.call-update) | async-done | bytes 1179664 | tf_op jit(solution)/shard_map/all_gather | solution.py:187
  827.7 9.2 all_gather.77
  839.3 7.3 reduce-scatter.47.cloned.1.call-done
  854.4 8.9 all_gather.76
  879.2 28.2 %reduce-scatter.49.cloned.1.call-done = f32[120,1,768]{2,0,1:T(8,128)} async-done(((f32[480,1,768]{2,0,1:T(8,128)}), f32[120,1,768]{2,0,1:T(8,128)}) %reduce-scatter.49.cloned.1.call-update) | async-done | bytes 368656 | tf_op jit(solution)/shard_map/reduce_scatter | solution.py:209
  909.3 8.6 all_gather.156
  924.2 27.5 %reduce-scatter.51.cloned.1.call-done = f32[120,1,768]{2,0,1:T(8,128)} async-done(((f32[480,1,768]{2,0,1:T(8,128)}), f32[120,1,768]{2,0,1:T(8,128)}) %reduce-scatter.51.cloned.1.call-update) | async-done | bytes 368656 | tf_op jit(solution)/shard_map/reduce_scatter | solution.py:209
  953.8 8.7 all_gather.157
  977.1 8.4 all_gather.159
  987.9 7.2 reduce-scatter.53.cloned.1.call-done
  1004.5 8.8 all_gather.158
  1030.4 28.2 %reduce-scatter.55.cloned.1.call-done = f32[120,1,768]{2,0,1:T(8,128)} async-done(((f32[480,1,768]{2,0,1:T(8,128)}), f32[120,1,768]{2,0,1:T(8,128)}) %reduce-scatter.55.cloned.1.call-update) | async-done | bytes 368656 | tf_op jit(solution)/shard_map/reduce_scatter | solution.py:209
  1060.6 9.0 all_gather.160
  1079.9 8.9 all-gather
  1088.8 14.7 reduce-scatter.57.cloned.1.call-done
  1105.6 8.5 all_gather.161
  1121.9 26.4 %reduce-scatter.61.cloned.1.call-done = f32[120,1,768]{2,0,1:T(8,128)} async-done(((f32[480,1,768]{2,0,1:T(8,128)}), f32[120,1,768]{2,0,1:T(8,128)}) %reduce-scatter.61.cloned.1.call-update) | async-done | bytes 368656 | tf_op jit(solution)/shard_map/reduce_scatter | solution.py:221
  1151.6 8.6 all_gather.163
  1174.7 19.9 %reduce-scatter.63.cloned.1.call-done = f32[120,1,768]{2,0,1:T(8,128)} async-done(((f32[480,1,768]{2,0,1:T(8,128)}), f32[120,1,768]{2,0,1:T(8,128)}) %reduce-scatter.63.cloned.1.call-update) | async-done | bytes 368656 | tf_op jit(solution)/shard_map/reduce_scatter | solution.py:221
  1199.6 8.6 all_gather.164
  1222.8 27.5 %reduce-scatter.67.cloned.1.call-done = f32[120,1,768]{2,0,1:T(8,128)} async-done(((f32[480,1,768]{2,0,1:T(8,128)}), f32[120,1,768]{2,0,1:T(8,128)}) %reduce-scatter.67.cloned.1.call-update) | async-done | bytes 368656 | tf_op jit(solution)/shard_map/reduce_scatter | solution.py:432
  1254.6 6.1 collective-permute-done.2
  1260.7 8.8 all_gather.165
  1277.3 25.3 %reduce-scatter.69.cloned.1.call-done = f32[120,1,768]{2,0,1:T(8,128)} async-done(((f32[480,1,768]{2,0,1:T(8,128)}), f32[120,1,768]{2,0,1:T(8,128)}) %reduce-scatter.69.cloned.1.call-update) | async-done | bytes 368656 | tf_op jit(solution)/shard_map/reduce_scatter | solution.py:221
  1307.2 8.8 all_gather.166
  1330.2 20.2 %reduce-scatter.71.cloned.1.call-done = f32[120,1,768]{2,0,1:T(8,128)} async-done(((f32[480,1,768]{2,0,1:T(8,128)}), f32[120,1,768]{2,0,1:T(8,128)}) %reduce-scatter.71.cloned.1.call-update) | async-done | bytes 368656 | tf_op jit(solution)/shard_map/reduce_scatter | solution.py:221
  1354.9 8.6 all_gather.167
  1378.2 27.5 %reduce-scatter.75.cloned.1.call-done = f32[120,1,768]{2,0,1:T(8,128)} async-done(((f32[480,1,768]{2,0,1:T(8,128)}), f32[120,1,768]{2,0,1:T(8,128)}) %reduce-scatter.75.cloned.1.call-update) | async-done | bytes 368656 | tf_op jit(solution)/shard_map/reduce_scatter | solution.py:432
  1409.8 6.1 collective-permute-done.3
  1416.0 9.2 all_gather.168
  1431.3 26.6 %reduce-scatter.77.cloned.1.call-done = f32[120,1,768]{2,0,1:T(8,128)} async-done(((f32[480,1,768]{2,0,1:T(8,128)}), f32[120,1,768]{2,0,1:T(8,128)}) %reduce-scatter.77.cloned.1.call-update) | async-done | bytes 368656 | tf_op jit(solution)/shard_map/reduce_scatter | solution.py:221
  1461.5 8.6 all_gather.169
  1496.6 6.7 copy.136
  1519.2 9.7 all_gather.170
  1591.7 10.8 rev.19
  1613.0 6.0 reshape.4256
  1621.4 8.1 rev.18
  1641.7 6.0 reshape.4254
  1670.2 11.0 rev.21
  1730.6 49.8 %reduce-scatter.99.cloned.1.call-done = f32[96,192]{1,0:T(8,128)} async-done(((f32[768,192]{1,0:T(8,128)}), f32[96,192]{1,0:T(8,128)}) %reduce-scatter.99.cloned.1.call-update) | async-done | bytes 73744
  1785.0 15.1 all-reduce.16
  1815.5 10.8 rev.22
  1839.5 9.7 all-reduce.15
  1861.9 8.8 reduce-scatter.97.cloned.1.call-done
  1872.0 12.8 all-reduce.17
  1884.8 53.4 %reduce-scatter.87.cloned.1.call-done = f32[96,192]{1,0:T(8,128)} async-done(((f32[768,192]{1,0:T(8,128)}), f32[96,192]{1,0:T(8,128)}) %reduce-scatter.87.cloned.1.call-update) | async-done | bytes 73744 | tf_op jit(solution)/shard_map/reduce_scatter | solution.py:505
  (1312 shorter events, 511.2 us)
Async XLA Ops:
  8.0 707.1 %reduce-scatter.43.cloned.1.call-start = ((), (), s32[]{:S(2)}) async-start(), calls=%async_computation.29 | async-start | bytes 1843200 | tf_op jit(solution)/shard_map/reduce_scatter | solution.py:209
  11.0 813.4 %copy-start.284 = (s32[1,1,480]{2,1,0:T(1,128)}, s32[1,1,480]{2,1,0:T(1,128)S(1)}, u32[]{:S(2)}) copy-start(s32[1,1,480]{2,1,0:T(1,128)S(1)} %get-tuple-element.163) | copy-start | bytes 5764
  14.4 700.7 %copy-start.111 = (bf16[120,1,768]{2,0,1:T(8,128)(2,1)}, bf16[120,1,768]{2,0,1:T(8,128)(2,1)S(1)}, u32[]{:S(2)}) copy-start(bf16[120,1,768]{2,0,1:T(8,128)(2,1)S(1)} %get-tuple-element.122) | copy-start | bytes 552964
  34.3 43.5 %copy-start.263 = (f32[768]{0:T(1024)}, f32[768]{0:T(1024)S(1)}, u32[]{:S(2)}) copy-start(f32[768]{0:T(1024)S(1)} %get-tuple-element.83) | copy-start | bytes 9220
  78.6 758.3 %copy-start.52 = (bf16[1,768,3,192]{1,3,2,0:T(8,128)(2,1)}, bf16[1,768,3,192]{1,3,2,0:T(8,128)(2,1)S(1)}, u32[]{:S(2)}) copy-start(bf16[1,768,3,192]{1,3,2,0:T(8,128)(2,1)S(1)} %copy.105) | copy-start | bytes 2654212
  113.8 749.6 %copy-start.66 = (bf16[1,768,2,192]{1,3,2,0:T(8,128)(2,1)}, bf16[1,768,2,192]{1,3,2,0:T(8,128)(2,1)S(1)}, u32[]{:S(2)}) copy-start(bf16[1,768,2,192]{1,3,2,0:T(8,128)(2,1)S(1)} %copy.102) | copy-start | bytes 1769476
  116.0 634.4 %copy-start.59 = (bf16[480,384]{0,1:T(8,128)(2,1)}, bf16[480,384]{0,1:T(8,128)(2,1)S(1)}, u32[]{:S(2)}) copy-start(bf16[480,384]{0,1:T(8,128)(2,1)S(1)} %copy.103) | copy-start | bytes 1105924
  340.4 32.8 %copy-start.333 = (s32[240]{0:T(256)S(1)}, s32[240]{0:T(256)}, u32[]{:S(2)}) copy-start(s32[240]{0:T(256)} %iota_add_fusion) | copy-start | bytes 2884
  585.5 32.8 %copy-start.288 = (s32[1,1,480]{2,1,0:T(1,128)S(1)}, s32[1,1,480]{2,1,0:T(1,128)}, u32[]{:S(2)}) copy-start(s32[1,1,480]{2,1,0:T(1,128)} %copy-done.287) | copy-start | bytes 5764
  585.5 32.8 %copy-start.329 = (s32[1,240]{1,0:T(1,128)S(1)}, s32[1,240]{1,0:T(1,128)}, u32[]{:S(2)}) copy-start(s32[1,240]{1,0:T(1,128)} %get-tuple-element.199) | copy-start | bytes 2884
  585.5 32.8 %copy-start.331 = (s32[1,240]{1,0:T(1,128)S(1)}, s32[1,240]{1,0:T(1,128)}, u32[]{:S(2)}) copy-start(s32[1,240]{1,0:T(1,128)} %get-tuple-element.200) | copy-start | bytes 2884
  646.6 67.6 %copy-start.330 = (s32[1,240]{1,0:T(1,128)S(1)}, s32[1,240]{1,0:T(1,128)}, u32[]{:S(2)}) copy-start(s32[1,240]{1,0:T(1,128)} %get-tuple-element.199) | copy-start | bytes 2884
  646.6 67.6 %copy-start.332 = (s32[1,240]{1,0:T(1,128)S(1)}, s32[1,240]{1,0:T(1,128)}, u32[]{:S(2)}) copy-start(s32[1,240]{1,0:T(1,128)} %get-tuple-element.200) | copy-start | bytes 2884
  646.6 133.9 %reduce-scatter.45.cloned.1.call-start = ((), (), s32[]{:S(2)}) async-start(), calls=%async_computation.30 | async-start | bytes 1843200 | tf_op jit(solution)/shard_map/reduce_scatter | solution.py:209
  714.1 37.0 %copy-start.24 = (bf16[192,768]{0,1:T(8,128)(2,1)}, bf16[192,768]{0,1:T(8,128)(2,1)S(1)}, u32[]{:S(2)}) copy-start(bf16[192,768]{0,1:T(8,128)(2,1)S(1)} %all_gather.72) | copy-start | bytes 884740
  716.2 30.6 %copy-start.382 = (f32[120]{0:T(128)}, f32[120]{0:T(128)S(1)}, u32[]{:S(2)}) copy-start(f32[120]{0:T(128)S(1)} %get-tuple-element.119) | copy-start | bytes 1444
  716.2 64.3 %copy-start.71 = (f32[120,1,768]{2,0,1:T(8,128)}, f32[120,1,768]{2,0,1:T(8,128)S(1)}, u32[]{:S(2)}) copy-start(f32[120,1,768]{2,0,1:T(8,128)S(1)} %get-tuple-element.120) | copy-start | bytes 1105924
  716.2 31.1 %copy-start.353 = (f32[120]{0:T(128)}, f32[120]{0:T(128)S(1)}, u32[]{:S(2)}) copy-start(f32[120]{0:T(128)S(1)} %fusion.416) | copy-start | bytes 1444
  716.2 31.1 %copy-start.228 = (pred[240,480]{1,0:T(8,128)(4,1)S(1)}, pred[240,480]{1,0:T(8,128)(4,1)}, u32[]{:S(2)}) copy-start(pred[240,480]{1,0:T(8,128)(4,1)} %get-tuple-element.191) | copy-start | bytes 345604
  752.8 36.9 %all-gather.4.cloned.1.call-start = ((), (), s32[]{:S(2)}) async-start(), calls=%async_computation.31 | async-start | bytes 1474560 | tf_op jit(solution)/shard_map/all_gather | solution.py:186
  753.4 61.8 %all-gather.6.cloned.1.call-start = ((), (), s32[]{:S(2)}) async-start(), calls=%async_computation.32 | async-start | bytes 1474560 | tf_op jit(solution)/shard_map/all_gather | solution.py:187
  754.0 92.6 %reduce-scatter.47.cloned.1.call-start = ((), (), s32[]{:S(2)}) async-start(), calls=%async_computation.33 | async-start | bytes 1843200 | tf_op jit(solution)/shard_map/reduce_scatter | solution.py:209
  780.6 66.0 %copy-start.75 = (f32[120,1,768]{2,0,1:T(8,128)}, f32[120,1,768]{2,0,1:T(8,128)S(1)}, u32[]{:S(2)}) copy-start(f32[120,1,768]{2,0,1:T(8,128)S(1)} %get-tuple-element.118) | copy-start | bytes 1105924
  819.0 88.3 %reduce-scatter.49.cloned.1.call-start = ((), (), s32[]{:S(2)}) async-start(), calls=%async_computation.34 | async-start | bytes 1843200 | tf_op jit(solution)/shard_map/reduce_scatter | solution.py:209
  847.7 6.4 collective-permute-start
  876.5 30.9 %copy-start.114 = (bf16[120,1,768]{2,0,1:T(8,128)(2,1)S(1)}, bf16[120,1,768]{2,0,1:T(8,128)(2,1)}, u32[]{:S(2)}) copy-start(bf16[120,1,768]{2,0,1:T(8,128)(2,1)} %copy-done.113) | copy-start | bytes 552964
  878.2 73.5 %reduce-scatter.51.cloned.1.call-start = ((), (), s32[]{:S(2)}) async-start(), calls=%async_computation.35 | async-start | bytes 1843200 | tf_op jit(solution)/shard_map/reduce_scatter | solution.py:209
  924.1 70.9 %reduce-scatter.53.cloned.1.call-start = ((), (), s32[]{:S(2)}) async-start(), calls=%async_computation.36 | async-start | bytes 1843200 | tf_op jit(solution)/shard_map/reduce_scatter | solution.py:209
  967.4 91.2 %reduce-scatter.55.cloned.1.call-start = ((), (), s32[]{:S(2)}) async-start(), calls=%async_computation.37 | async-start | bytes 1843200 | tf_op jit(solution)/shard_map/reduce_scatter | solution.py:209
  997.0 6.5 collective-permute-start.1
  1027.7 30.8 %copy-start.117 = (bf16[120,1,768]{2,0,1:T(8,128)(2,1)S(1)}, bf16[120,1,768]{2,0,1:T(8,128)(2,1)}, u32[]{:S(2)}) copy-start(bf16[120,1,768]{2,0,1:T(8,128)(2,1)} %copy-done.116) | copy-start | bytes 552964
  1029.4 74.1 %reduce-scatter.57.cloned.1.call-start = ((), (), s32[]{:S(2)}) async-start(), calls=%async_computation.38 | async-start | bytes 1843200 | tf_op jit(solution)/shard_map/reduce_scatter | solution.py:209
  1075.8 72.5 %reduce-scatter.61.cloned.1.call-start = ((), (), s32[]{:S(2)}) async-start(), calls=%async_computation.40 | async-start | bytes 1843200 | tf_op jit(solution)/shard_map/reduce_scatter | solution.py:221
  1104.8 45.4 %copy-start.343 = (f32[120]{0:T(128)}, f32[120]{0:T(128)S(1)}, u32[]{:S(2)}) copy-start(f32[120]{0:T(128)S(1)} %fusion.425) | copy-start | bytes 1444
  1120.6 73.9 %reduce-scatter.63.cloned.1.call-start = ((), (), s32[]{:S(2)}) async-start(), calls=%async_computation.41 | async-start | bytes 1843200 | tf_op jit(solution)/shard_map/reduce_scatter | solution.py:221
  1167.0 83.3 %reduce-scatter.67.cloned.1.call-start = ((), (), s32[]{:S(2)}) async-start(), calls=%async_computation.43 | async-start | bytes 1843200 | tf_op jit(solution)/shard_map/reduce_scatter | solution.py:432
  1221.1 29.3 %copy-start.359 = (f32[120]{0:T(128)S(1)}, f32[120]{0:T(128)}, u32[]{:S(2)}) copy-start(f32[120]{0:T(128)} %copy-done.358) | copy-start | bytes 1444
  1222.7 29.4 %copy-start.391 = (f32[120]{0:T(128)S(1)}, f32[120]{0:T(128)}, u32[]{:S(2)}) copy-start(f32[120]{0:T(128)} %copy-done.390) | copy-start | bytes 1444
  1222.8 79.8 %reduce-scatter.69.cloned.1.call-start = ((), (), s32[]{:S(2)}) async-start(), calls=%async_computation.44 | async-start | bytes 1843200 | tf_op jit(solution)/shard_map/reduce_scatter | solution.py:221
  1253.3 7.4 collective-permute-start.2
  1275.4 75.0 %reduce-scatter.71.cloned.1.call-start = ((), (), s32[]{:S(2)}) async-start(), calls=%async_computation.45 | async-start | bytes 1843200 | tf_op jit(solution)/shard_map/reduce_scatter | solution.py:221
  1322.8 82.9 %reduce-scatter.75.cloned.1.call-start = ((), (), s32[]{:S(2)}) async-start(), calls=%async_computation.47 | async-start | bytes 1843200 | tf_op jit(solution)/shard_map/reduce_scatter | solution.py:432
  1376.4 29.3 %copy-start.141 = (bf16[120,1,768]{2,0,1:T(8,128)(2,1)S(1)}, bf16[120,1,768]{2,0,1:T(8,128)(2,1)}, u32[]{:S(2)}) copy-start(bf16[120,1,768]{2,0,1:T(8,128)(2,1)} %copy-done.140) | copy-start | bytes 552964
  1376.4 29.3 %copy-start.357 = (f32[120]{0:T(128)S(1)}, f32[120]{0:T(128)}, u32[]{:S(2)}) copy-start(f32[120]{0:T(128)} %copy-done.356) | copy-start | bytes 1444
  1378.1 29.3 %copy-start.389 = (f32[120]{0:T(128)S(1)}, f32[120]{0:T(128)}, u32[]{:S(2)}) copy-start(f32[120]{0:T(128)} %copy-done.388) | copy-start | bytes 1444
  1378.1 37.9 %copy-start.126 = (bf16[1,120,1,768]{3,2,1,0:T(2,128)(2,1)S(1)}, bf16[1,120,1,768]{3,2,1,0:T(2,128)(2,1)}, u32[]{:S(2)}) copy-start(bf16[1,120,1,768]{3,2,1,0:T(2,128)(2,1)} %get-tuple-element.135) | copy-start | bytes 552964
  1378.1 79.7 %reduce-scatter.77.cloned.1.call-start = ((), (), s32[]{:S(2)}) async-start(), calls=%async_computation.48 | async-start | bytes 1843200 | tf_op jit(solution)/shard_map/reduce_scatter | solution.py:221
  1408.5 7.4 collective-permute-start.3
  1430.6 85.2 %reduce-scatter.79.cloned.1.call-start = ((), (), s32[]{:S(2)}) async-start(), calls=%async_computation.49 | async-start | bytes 1843200 | tf_op jit(solution)/shard_map/reduce_scatter | solution.py:221
  1476.8 83.8 %reduce-scatter.59.cloned.1.call-start = ((), (), s32[]{:S(2)}) async-start(), calls=%async_computation.39 | async-start | bytes 1843200 | tf_op jit(solution)/shard_map/reduce_scatter | solution.py:209
  1480.8 172.4 %reduce-scatter.65.cloned.1.call-start = ((), (), s32[]{:S(2)}) async-start(), calls=%async_computation.42 | async-start | bytes 1843200 | tf_op jit(solution)/shard_map/reduce_scatter | solution.py:221
  1490.1 225.6 %reduce-scatter.95.cloned.1.call-start = ((), (), s32[]{:S(2)}) async-start(), calls=%async_computation.57 | async-start | bytes 1474560
  1506.2 212.3 %reduce-scatter.83.cloned.1.call-start = ((), (), s32[]{:S(2)}) async-start(), calls=%async_computation.51 | async-start | bytes 1474560 | tf_op jit(solution)/shard_map/reduce_scatter | solution.py:491
  1512.2 208.2 %reduce-scatter.85.cloned.1.call-start = ((), (), s32[]{:S(2)}) async-start(), calls=%async_computation.52 | async-start | bytes 1843200 | tf_op jit(solution)/shard_map/reduce_scatter | solution.py:432
  1542.2 179.3 %reduce-scatter.73.cloned.1.call-start = ((), (), s32[]{:S(2)}) async-start(), calls=%async_computation.46 | async-start | bytes 1843200 | tf_op jit(solution)/shard_map/reduce_scatter | solution.py:221
  1549.5 172.1 %reduce-scatter.81.cloned.1.call-start = ((), (), s32[]{:S(2)}) async-start(), calls=%async_computation.50 | async-start | bytes 1843200 | tf_op jit(solution)/shard_map/reduce_scatter | solution.py:221
  1557.4 223.0 %reduce-scatter.99.cloned.1.call-start = ((), (), s32[]{:S(2)}) async-start(), calls=%async_computation.59 | async-start | bytes 884736
  1567.4 282.5 %reduce-scatter.91.cloned.1.call-start = ((), (), s32[]{:S(2)}) async-start(), calls=%async_computation.55 | async-start | bytes 491520
  1578.9 272.8 %reduce-scatter.93.cloned.1.call-start = ((), (), s32[]{:S(2)}) async-start(), calls=%async_computation.56 | async-start | bytes 737280
  1589.8 264.1 %reduce-scatter.89.cloned.1.call-start = ((), (), s32[]{:S(2)}) async-start(), calls=%async_computation.54 | async-start | bytes 1228800
  1664.0 206.7 %reduce-scatter.97.cloned.1.call-start = ((), (), s32[]{:S(2)}) async-start(), calls=%async_computation.58 | async-start | bytes 245760
  1727.9 210.3 %reduce-scatter.87.cloned.1.call-start = ((), (), s32[]{:S(2)}) async-start(), calls=%async_computation.53 | async-start | bytes 884736 | tf_op jit(solution)/shard_map/reduce_scatter | solution.py:505
  1728.0 54.1 %copy-start.45 = (bf16[3,240,960]{2,1,0:T(8,128)(2,1)S(1)}, bf16[3,240,960]{2,1,0:T(8,128)(2,1)}, u32[]{:S(2)}) copy-start(bf16[3,240,960]{2,1,0:T(8,128)(2,1)} %copy-done.43) | copy-start | bytes 4147204
  1730.6 52.9 %copy-start.42 = (bf16[3,240,960]{2,1,0:T(8,128)(2,1)S(1)}, bf16[3,240,960]{2,1,0:T(8,128)(2,1)}, u32[]{:S(2)}) copy-start(bf16[3,240,960]{2,1,0:T(8,128)(2,1)} %copy-done.40) | copy-start | bytes 4147204
  (381 other events, 1764.8 us)
Sparse Core Ops, SparseCore 0:
  646.7 34.3 reduce-scatter.42
  752.9 27.5 reduce-scatter.44
  819.1 27.4 reduce-scatter.46
  878.3 28.9 reduce-scatter.48
  924.2 27.3 reduce-scatter.50
  967.5 27.5 reduce-scatter.52
  1029.5 29.0 reduce-scatter.54
  1075.9 27.5 reduce-scatter.56
  1120.8 27.5 reduce-scatter.60
  1167.1 27.4 reduce-scatter.62
  1222.9 27.3 reduce-scatter.66
  1275.5 27.0 reduce-scatter.68
  1322.9 27.4 reduce-scatter.70
  1378.2 27.4 reduce-scatter.74
  1430.7 27.0 reduce-scatter.76
  1476.9 27.4 reduce-scatter.78
  1506.9 28.5 reduce-scatter.58
  1538.1 27.3 reduce-scatter.64
  1567.8 27.2 reduce-scatter.94
  1597.2 27.8 reduce-scatter.82
  1627.7 28.2 reduce-scatter.84
  1658.7 27.5 reduce-scatter.72
  1688.9 27.5 reduce-scatter.80
  1720.0 60.3 reduce-scatter.98
  1783.3 17.6 reduce-scatter.90
  1803.8 20.6 reduce-scatter.92
  1826.8 26.1 reduce-scatter.88
  1855.3 15.4 reduce-scatter.96
  1875.0 63.1 reduce-scatter.86
Sparse Core Ops, SparseCore 1:
  754.8 29.4 all-gather.3
  785.7 29.4 all-gather.5
where the time goes:
time: 1970 us; the launch traced here: 1950 us
  local copies, waits for them, and re-layouts  769 us (39%)
  waiting for transfers between devices  467 us (24%)
  blocking collectives  398 us (20%)
  matrix products  171 us (9%)
  other arithmetic  107 us (5%)
  between operations  22.7 us (1%)
    gather x4, local copies, waits for them, and re-layouts, block_scores(): own_part = offset_bias[:, offset_index(first_row, row_count, seq_width)]  489 us
    reduce_scatter x9, waiting for transfers between devices, collect(): lax.psum_scatter(term_rows(jnp.int32(0), lax.axis_size('tensor') * shard_...  140 us
    reduce_scatter x9, waiting for transfers between devices, collect_grad(): lax.psum_scatter(term_rows(jnp.int32(0), lax.axis_size('tensor') * shard_...  118 us
    all_gather x9, blocking collectives, spread(): return lax.all_gather(rows_part, 'tensor', axis=0, tiled=True)  105 us
    unnamed x861, local copies, waits for them, and re-layouts  97.9 us
    all_gather x9, blocking collectives, spread_grad(): return lax.all_gather(rows_part, 'tensor', axis=0, tiled=True)  79.7 us
    unnamed x37, waiting for transfers between devices  60.2 us
    reduce_scatter x3, waiting for transfers between devices, body(): lax.psum_scatter(project_back(grad_kv_src, flat_kv), 'tensor', scatter_di...  55 us
  transfers between devices with their start and end apart: 35, of which 22 were waited for; matrix products, arithmetic and copies ran while one was open for 17% of the time, Pallas kernels for 0%

commit v1 on v0

v1 whole, which is shorter than its diff:
```python
import functools

import jax
import jax.numpy as jnp
from jax import lax
from jax.experimental import pallas as pl
from jax.experimental.pallas import tpu as pltpu
from jax.sharding import PartitionSpec as P

HD = 64
NB = 32
MEM = 20
HALO = 48
EXT = 128
REL_AT = 8
EPSILON = 1e-06
NEG = -1000000000.0
BF = jnp.bfloat16
F32 = jnp.float32
MESH = pl.DeviceIdType.MESH
CW = 256
RT = 48


def dot(a, b):
    return lax.dot_general(a, b, (((1,), (0,)), ((), ())), preferred_element_type=F32)


def dot_nt(a, b):
    return lax.dot_general(a, b, (((1,), (1,)), ((), ())), preferred_element_type=F32)


def dot_tn(a, b):
    return lax.dot_general(a, b, (((0,), (0,)), ((), ())), preferred_element_type=F32)


class Refs:
    pass


def kernel(dims, names, *refs):
    L, D, hs, fs, nz, qb_rows, win_w = dims
    hc, fc = 2 * hs, 2 * fs
    at_o, at_kv, at_ext = 3 * hs, 4 * hs, 6 * hs
    chunk_rows = D // nz
    cross_rows = chunk_rows // 2
    n_blk = L // qb_rows
    n_pair = hc // 128
    n_cw = D // CW
    o = Refs()
    for name, ref in zip(names, refs, strict=True):
        setattr(o, name, ref)
    p = lax.axis_index("pipe")
    d = lax.axis_index("dp")
    t = lax.axis_index("tensor")
    enc, dec = p == 0, p == 1
    core = lax.rem(t, 2)
    y = t // 2
    sibling = (p, d, t + 1 - 2 * core)
    across = (1 - p, d, t)
    beside = (p, d, lax.rem(t + 2, 4))
    half = L // 2
    held = L // 4
    A, B, C, X = range(4)
    shard = (o.sa, o.sb, o.sc, o.sx)
    W = (o.wa, o.wb, o.wc, o.wx)
    RY = (o.ya, o.yb, o.yc, o.yx)
    RZ = (o.za, o.zb, o.zc, o.zx)
    place = (
        [(o.oa, o.xmid, chunk_rows, 0, fs), (o.oa, o.xlate, chunk_rows, fs, 6 * hs + EXT - fs)],
        [(o.ob, o.xlate, 0, 0, fs)],
        [(o.oc, o.xmid, 0, 0, fs)],
    )
    ROWS = ((o.xs, o.xq), (o.cs, o.cq), (o.ms, o.mq))

    def chunk(k):
        return pl.ds(pl.multiple_of(k * chunk_rows, 16), chunk_rows)

    def remote(src, dst, send, recv, device):
        return pltpu.make_async_remote_copy(
            src_ref=src,
            dst_ref=dst,
            send_sem=send,
            recv_sem=recv,
            device_id=device,
            device_id_type=MESH,
        )


    def ag_right(g, k):
        slot = W[g].at[y, chunk(k)]
        return remote(slot, slot, o.gr.at[g, k], o.gz.at[g, k], (p, d + 1, t))

    def ag_left(g, k):
        slot = W[g].at[y, chunk(k)]
        return remote(slot, slot, o.gl.at[g, k], o.gz.at[g, k], (p, d - 1, t))

    def ag_beside(g, k):
        slot = W[g].at[y, chunk(k)]
        return remote(slot, slot, o.gs.at[g, k], o.gy.at[g, k], beside)

    def ag_came(g, k):
        slot = W[g].at[y, chunk(k)]
        remote(slot, slot, o.gr.at[g, k], o.gz.at[g, k], beside).wait_recv()

    def ag_each(g, h, act):
        if h == 0:
            act(d, d + 1 < nz, d > 0, True)
        else:
            act(d - h, d + 1 < nz, False, d - h >= 0)
            act(d + h, False, d > 0, d + h < nz)

    def when(cond, fn):
        if cond is True:
            fn()
        elif cond is not False:
            pl.when(cond)(fn)

    def ag_hop(g, h):
        if h >= nz:
            return

        def act(k, right, left, here):
            def go():
                if h > 0:
                    ag_came(g, k)
                if nz > 1:
                    when(right, lambda: ag_right(g, k).start())
                    when(left, lambda: ag_left(g, k).start())
                ag_beside(g, k).start()

            when(here, go)

        ag_each(g, h, act)

    def ag_wait(g):
        for k in range(nz):
            slot = W[g].at[1 - y, chunk(k)]
            remote(slot, slot, o.gs.at[g, k], o.gy.at[g, k], beside).wait_recv()

    def ag_finish(g):
        for h in range(nz):

            def act(k, right, left, here):
                def go():
                    if nz > 1:
                        when(right, lambda: ag_right(g, k).wait_send())
                        when(left, lambda: ag_left(g, k).wait_send())
                    ag_beside(g, k).wait_send()

                when(here, go)

            ag_each(g, h, act)

    def own_copy(g):
        return pltpu.make_async_copy(shard[g], W[g].at[y, chunk(d)], o.oc_sem.at[g])

    def cross_part(k, part):
        start = k * chunk_rows + part * cross_rows
        return pl.ds(pl.multiple_of(start, 16), cross_rows)

    cross_own = pltpu.make_async_copy(o.sx, W[X].at[y, cross_part(d, 1)], o.oc_sem.at[X])
    cross_in = remote(
        o.sx, W[X].at[y, cross_part(d, 0)], o.xw.at[0], o.xw.at[1], across
    )
    cross_out = remote(o.xo, o.xi, o.xw.at[2], o.xw.at[3], across)


    def rs_y(g, k):
        return remote(
            W[g].at[1 - y, chunk(k)], RY[g].at[chunk(k)], o.rs_s.at[g, k], o.rs_r.at[g, k], beside
        )

    def rs_z(g, k):
        away = lax.rem(d + nz - 1 - k, nz)
        return remote(
            RY[g].at[chunk(k)], RZ[g].at[away], o.rz_s.at[g, k], o.rz_r.at[g, away], (p, k, t)
        )

    def rs_z_came(g, i):
        remote(
            RY[g].at[chunk(d)], RZ[g].at[i], o.rz_s.at[g, d], o.rz_r.at[g, i], beside
        ).wait_recv()

    def rs_start(g):
        for i in range(nz):
            rs_y(g, lax.rem(d + 1 + i, nz)).start()

    def rs_mid(g):
        for i in range(nz):
            k = lax.rem(d + 1 + i, nz)
            rs_y(g, k).wait_recv()
            start = pl.multiple_of(k * chunk_rows, 16)

            @pl.loop(0, chunk_rows // 32)
            def _(r):
                rows = pl.ds(pl.multiple_of(start + r * 32, 16), 32)
                both = W[g][y, rows, :].astype(F32) + RY[g][rows, :].astype(F32)
                RY[g][rows, :] = both.astype(BF)

            if i < nz - 1:
                rs_z(g, k).start()

    def rs_end(g, put):
        for i in range(nz - 1):
            rs_z_came(g, i)
        start = pl.multiple_of(d * chunk_rows, 16)

        @pl.loop(0, chunk_rows // 32)
        def _(r):
            rows = pl.ds(pl.multiple_of(r * 32, 16), 32)
            total = RY[g][pl.ds(pl.multiple_of(start + r * 32, 16), 32), :].astype(F32)
            for i in range(nz - 1):
                total = total + RZ[g][i, rows, :].astype(F32)
            put(rows, total)

    def rs_sent(g):
        for i in range(nz):
            k = lax.rem(d + 1 + i, nz)
            rs_y(g, k).wait_send()
            if i < nz - 1:
                rs_z(g, k).wait_send()

    def rs_copies(g):
        return [
            pltpu.make_async_copy(
                buffer.at[pl.ds(first, chunk_rows), pl.ds(0, width)],
                out.at[:, pl.ds(at, width)],
                o.lc.at[g + 3 * i],
            )
            for i, (out, buffer, first, at, width) in enumerate(place[g])
        ]

    def rs_out(g):
        if nz == 1:
            start = 0

            @pl.loop(0, chunk_rows // 32)
            def _(r):
                rows = pl.ds(pl.multiple_of(r * 32, 16), 32)
                (o.oa, o.ob, o.oc)[g][rows, :] = RY[g][rows, :]

        else:

            def put(rows, total):
                for out, buffer, first, at, width in place[g]:
                    into = pl.ds(pl.multiple_of(rows.start + first, 16), 32)
                    buffer[into, :width] = total[:, at : at + width]

            rs_end(g, put)
            for copy in rs_copies(g):
                copy.start()
        rs_sent(g)


    def rows_sib(i, k, n):
        own, landing = ROWS[i]
        src = own.at[y] if n == 0 else landing.at[k]
        return remote(src, landing.at[k], o.qs.at[i, n], o.qr.at[i, n], sibling)

    def rows_beside(i, k):
        own, landing = ROWS[i]
        return remote(own.at[1 - y], landing.at[k], o.qs.at[i, 2], o.qr.at[i, 2], beside)

    def rows_own(i):
        own, landing = ROWS[i]
        return pltpu.make_async_copy(own.at[y], landing.at[t], o.ql.at[i])

    def rows_start(i):
        rows_own(i).start()
        rows_beside(i, t).start()
        rows_sib(i, t, 0).start()

    other = lax.rem(t + 2, 4)

    def rows_pass(i):
        rows_beside(i, other).wait_recv()
        rows_sib(i, other, 1).start()

    def rows_done(i):
        rows_own(i).wait()
        rows_sib(i, t, 0).wait()
        rows_sib(i, other, 1).wait()
        rows_beside(i, t).wait_send()

    def rows_join(i, out_ref):
        landing = ROWS[i][1]
        for k in range(0, 4, 2):
            value = jnp.concatenate(
                [landing[k, :held].astype(F32), landing[k + 1, :held].astype(F32)], axis=0
            )
            out_ref[k * held : (k + 2) * held, :] = value.astype(out_ref.dtype)


    def home_copy(i):
        return remote(o.hs.at[i], o.hr.at[i], o.hx.at[i], o.hy.at[i], beside)

    def home_block(buffer, k):
        value = buffer[pl.ds(pl.multiple_of(k * held, 8), held), :]
        pad = o.hs.shape[1] - held
        return jnp.concatenate([value, jnp.zeros((pad, D), F32)], axis=0).astype(BF)

    def home_send(i, buffer):
        o.hs[i] = home_block(buffer, other)
        home_copy(i).start()

    home_out = (
        pltpu.make_async_copy(o.ho, o.oh.at[y], o.lh.at[0]),
        pltpu.make_async_copy(o.hr.at[0], o.oh.at[1 - y], o.lh.at[1]),
        pltpu.make_async_copy(
            o.gres.at[pl.ds(pl.multiple_of(t * held, 8), held)], o.gh.at[y], o.lh.at[2]
        ),
        pltpu.make_async_copy(o.ext.at[pl.ds(0, held)], o.gh.at[1 - y], o.lh.at[3]),
    )

    barrier = pltpu.get_barrier_semaphore()
    for g in (A, B, C):
        own_copy(g).start()
    when(dec, cross_own.start)
    for peer in (sibling, across, beside):
        pl.semaphore_signal(barrier, inc=1, device_id=peer, device_id_type=MESH)
    for i in range(1, nz):
        pl.semaphore_signal(
            barrier, inc=1, device_id=(p, lax.rem(d + i, nz), t), device_id_type=MESH
        )
    pl.semaphore_wait(barrier, 3 + nz - 1)
    rows_start(0)
    when(enc, lambda: rows_start(2))
    own_copy(A).wait()
    ag_hop(A, 0)
    when(enc, cross_in.start)
    own_copy(B).wait()
    ag_hop(B, 0)
    own_copy(C).wait()

    lane = lax.broadcasted_iota(jnp.int32, (1, 128), 1)
    lo = jnp.where(lane < 64, 1.0, 0.0).astype(BF)
    hi = jnp.where(lane < 64, 0.0, 1.0).astype(BF)

    def rows_loop(fn, step=RT):
        @pl.loop(0, L // step)
        def _(i):
            fn(pl.ds(pl.multiple_of(i * step, step), step))

    def norm_rows(x_ref, gain_no, out_ref):
        def one(rows):
            v = x_ref[rows, :].astype(F32)
            r = lax.rsqrt(jnp.mean(v * v, axis=-1, keepdims=True) + EPSILON)
            out_ref[rows, :] = (v * r * o.g[gain_no : gain_no + 1, :]).astype(BF)

        rows_loop(one)

    def exchange(slot, chunk_fn):
        copies = []
        for n in range(n_cw):
            o.exs[slot, n] = chunk_fn(n).astype(BF)
            copy = remote(
                o.exs.at[slot, n], o.exr.at[slot, n], o.ss.at[slot, n], o.rs.at[slot, n], sibling
            )
            copy.start()
            copies.append(copy)
        return copies

    def landed(copies):
        for copy in copies:
            copy.wait()

    def ex_rows(slot, rows):
        parts = [
            o.exs[slot, n, rows, :].astype(F32) + o.exr[slot, n, rows, :].astype(F32)
            for n in range(n_cw)
        ]
        return jnp.concatenate(parts, axis=1)

    def residual(slot, base_ref, put):
        def one(rows):
            put(rows, base_ref[rows, :].astype(F32) + ex_rows(slot, rows))

        rows_loop(one)

    def keep(ref):
        def put(rows, value):
            ref[rows, :] = value

        return put

    def norm_back(slot, x_ref, gain_no, put):
        o.dgacc[gain_no] = jnp.zeros((8, D), F32)

        def one(rows):
            dh = ex_rows(slot, rows)
            v = x_ref[rows, :].astype(F32)
            r = lax.rsqrt(jnp.mean(v * v, axis=-1, keepdims=True) + EPSILON)
            n = v * r
            dhg = dh * o.g[gain_no : gain_no + 1, :]
            mu = jnp.mean(dhg * n, axis=-1, keepdims=True)
            put(rows, r * (dhg - n * mu))
            o.dgacc[gain_no] += jnp.sum((dh * n).reshape(RT // 8, 8, D), axis=0)

        rows_loop(one)

    def split(a):
        return slice(a * hs, (a + 1) * hs)

    def kv_project():
        for a in range(2):
            r = dot(o.ns[...], W[A][a, :, at_kv:at_ext]).astype(BF)
            o.ks[:, split(a)] = r[:, :hs]
            o.vs[:, split(a)] = r[:, hs:]

    def pair_stack(block):
        return jnp.concatenate([block * lo, block * hi], axis=0)

    def pair_pick(stacked):
        return jnp.where(lane < 64, stacked[:qb_rows], stacked[qb_rows:])

    def attn_fwd(q_ref, mix_ref, mem, own, causal, hooks=()):
        @pl.loop(0, n_blk)
        def _(b):
            for i, hook in enumerate(hooks):
                pl.when(b == i)(hook)
            rows = pl.ds(pl.multiple_of(b * qb_rows, 16), qb_rows)
            wrows = pl.ds(pl.multiple_of(b * qb_rows, 16), win_w)
            sq = o.segq[rows, :]
            if mem:
                o.mm[...] = jnp.where(sq == o.srcseg[...], 0.0, NEG)
            if own:
                allowed = sq == o.segw[b]
                if causal:
                    qi = lax.broadcasted_iota(jnp.int32, (qb_rows, win_w), 0)
                    kj = lax.broadcasted_iota(jnp.int32, (qb_rows, win_w), 1)
                    allowed = allowed & (kj - HALO <= qi)
                o.mo[...] = jnp.where(allowed, 0.0, NEG)

            @pl.loop(0, n_pair)
            def _(j):
                cols = pl.ds(pl.multiple_of(j * 128, 128), 128)
                q2 = pair_stack(q_ref[rows, cols])
                parts = []
                if mem:
                    s = dot_nt(q2, o.ks[:, cols]).reshape(2, qb_rows, L)
                    parts.append(s + o.mm[...][None])
                if own:
                    s = dot_nt(q2, o.kp[wrows, cols]).reshape(2, qb_rows, win_w)
                    parts.append(s + o.tb[pl.ds(2 * j, 2)] + o.mo[...][None])
                top = [jnp.max(s, axis=-1, keepdims=True) for s in parts]
                top = functools.reduce(jnp.maximum, top)
                exps = [jnp.exp(s - top) for s in parts]
                total = sum(jnp.sum(e, axis=-1, keepdims=True) for e in exps)
                inv = 1.0 / total
                probs = [(e * inv).astype(BF).reshape(2 * qb_rows, -1) for e in exps]
                mixed = 0.0
                if mem:
                    o.pm[b * n_pair + j] = probs[0]
                    mixed = mixed + dot(probs[0], o.vs[:, cols])
                if own:
                    o.po[b * n_pair + j] = probs[-1]
                    mixed = mixed + dot(probs[-1], o.vp[wrows, cols])
                mix_ref[rows, cols] = pair_pick(mixed).astype(BF)

    def attn_back(q_ref, mix_ref, mem, own):
        if mem:
            o.dks[...] = jnp.zeros(o.dks.shape, F32)
            o.dvs[...] = jnp.zeros(o.dvs.shape, F32)
        if own:
            o.dkp[...] = jnp.zeros(o.dkp.shape, F32)
            o.dvp[...] = jnp.zeros(o.dvp.shape, F32)
            o.tb[...] = jnp.zeros(o.tb.shape, F32)

        @pl.loop(0, n_blk)
        def _(b):
            rows = pl.ds(pl.multiple_of(b * qb_rows, 16), qb_rows)
            wrows = pl.ds(pl.multiple_of(b * qb_rows, 16), win_w)

            @pl.loop(0, n_pair)
            def _(j):
                cols = pl.ds(pl.multiple_of(j * 128, 128), 128)
                q2 = pair_stack(q_ref[rows, cols])
                do2 = pair_stack(o.dmix[rows, cols])
                mix = mix_ref[rows, cols].astype(F32)
                delta = jnp.sum(
                    do2.astype(F32).reshape(2, qb_rows, 128) * mix[None], axis=-1, keepdims=True
                ).reshape(2 * qb_rows, 1)
                dq2 = 0.0
                if mem:
                    probs = o.pm[b * n_pair + j]
                    dp = dot_nt(do2, o.vs[:, cols])
                    ds = (probs.astype(F32) * (dp - delta)).astype(BF)
                    dq2 = dq2 + dot(ds, o.ks[:, cols])
                    o.dks[:, cols] += dot_tn(ds, q2)
                    o.dvs[:, cols] += dot_tn(probs, do2)
                if own:
                    probs = o.po[b * n_pair + j]
                    dp = dot_nt(do2, o.vp[wrows, cols])
                    ds = (probs.astype(F32) * (dp - delta)).astype(BF)
                    dq2 = dq2 + dot(ds, o.kp[wrows, cols])
                    o.dkp[wrows, cols] += dot_tn(ds, q2)
                    o.dvp[wrows, cols] += dot_tn(probs, do2)
                    o.tb[pl.ds(2 * j, 2)] += ds.astype(F32).reshape(2, qb_rows, win_w)
                o.dq[rows, cols] = (pair_pick(dq2) * (HD**-0.5)).astype(BF)

    def out_project(slot, mix_ref, weight_ref, at):
        mixed = [mix_ref[:, split(a)] for a in range(2)]
        return exchange(
            slot,
            lambda n: sum(
                dot_nt(mixed[a], weight_ref[a, n * CW : (n + 1) * CW, at : at + hs])
                for a in range(2)
            ),
        )

    def mix_grads(weight_ref, at):
        for a in range(2):
            o.dmix[:, split(a)] = dot(o.gb[...], weight_ref[a, :, at : at + hs]).astype(BF)

    fw = fs // 2

    def ff_half(n):
        a = n // 2
        return a, pl.ds(pl.multiple_of((n - 2 * a) * fw, 128), fw)

    def ff_fwd(x_ref):
        norm_rows(x_ref, 1, o.nc)
        ag_wait(B)

        @pl.loop(0, 4)
        def _(n):
            a, half_cols = ff_half(n)
            cols = pl.ds(pl.multiple_of(n * fw, 128), fw)
            o.pre[...] = dot(o.nc[...], W[B][a, :, half_cols])

            def one(rows):
                v = o.pre[rows, :]
                v2 = v * v
                th = jnp.tanh(0.7978845608028654 * v * (1.0 + 0.044715 * v2))
                cdf = 0.5 * (1.0 + th)
                slope = (0.5 * 0.7978845608028654) * v * (1.0 - th * th)
                o.hidden[rows, cols] = (v * cdf).astype(BF)
                o.gp[rows, cols] = (cdf + slope * (1.0 + (3 * 0.044715) * v2)).astype(BF)

            rows_loop(one, 32)

        ag_wait(C)
        return exchange(
            2,
            lambda n: sum(
                dot_nt(o.hidden[:, a * fs : (a + 1) * fs], W[C][a, n * CW : (n + 1) * CW, :])
                for a in range(2)
            ),
        )

    def sides():
        return (1 - y, y)

    def side_cols(a, width):
        return pl.ds(pl.multiple_of(a * width, 128), width)

    def ff_back(x_ref):
        ag_finish(B)
        ag_finish(C)

        @pl.loop(0, 4)
        def _(n):
            a, half_cols = ff_half(n)
            cols = pl.ds(pl.multiple_of(n * fw, 128), fw)
            o.gp[:, cols] = (
                dot(o.gb[...], W[C][a, :, half_cols]) * o.gp[:, cols].astype(F32)
            ).astype(BF)

        copies = exchange(
            0,
            lambda n: sum(
                dot_nt(o.gp[:, a * fs : (a + 1) * fs], W[B][a, n * CW : (n + 1) * CW, :])
                for a in range(2)
            ),
        )
        for i, a in enumerate(sides()):
            W[C][a] = dot_tn(o.gb[...], o.hidden[:, side_cols(a, fs)]).astype(BF)
            if i == 0:
                rs_start(C)
        landed(copies)

        def put(rows, dv):
            new = o.gres[rows, :] + dv
            o.gres[rows, :] = new
            o.gb[rows, :] = new.astype(BF)

        norm_back(0, x_ref, 1, put)

    def ff_weights():
        for i, a in enumerate(sides()):
            W[B][a] = dot_tn(o.nc[...], o.gp[:, side_cols(a, fs)]).astype(BF)
            if i == 0:
                rs_start(B)

    def x_part():
        return pl.ds(pl.multiple_of(core * half, 16), half)

    def x_copy(way):
        rows = x_part()
        return remote(
            o.xsend.at[rows], o.xbuf.at[rows], o.xss.at[way, 0], o.xrs.at[way, 0], across
        )

    def x_recv(way):
        x_copy(way).wait_recv()
        rows = x_part()
        copy = remote(
            o.xbuf.at[rows], o.xbuf.at[rows], o.xss.at[way, 1], o.xrs.at[way, 1], sibling
        )
        copy.start()
        copy.wait()

    def dkv_grads():
        for a in range(2):
            o.dkv[a, :, :hs] = o.dks[:, split(a)].astype(BF)
            o.dkv[a, :, hs:] = o.dvs[:, split(a)].astype(BF)
        return exchange(
            2,
            lambda n: sum(
                dot_nt(o.dkv[a], W[A][a, n * CW : (n + 1) * CW, at_kv:at_ext]) for a in range(2)
            ),
        )

    rows_pass(0)
    when(enc, lambda: rows_pass(2))
    ag_hop(A, 1)
    rows_start(1)
    ag_hop(A, 2)
    ag_hop(C, 0)
    rows_pass(1)
    ag_hop(A, 3)
    rows_done(0)
    rows_join(0, o.x)

    @pl.when(dec)
    def _():
        cross_own.wait()
        cross_in.wait_recv()
        ag_hop(X, 0)

    ag_wait(A)
    o.g[...] = W[A][0, :, at_ext:].astype(F32).T[:8]
    rel_lanes = [dot_tn(W[A][a, :, at_ext:], o.hot[...]) for a in range(2)]
    for h in range(2 * n_pair):
        a = h // (hs // HD)
        row = REL_AT + h - a * (hs // HD)
        line = rel_lanes[a][row : row + 1, :]
        o.tb[h] = pltpu.roll(
            jnp.broadcast_to(line, (qb_rows, win_w)), 0, 1, stride=1, stride_axis=0
        )
    pad = jnp.zeros((HALO, hc), BF)
    for ref in (o.kp, o.vp):
        ref[:HALO, :] = pad
        ref[HALO + L :, :] = pad
    norm_rows(o.x, 0, o.na)
    for a in range(2):
        r = dot(o.na[...], W[A][a, :, :at_o]).astype(BF)
        o.q[:, split(a)] = (r[:, :hs] * (HD**-0.5)).astype(BF)
        o.kp[HALO : HALO + L, split(a)] = r[:, hs : 2 * hs]
        o.vp[HALO : HALO + L, split(a)] = r[:, 2 * hs :]
    ag_hop(B, 1)
    hooks = (
        lambda: ag_hop(C, 1),
        lambda: ag_hop(B, 2),
        lambda: ag_hop(C, 2),
    )

    @pl.when(enc)
    def _():
        rows_done(2)
        rows_join(2, o.nb)
        norm_rows(o.nb, 2, o.ns)
        kv_project()
        attn_fwd(o.q, o.mixa, True, True, False, hooks)

    @pl.when(dec)
    def _():
        attn_fwd(o.q, o.mixa, False, True, True, hooks)
        ag_hop(X, 1)

    ag_hop(B, 3)
    copies = out_project(0, o.mixa, W[A], at_o)
    ag_hop(C, 3)
    landed(copies)
    residual(0, o.x, keep(o.xmid))

    @pl.when(enc)
    def _():
        landed(ff_fwd(o.xmid))

        def put_out(rows, value):
            o.xlate[rows, :] = value
            o.xsend[rows, :] = value.astype(BF)

        residual(2, o.xmid, put_out)
        x_copy(0).start()
        home_send(0, o.xlate)
        o.ho[...] = home_block(o.xlate, t)
        home_out[0].start()
        ag_finish(A)
        rows_done(1)
        rows_join(1, o.gres)
        x_copy(0).wait_send()
        x_recv(1)

        def one(rows):
            value = o.gres[rows, :] + o.xbuf[rows, :].astype(F32)
            o.gres[rows, :] = value
            o.gb[rows, :] = value.astype(BF)

        rows_loop(one)
        ff_back(o.xmid)
        ff_weights()

    @pl.when(dec)
    def _():
        ag_hop(X, 2)
        ag_hop(X, 3)
        ag_wait(X)
        ag_finish(X)
        for a in range(2):
            for k in range(nz):
                for part in range(2):
                    at = part * (D // 2) + k * cross_rows
                    o.xg[a, at : at + cross_rows, :] = W[X][
                        a, k * chunk_rows + part * cross_rows :, :
                    ][:cross_rows]
        o.g[3:4, :] = o.xg[0, :, 2 * hs :].astype(F32).T[:1]
        norm_rows(o.xmid, 3, o.nb)
        for a in range(2):
            r = dot(o.nb[...], o.xg[a, :, :hs]).astype(BF)
            o.qb[:, split(a)] = (r * (HD**-0.5)).astype(BF)
        x_recv(0)
        norm_rows(o.xbuf, 2, o.ns)
        kv_project()
        attn_fwd(o.qb, o.mixb, True, False, False)
        landed(out_project(1, o.mixb, o.xg, hs))
        residual(1, o.xmid, keep(o.xlate))
        landed(ff_fwd(o.xlate))
        residual(2, o.xlate, keep(o.gres))
        home_send(0, o.gres)
        o.ho[...] = home_block(o.gres, t)
        home_out[0].start()
        rows_done(1)
        rows_join(1, o.gres)
        rows_join(1, o.gb)
        ff_back(o.xlate)
        mix_grads(o.xg, hs)
        attn_back(o.qb, o.mixb, True, False)
        copies = dkv_grads()
        parts = [o.dq[:, split(a)] for a in range(2)]
        more = exchange(
            1,
            lambda n: sum(
                dot_nt(parts[a], o.xg[a, n * CW : (n + 1) * CW, :hs]) for a in range(2)
            ),
        )
        ff_weights()
        landed(copies)

        def put_source(rows, dv):
            o.xsend[rows, :] = dv.astype(BF)

        norm_back(2, o.xbuf, 2, put_source)
        x_copy(1).start()
        landed(more)

        def put_mid(rows, dv):
            new = o.gres[rows, :] + dv
            o.gres[rows, :] = new
            o.nc[rows, :] = new.astype(BF)

        norm_back(1, o.xmid, 3, put_mid)
        line = jnp.sum(o.dgacc[3], axis=0, keepdims=True)
        tall = jnp.broadcast_to(line, (EXT, D)).T.astype(BF)
        for a in range(2):
            full = jnp.concatenate(
                [
                    dot_tn(o.nb[...], parts[a]).astype(BF),
                    dot_tn(o.gb[...], o.mixb[:, split(a)]).astype(BF),
                    tall,
                ],
                axis=1,
            )
            for k in range(nz):
                for part in range(2):
                    at = part * (D // 2) + k * cross_rows
                    to = k * chunk_rows + part * cross_rows
                    W[X][a, to : to + cross_rows, :] = full[at : at + cross_rows]
        rs_start(X)
        ag_finish(A)
        rs_mid(C)
        x_copy(1).wait_send()
        o.gb[...] = o.nc[...]

    mix_grads(W[A], at_o)
    for a in range(2):
        W[A][a, :, at_o : at_o + hs] = dot_tn(o.gb[...], o.mixa[:, split(a)]).astype(BF)

    @pl.when(enc)
    def _():
        attn_back(o.q, o.mixa, True, True)
        landed(dkv_grads())

        def put_source(rows, dv):
            pass

        norm_back(2, o.nb, 2, put_source)
        rs_mid(C)

    @pl.when(dec)
    def _():
        attn_back(o.q, o.mixa, False, True)
        rs_mid(B)

    for a in range(2):
        o.dqkv[a, :, :hs] = o.dq[:, split(a)]
        o.dqkv[a, :, hs : 2 * hs] = o.dkp[HALO : HALO + L, split(a)].astype(BF)
        o.dqkv[a, :, 2 * hs :] = o.dvp[HALO : HALO + L, split(a)].astype(BF)
    copies = exchange(
        0,
        lambda n: sum(
            dot_nt(o.dqkv[a], W[A][a, n * CW : (n + 1) * CW, :at_o]) for a in range(2)
        ),
    )
    heads = 2 * n_pair
    acc = jnp.zeros((heads * 8, win_w), F32)
    for k in range(qb_rows // 8):
        part = o.tb[:, 8 * k : 8 * k + 8, :].reshape(heads * 8, win_w)
        acc = acc + (part if k == 0 else pltpu.roll(part, win_w - 8 * k, 1))
    sub = lax.rem(lax.broadcasted_iota(jnp.int32, (heads * 8, win_w), 0), 8)
    diag = jnp.zeros((heads * 8, win_w), F32)
    for k in range(8):
        turned = acc if k == 0 else pltpu.roll(acc, win_w - k, 1)
        diag = diag + jnp.where(sub == k, turned, 0.0)
    lines = jnp.sum(diag.reshape(heads, 8, win_w), axis=1)
    landed(copies)

    def put_in(rows, dv):
        o.gres[rows, :] = o.gres[rows, :] + dv

    norm_back(0, o.x, 0, put_in)
    home_send(1, o.gres)
    home_out[2].start()
    for i, a in enumerate(sides()):
        W[A][a, :, :at_o] = dot_tn(o.na[...], o.dqkv[a]).astype(BF)
        W[A][a, :, at_kv:at_ext] = dot_tn(o.ns[...], o.dkv[a]).astype(BF)
    per = hs // HD
    for a in range(2):
        o.ext[...] = jnp.zeros(o.ext.shape, F32)
        for k in range(3):
            o.ext[k : k + 1, :] = jnp.sum(o.dgacc[k], axis=0, keepdims=True)
        tall = o.ext[...].T
        o.lines[...] = jnp.zeros((EXT, win_w), F32)
        o.lines[REL_AT : REL_AT + per, :] = lines[per * a : per * (a + 1), :]
        whole = o.lines[...]
        high = whole.astype(BF)
        low = (whole - high.astype(F32)).astype(BF)
        tall = tall + dot_nt(o.hot[...], high) + dot_nt(o.hot[...], low)
        W[A][a, :, at_ext:] = tall.astype(BF)
    rs_start(A)
    home_copy(0).wait()
    home_out[1].start()

    @pl.when(enc)
    def _():
        rs_mid(B)

    rs_out(C)

    @pl.when(dec)
    def _():
        rs_mid(X)

    rs_mid(A)
    rs_out(B)

    @pl.when(dec)
    def _():
        def put(rows, total):
            o.xt[rows, :] = total

        rs_end(X, put)
        rs_sent(X)
        o.xo[...] = o.xt[:cross_rows, :]
        cross_out.start()
        o.ox[...] = o.xt[cross_rows:, :].astype(o.ox.dtype)
        cross_out.wait_send()

    @pl.when(enc)
    def _():
        cross_in.wait_send()
        cross_out.wait_recv()
        o.ox[...] = o.xi[...].astype(o.ox.dtype)

    home_copy(1).wait()
    o.ext[...] = o.hr[1].astype(F32)
    home_out[3].start()
    rs_out(A)
    for copy in home_out:
        copy.wait()
    if nz > 1:
        for g in (A, B, C):
            for copy in rs_copies(g):
                copy.wait()


def run_kernel(dims, given):
    L, D, hs, fs, nz, qb_rows, win_w = dims
    hc, fc = 2 * hs, 2 * fs
    n_blk, n_pair, n_cw = L // qb_rows, hc // 128, D // CW
    LP = L + 2 * HALO
    LBP = -(-(L // 4) // 16) * 16
    CR = D // nz
    widths = dict(a=6 * hs + EXT, b=fs, c=fs, x=2 * hs + EXT)
    S = jax.ShapeDtypeStruct
    SUM = F32 if nz > 1 else BF
    outs = dict(
        oh=S((2, LBP, D), BF),
        gh=S((2, L // 4, D), F32),
        oa=S((CR, widths["a"]), SUM),
        ob=S((CR, widths["b"]), SUM),
        oc=S((CR, widths["c"]), SUM),
        ox=S((CR // 2, widths["x"]), SUM),
    )
    V = pltpu.VMEM
    LD, LH, LF = (L, D), (L, hc), (L, fc)
    scratch = dict(
        na=V(LD, BF), ns=V(LD, BF), nb=V(LD, BF), nc=V(LD, BF),
        xmid=V(LD, F32), xlate=V(LD, F32), gres=V(LD, F32),
        q=V(LH, BF), kp=V((LP, hc), BF), vp=V((LP, hc), BF), ks=V(LH, BF), vs=V(LH, BF),
        qb=V(LH, BF), mixa=V(LH, BF), mixb=V(LH, BF),
        pm=V((n_blk * n_pair, 2 * qb_rows, L), BF), po=V((n_blk * n_pair, 2 * qb_rows, win_w), BF),
        hidden=V(LF, BF), gp=V(LF, BF), pre=V((L, fs // 2), F32),
        tb=V((2 * n_pair, qb_rows, win_w), F32),
        mm=V((qb_rows, L), F32), mo=V((qb_rows, win_w), F32),
        dmix=V(LH, BF), dq=V(LH, BF), dqkv=V((2, L, 3 * hs), BF), dkv=V((2, L, 2 * hs), BF),
        dkp=V((LP, hc), F32), dvp=V((LP, hc), F32), dks=V(LH, F32), dvs=V(LH, F32),
        gb=V(LD, BF), xbuf=V(LD, BF), xsend=V(LD, BF),
        exs=V((3, n_cw, L, CW), BF), exr=V((3, n_cw, L, CW), BF), dgacc=V((4, 8, D), F32),
        g=V((8, D), F32), ext=V((LBP, D), F32), lines=V((EXT, win_w), F32),
        x=V(LD, BF), xq=V((4, LBP, D), BF), cq=V((4, LBP, D), BF), mq=V((4, LBP, D), BF),
        hs=V((2, LBP, D), BF), hr=V((2, LBP, D), BF), ho=V((LBP, D), BF),
        xg=V((2, D, widths["x"]), BF), xt=V((CR, widths["x"]), F32),
        xo=V((CR // 2, widths["x"]), F32), xi=V((CR // 2, widths["x"]), F32),
    )
    for g, width in widths.items():
        scratch["w" + g] = V((2, D, width), BF)
        scratch["y" + g] = V((D, width), BF)
        scratch["z" + g] = V((nz - 1, CR, width) if nz > 1 else (1, 16, width), BF)
    sem = pltpu.SemaphoreType.DMA
    scratch.update(ss=sem((3, n_cw)), rs=sem((3, n_cw)), xss=sem((2, 2)), xrs=sem((2, 2)))
    scratch.update(xw=sem((4,)), oc_sem=sem((4,)), lc=sem((5,)), lh=sem((4,)))
    scratch.update(qs=sem((3, 3)), qr=sem((3, 3)), ql=sem((3,)), hx=sem((2,)), hy=sem((2,)))
    for name in ("gr", "gl", "gs", "gz", "gy", "rs_s", "rs_r", "rz_s", "rz_r"):
        scratch[name] = sem((4, nz))
    spec = pl.BlockSpec(memory_space=pltpu.VMEM)
    far = pl.BlockSpec(memory_space=pl.ANY)
    names = list(given) + list(outs) + list(scratch)
    FAR = ["sa", "sb", "sc", "sx", "xs", "cs", "ms", "oh", "gh"]
    if nz > 1:
        FAR += ["oa", "ob", "oc"]
    return pl.pallas_call(
        functools.partial(kernel, dims, names),
        out_shape=list(outs.values()),
        in_specs=[far if name in FAR else spec for name in given],
        out_specs=[far if name in FAR else spec for name in outs],
        scratch_shapes=list(scratch.values()),
        compiler_params=pltpu.CompilerParams(
            collective_id=0, has_side_effects=True, vmem_limit_bytes=63 << 20
        ),
        name="layers",
    )(*given.values())


def body(
    layer_inputs,
    segment_ids,
    slot_ids,
    memory_table,
    buckets,
    self_qkv,
    self_out,
    source_kv,
    ff_in,
    ff_out,
    rel_bias,
    gains,
    cross_query,
    cross_out,
    cross_gain,
    cotangents,
):
    section = lax.axis_index("pipe")
    t = lax.axis_index("tensor")
    nt = lax.axis_size("tensor")
    n_dp = lax.axis_size("dp")
    y = t // 2
    assert nt == 4 and layer_inputs.shape[2] == 2
    D = layer_inputs.shape[3]
    L = segment_ids.shape[2]
    hs = self_qkv.shape[3]
    fs = ff_in.shape[2]
    qb_rows, win_w = 160, 256
    rows = D // n_dp
    nz = n_dp if (rows // 2) % 32 == 0 else 1
    dims = (L, D, hs, fs, nz, qb_rows, win_w)

    held = L // nt
    fill = -(-held // 16) * 16 - held

    def by_row(block):
        return jnp.pad(block.transpose(1, 0, 2), ((0, 0), (0, fill), (0, 0)))

    xs = by_row(layer_inputs[0])
    cs = by_row(cotangents[0])
    ms = jnp.pad(memory_table[slot_ids.T], ((0, 0), (0, fill), (0, 0)))
    segs = lax.dynamic_index_in_dim(segment_ids, y, 1, keepdims=False)
    own_seg = lax.dynamic_index_in_dim(segs, section, 0, keepdims=False)
    padded = jnp.pad(own_seg, (HALO, HALO), constant_values=-1)
    segw = jnp.stack(
        [padded[b * qb_rows : b * qb_rows + win_w][None] for b in range(L // qb_rows)]
    )
    srcseg = jnp.where(section == 0, jnp.arange(L, dtype=jnp.int32) // MEM, segs[0])[None]

    heads = rel_bias.shape[2]
    nb_rows = rel_bias.shape[1]
    ext = jnp.pad(gains[0].T, ((0, 0), (0, EXT - gains.shape[1]))) + jnp.pad(
        rel_bias[0], ((0, rows - nb_rows), (REL_AT, EXT - REL_AT - heads))
    )
    shards = [
        jnp.concatenate(
            [
                self_qkv[0].reshape(rows, 3 * hs),
                self_out[0].T,
                source_kv[0].reshape(rows, 2 * hs),
                ext,
            ],
            axis=1,
        ),
        ff_in[0],
        ff_out[0].T,
        jnp.concatenate(
            [cross_query, cross_out.T, jnp.pad(cross_gain[:, None], ((0, 0), (0, EXT - 1)))],
            axis=1,
        ),
    ]
    if nz != n_dp:
        shards = [lax.all_gather(shard, "dp", axis=0, tiled=True) for shard in shards]
    window = jnp.concatenate([buckets[L - HALO : L + HALO], jnp.full((win_w - 2 * HALO,), -1)])
    place = jnp.arange(D, dtype=jnp.int32)
    bucket_at = jnp.where(place % rows < nb_rows, place // rows * nb_rows + place % rows, -2)
    hot = (window[None, :] == bucket_at[:, None]).astype(BF)

    given = dict(
        xs=xs, cs=cs, ms=ms, segq=own_seg[:, None], segw=segw, srcseg=srcseg, hot=hot,
        sa=shards[0], sb=shards[1], sc=shards[2], sx=shards[3],
    )
    oh, gh, *sums = run_kernel(dims, given)
    if nz != n_dp:
        sums = [
            lax.psum_scatter(full, "dp", scatter_dimension=0, tiled=True).astype(F32)
            for full in sums
        ]
    ga, gb, gc, gx = sums

    at_ext = 6 * hs
    return (
        oh[:, :held].transpose(1, 0, 2)[None],
        gh.transpose(1, 0, 2)[None],
        ga[:, : 3 * hs].reshape(1, rows, 3, hs),
        ga[:, 3 * hs : 4 * hs].T[None],
        ga[:, 4 * hs : at_ext].reshape(1, rows, 2, hs),
        gb[None],
        gc.T[None],
        ga[:nb_rows, at_ext + REL_AT : at_ext + REL_AT + heads][None],
        ga[:, at_ext : at_ext + gains.shape[1]].T[None],
        gx[:, :hs],
        gx[:, hs : 2 * hs].T,
        gx[:, 2 * hs],
    )


def solution(mesh):
    placed = (
        P("pipe", "tensor", "dp", None),
        P(None, "dp", None),
        P("tensor", "dp"),
        P(),
        P(),
        P("pipe", "dp", None, "tensor"),
        P("pipe", "tensor", "dp"),
        P("pipe", "dp", None, "tensor"),
        P("pipe", "dp", "tensor"),
        P("pipe", "tensor", "dp"),
        P("pipe", "dp", "tensor"),
        P("pipe", None, "dp"),
        P(("pipe", "dp"), "tensor"),
        P("tensor", ("pipe", "dp")),
        P(("pipe", "dp")),
        P("pipe", "tensor", "dp", None),
    )
    return jax.shard_map(
        body,
        mesh=mesh,
        in_specs=placed,
        out_specs=(
            P("pipe", "tensor", "dp", None),
            P("pipe", "tensor", "dp", None),
            P("pipe", "dp", None, "tensor"),
            P("pipe", "tensor", "dp"),
            P("pipe", "dp", None, "tensor"),
            P("pipe", "dp", "tensor"),
            P("pipe", "tensor", "dp"),
            P("pipe", "dp", "tensor"),
            P("pipe", None, "dp"),
            P(("pipe", "dp"), "tensor"),
            P("tensor", ("pipe", "dp")),
            P(("pipe", "dp")),
        ),
        check_vma=False,
    )
```

time: 1970 us -> 365 us (0.19); the launches traced: 1950 us -> 361 us
  local copies, waits for them, and re-layouts: 769 us -> 37.9 us
  waiting for transfers between devices: 467 us -> 0 us
  blocking collectives: 398 us -> 0 us
  Pallas kernels: 0 us -> 317 us
  matrix products: 171 us -> 0 us
  other arithmetic: 107 us -> 5.09 us
  between operations: 22.7 us -> 0.99 us
    gather x7 -> x1, local copies, waits for them, and re-layouts: 503 us -> 4.94 us  [body(): ms = jnp.pad(memory_table[slot_ids.T], ((0, 0), (0, fill), (0, 0)))]
    reduce_scatter x23 -> x0, waiting for transfers between devices: 366 us -> none  [the longest x9 140 us: collect(): lax.psum_scatter(term_rows(jnp.int32(0), lax.axis_size('tensor') * shard_...]
    all_gather x28 -> x0, blocking collectives: 344 us -> none  [the longest x9 105 us: spread(): return lax.all_gather(rows_part, 'tensor', axis=0, tiled=True)]
    pallas_call x0 -> x1, Pallas kernels: none -> 317 us  [run_kernel(): pl.pallas_call(functools.partial(kernel, dims, names), out_shape=list(out...]
    dot_general x137 -> x0, matrix products: 171 us -> none  [the longest x21 35 us: project(): jnp.einsum('qre,ed->qrd', left, weight, preferred_element_type=jnp.float32)]
    unnamed x861 -> x23, local copies, waits for them, and re-layouts: 97.9 us -> 12.8 us
    unnamed x37 -> x0, waiting for transfers between devices: 60.2 us -> none
    reshape x12 -> x1, local copies, waits for them, and re-layouts: 60.4 us -> 1.03 us  [body(): ga[:, 4 * hs:at_ext].reshape(1, rows, 2, hs)]
  transfers between devices with their start and end apart: 35 -> 0, of which waited for: 22 -> 0; matrix products, arithmetic and copies ran while one was open for 17% -> 0% of each run, Pallas kernels for 0% -> 0%
where the time goes in v1:
time: 365 us; the launch traced here: 361 us
  Pallas kernels  317 us (87%)
  local copies, waits for them, and re-layouts  37.9 us (10%)
  other arithmetic  5.09 us (1%)
    pallas_call x1, Pallas kernels, run_kernel(): pl.pallas_call(functools.partial(kernel, dims, names), out_shape=list(out...  317 us
    unnamed x23, local copies, waits for them, and re-layouts  12.8 us

profile of v1, /device:TPU:9, one launch (start us, length us, event | category | flops | bytes accessed | tf_op | source)
XLA Modules:
  0.0 361.5 jit_solution(17672066903050520161)
XLA Ops:
  0.6 0.0 copy-start.3
  0.7 0.0 copy-start.2
  0.7 0.8 slice.49
  1.5 0.8 dynamic-slice.2
  2.3 0.7 compare_select_fusion
  3.0 0.1 reshape.107
  3.0 1.3 broadcast_select_fusion.refs_5_
  4.3 0.8 copy.49
  5.1 0.7 fusion.13
  5.8 0.7 constant_dynamic-slice_fusion
  6.5 0.1 pad_slice_fusion.1
  6.6 0.6 pad_add_fusion.1.refs_4_
  7.2 0.8 copy.52
  7.9 0.8 copy.48
  8.8 0.1 pad_add_fusion
  8.8 0.9 copy.51
  9.7 1.5 fusion.1.refs_10_
  11.3 1.0 copy.47
  12.3 1.1 reshape_squeeze.7
  13.4 0.8 copy.53.refs_3_
  14.2 1.1 copy.46
  15.3 0.2 copy.50
  15.5 0.9 concatenate.10.refs_7_
  16.4 4.9 %gather_fusion = bf16[240,768]{1,0:T(8,128)(2,1)S(1)} fusion(bf16[4096,768]{1,0:T(8,128)(2,1)} %param.19, s32[1024]{0:T(1024)S(1)} %pad_clamp_fusion), kind=kCustom, calls=%fused_computation | custom fusion | bytes 738240 | tf_op jit(solution)/shard_map/gather | solution.py:1018
  21.4 0.8 pad.29.refs_2_
  22.1 0.0 copy-done.2
  22.2 0.8 pad.27.refs_0_
  23.0 0.0 copy-done.3
  23.0 0.8 pad.28.refs_1_
  23.8 0.9 compare_convert_fusion.refs_6_
  24.7 317.5 %layers.1 = (bf16[2,128,768]{2,1,0:T(8,128)(2,1)}, f32[2,120,768]{2,1,0:T(8,128)}, f32[192,1280]{1,0:T(8,128)}, f32[192,768]{1,0:T(8,128)}, f32[192,768]{1,0:T(8,128)}, /*index=5*/f32[96,512]{1,0:T(8,128)}) custom-call(bf16[2,128,768]{2,1,0:T(8,128)(2,1)} %pad.27.refs_0_, bf16[2,128,768]{2,1,0:T(8,128)(2,1)} %pad.28.refs_1_, ...), custom_call_target="tpu_custom_call" | custom-call | tf_op jit(solution)/shard_map/layers/pallas_call | solution.py:964
  342.2 0.0 copy-start.1
  342.2 0.0 copy-start
  342.2 1.1 slice_bitcast_fusion
  343.3 1.0 copy.56
  344.3 2.4 copy.57
  346.7 1.4 slice_reduce_fusion
  348.1 1.6 slice_bitcast_fusion.2
  349.7 0.7 copy.62
  350.5 0.8 slice_bitcast_fusion.4
  351.2 0.6 copy.60
  351.9 0.9 slice_bitcast_fusion.3
  352.8 0.7 copy.61
  353.4 1.1 slice_bitcast_fusion.1
  354.5 0.8 copy.59
  355.3 1.0 slice.53
  356.3 1.1 slice.51
  357.4 0.2 copy.54
  357.6 1.1 copy.58
  358.6 1.0 reshape.104
  359.7 0.0 copy-done.1
  359.7 0.8 copy.71
  360.5 0.0 copy-done
  360.5 0.8 copy.72
  (5 shorter events, 0.1 us)
Async XLA Ops:
  0.6 22.3 %copy-start.3 = (bf16[1,120,2,768]{3,2,1,0:T(2,128)(2,1)S(1)}, bf16[1,120,2,768]{3,2,1,0:T(2,128)(2,1)}, u32[]{:S(2)}) copy-start(bf16[1,120,2,768]{3,2,1,0:T(2,128)(2,1)} %param.31) | copy-start | bytes 1105924
  0.7 21.5 %copy-start.2 = (bf16[1,120,2,768]{3,2,1,0:T(2,128)(2,1)S(1)}, bf16[1,120,2,768]{3,2,1,0:T(2,128)(2,1)}, u32[]{:S(2)}) copy-start(bf16[1,120,2,768]{3,2,1,0:T(2,128)(2,1)} %param.16) | copy-start | bytes 1105924
  342.2 17.5 %copy-start.1 = (f32[192,768]{1,0:T(8,128)S(1)}, f32[192,768]{1,0:T(8,128)}, u32[]{:S(2)}) copy-start(f32[192,768]{1,0:T(8,128)} %get-tuple-element.21) | copy-start | bytes 1769476
  342.2 18.3 %copy-start = (f32[192,768]{1,0:T(8,128)S(1)}, f32[192,768]{1,0:T(8,128)}, u32[]{:S(2)}) copy-start(f32[192,768]{1,0:T(8,128)} %get-tuple-element.22) | copy-start | bytes 1769476

commit v2 on v1

--- a/solution.py
+++ b/solution.py
@@ -974,6 +974,156 @@
     )(*given.values())
 
 
+def prep_kernel(dims, n_dp, names, *refs):
+    L, D, hs, fs, nz, qb_rows, win_w = dims
+    o = Refs()
+    for name, ref in zip(names, refs, strict=True):
+        setattr(o, name, ref)
+    section = lax.axis_index("pipe")
+    y = lax.axis_index("tensor") // 2
+    rows = D // n_dp
+    held = L // 4
+    for raw, out in ((o.li, o.xs), (o.co, o.cs)):
+        o.tmp[...] = raw[...].astype(F32)
+        pad = jnp.zeros((out.shape[1] - held, D), F32)
+        for r in range(2):
+            out[r] = jnp.concatenate([o.tmp[:, r, :], pad], axis=0).astype(BF)
+    for i in range(3):
+        o.sa[:, i * hs : (i + 1) * hs] = o.qkv[i]
+    o.sa[:, 3 * hs : 4 * hs] = o.so[...].astype(F32).T.astype(BF)
+    for i in range(2):
+        o.kvt[...] = o.kv[...].astype(F32)
+        o.sa[:, (4 + i) * hs : (5 + i) * hs] = o.kvt[:, i, :].astype(BF)
+    n_gain = o.gain.shape[0]
+    o.ext[...] = jnp.zeros(o.ext.shape, F32)
+    o.ext[:n_gain, :rows] = o.gain[...].astype(F32)
+    tall = o.ext[...].T
+    o.wide[...] = tall
+    nb_rows, heads = o.rel.shape
+    o.wide[:nb_rows, REL_AT : REL_AT + heads] = o.rel[...].astype(F32)
+    o.sa[:, 6 * hs :] = o.wide[:rows, :].astype(BF)
+    o.sx[:, :hs] = o.cq[...]
+    o.sx[:, hs : 2 * hs] = o.cw[...].astype(F32).T.astype(BF)
+    half = o.cg.shape[1]
+    o.ext[...] = jnp.zeros(o.ext.shape, F32)
+    o.ext[:1, :half] = o.cg[...].astype(F32)
+    o.wide[...] = o.ext[...].T
+    o.sx[:, 2 * hs :] = o.wide[:half, :].astype(BF)
+    own = o.seg[section, pl.ds(y, 1), :]
+    first = o.seg[0, pl.ds(y, 1), :]
+    o.segq[...] = jnp.broadcast_to(own.astype(F32), (8, L)).T[:, :1].astype(jnp.int32)
+    slots = lax.broadcasted_iota(jnp.int32, (1, L), 1).astype(F32)
+    slots = jnp.floor((slots + 0.5) * (1.0 / MEM)).astype(jnp.int32)
+    o.srcseg[...] = jnp.where(section == 0, slots, first)
+    o.line[...] = jnp.full(o.line.shape, -1, jnp.int32)
+    o.line[:, HALO : HALO + L] = own
+    for b in range(L // qb_rows):
+        o.segw[b] = o.line[:, b * qb_rows : b * qb_rows + win_w]
+    at = lax.broadcasted_iota(jnp.int32, (rows, win_w), 0)
+    for k in range(n_dp):
+        same = (at < nb_rows) & (o.win[...] == at + k * nb_rows)
+        o.hotf[k * rows : (k + 1) * rows, :] = jnp.where(same, 1.0, 0.0)
+    o.hot[...] = o.hotf[...].astype(BF)
+
+
+def run_prep(dims, n_dp, given):
+    L, D, hs, fs, nz, qb_rows, win_w = dims
+    rows, held = D // n_dp, L // 4
+    LBP = -(-held // 16) * 16
+    S = jax.ShapeDtypeStruct
+    outs = dict(
+        xs=S((2, LBP, D), BF),
+        cs=S((2, LBP, D), BF),
+        sa=S((rows, 6 * hs + EXT), BF),
+        sx=S((rows // 2, 2 * hs + EXT), BF),
+        segq=S((L, 1), jnp.int32),
+        segw=S((L // qb_rows, 1, win_w), jnp.int32),
+        srcseg=S((1, L), jnp.int32),
+        hot=S((D, win_w), BF),
+    )
+    V = pltpu.VMEM
+    up = -(-rows // 128) * 128
+    scratch = dict(
+        tmp=V((held, 2, D), F32),
+        kvt=V((rows, 2, hs), F32),
+        ext=V((EXT, up), F32),
+        wide=V((up, EXT), F32),
+        line=V((1, L + 2 * HALO), jnp.int32),
+        hotf=V((D, win_w), F32),
+    )
+    spec = pl.BlockSpec(memory_space=pltpu.VMEM)
+    names = list(given) + list(outs) + list(scratch)
+    return pl.pallas_call(
+        functools.partial(prep_kernel, dims, n_dp, names),
+        out_shape=list(outs.values()),
+        in_specs=[spec] * len(given),
+        out_specs=[spec] * len(outs),
+        scratch_shapes=list(scratch.values()),
+        compiler_params=pltpu.CompilerParams(vmem_limit_bytes=60 << 20),
+        name="prep",
+    )(*given.values())
+
+
+def finish_kernel(dims, names, *refs):
+    L, D, hs, fs, nz, qb_rows, win_w = dims
+    o = Refs()
+    for name, ref in zip(names, refs, strict=True):
+        setattr(o, name, ref)
+    o.ffi[...] = o.gb[...]
+    o.ffo[...] = o.gc[...]
+    for r in range(2):
+        o.gin[:, r, :] = o.gh[r]
+        o.tmp[:, r, :] = o.oh[r, : L // 4].astype(F32)
+    o.out[...] = o.tmp[...].astype(BF)
+    for i in range(3):
+        o.qkv[i] = o.ga[:, i * hs : (i + 1) * hs]
+    o.so[...] = o.ga[:, 3 * hs : 4 * hs].T
+    for i in range(2):
+        o.kv[:, i, :] = o.ga[:, (4 + i) * hs : (5 + i) * hs]
+    ext = o.ga[:, 6 * hs :].T
+    for i in range(o.gain.shape[0]):
+        o.gain[i] = ext[i : i + 1]
+    heads, _, nb_rows = o.rel.shape
+    for i in range(heads):
+        o.rel[i] = ext[REL_AT + i : REL_AT + i + 1, :nb_rows]
+    o.cq[...] = o.gx[:, :hs]
+    o.co[...] = o.gx[:, hs : 2 * hs].T
+    o.cg[...] = o.gx[:, 2 * hs :].T[:1]
+
+
+def run_finish(dims, rel_shape, sums):
+    L, D, hs, fs, nz, qb_rows, win_w = dims
+    rows = sums[2].shape[0]
+    held = L // 4
+    S = jax.ShapeDtypeStruct
+    outs = dict(
+        out=S((held, 2, D), BF),
+        gin=S((held, 2, D), F32),
+        qkv=S((3, rows, hs), F32),
+        so=S((hs, rows), F32),
+        kv=S((rows, 2, hs), F32),
+        rel=S((rel_shape[1], 1, rel_shape[0]), F32),
+        gain=S((3, 1, rows), F32),
+        cq=S((rows // 2, hs), F32),
+        co=S((hs, rows // 2), F32),
+        cg=S((1, rows // 2), F32),
+        ffi=S((rows, fs), F32),
+        ffo=S((rows, fs), F32),
+    )
+    spec = pl.BlockSpec(memory_space=pltpu.VMEM)
+    return pl.pallas_call(
+        functools.partial(
+            finish_kernel, dims, ["oh", "gh", "ga", "gb", "gc", "gx", *outs, "tmp"]
+        ),
+        out_shape=list(outs.values()),
+        in_specs=[spec] * 6,
+        out_specs=[spec] * len(outs),
+        scratch_shapes=[pltpu.VMEM((held, 2, D), F32)],
+        compiler_params=pltpu.CompilerParams(vmem_limit_bytes=60 << 20),
+        name="finish",
+    )(*sums)
+
+
 def body(
     layer_inputs,
     segment_ids,
@@ -992,11 +1142,8 @@
     cross_gain,
     cotangents,
 ):
-    section = lax.axis_index("pipe")
-    t = lax.axis_index("tensor")
     nt = lax.axis_size("tensor")
     n_dp = lax.axis_size("dp")
-    y = t // 2
     assert nt == 4 and layer_inputs.shape[2] == 2
     D = layer_inputs.shape[3]
     L = segment_ids.shape[2]
@@ -1006,55 +1153,37 @@
     rows = D // n_dp
     nz = n_dp if (rows // 2) % 32 == 0 else 1
     dims = (L, D, hs, fs, nz, qb_rows, win_w)
-
     held = L // nt
     fill = -(-held // 16) * 16 - held
-
-    def by_row(block):
-        return jnp.pad(block.transpose(1, 0, 2), ((0, 0), (0, fill), (0, 0)))
-
-    xs = by_row(layer_inputs[0])
-    cs = by_row(cotangents[0])
-    ms = jnp.pad(memory_table[slot_ids.T], ((0, 0), (0, fill), (0, 0)))
-    segs = lax.dynamic_index_in_dim(segment_ids, y, 1, keepdims=False)
-    own_seg = lax.dynamic_index_in_dim(segs, section, 0, keepdims=False)
-    padded = jnp.pad(own_seg, (HALO, HALO), constant_values=-1)
-    segw = jnp.stack(
-        [padded[b * qb_rows : b * qb_rows + win_w][None] for b in range(L // qb_rows)]
-    )
-    srcseg = jnp.where(section == 0, jnp.arange(L, dtype=jnp.int32) // MEM, segs[0])[None]
-
-    heads = rel_bias.shape[2]
-    nb_rows = rel_bias.shape[1]
-    ext = jnp.pad(gains[0].T, ((0, 0), (0, EXT - gains.shape[1]))) + jnp.pad(
-        rel_bias[0], ((0, rows - nb_rows), (REL_AT, EXT - REL_AT - heads))
-    )
-    shards = [
-        jnp.concatenate(
-            [
-                self_qkv[0].reshape(rows, 3 * hs),
-                self_out[0].T,
-                source_kv[0].reshape(rows, 2 * hs),
-                ext,
-            ],
-            axis=1,
+    ids = jnp.pad(slot_ids.T, ((0, 0), (0, fill)))
+    ms = memory_table.at[ids].get(mode="promise_in_bounds")
+    window = jnp.pad(
+        buckets[L - HALO : L + HALO], (0, win_w - 2 * HALO), constant_values=-1
+    )
+    prepared = run_prep(
+        dims,
+        n_dp,
+        dict(
+            li=layer_inputs[0],
+            co=cotangents[0],
+            qkv=self_qkv[0].transpose(1, 0, 2),
+            so=self_out[0],
+            kv=source_kv[0],
+            gain=gains[0],
+            rel=rel_bias[0],
+            cq=cross_query,
+            cw=cross_out,
+            cg=cross_gain[None],
+            seg=segment_ids,
+            win=window[None],
         ),
-        ff_in[0],
-        ff_out[0].T,
-        jnp.concatenate(
-            [cross_query, cross_out.T, jnp.pad(cross_gain[:, None], ((0, 0), (0, EXT - 1)))],
-            axis=1,
-        ),
-    ]
+    )
+    xs, cs, sa, sx, segq, segw, srcseg, hot = prepared
+    shards = [sa, ff_in[0], ff_out[0].T, sx]
     if nz != n_dp:
         shards = [lax.all_gather(shard, "dp", axis=0, tiled=True) for shard in shards]
-    window = jnp.concatenate([buckets[L - HALO : L + HALO], jnp.full((win_w - 2 * HALO,), -1)])
-    place = jnp.arange(D, dtype=jnp.int32)
-    bucket_at = jnp.where(place % rows < nb_rows, place // rows * nb_rows + place % rows, -2)
-    hot = (window[None, :] == bucket_at[:, None]).astype(BF)
-
     given = dict(
-        xs=xs, cs=cs, ms=ms, segq=own_seg[:, None], segw=segw, srcseg=srcseg, hot=hot,
+        xs=xs, cs=cs, ms=ms, segq=segq, segw=segw, srcseg=srcseg, hot=hot,
         sa=shards[0], sb=shards[1], sc=shards[2], sx=shards[3],
     )
     oh, gh, *sums = run_kernel(dims, given)
@@ -1063,22 +1192,21 @@
             lax.psum_scatter(full, "dp", scatter_dimension=0, tiled=True).astype(F32)
             for full in sums
         ]
-    ga, gb, gc, gx = sums
-
-    at_ext = 6 * hs
+    done = run_finish(dims, rel_bias.shape[1:], [oh, gh, *sums])
+    out, gin, qkv, so, kv, rel, gain, cq, co, cg, ff_i, ff_o = done
     return (
-        oh[:, :held].transpose(1, 0, 2)[None],
-        gh.transpose(1, 0, 2)[None],
-        ga[:, : 3 * hs].reshape(1, rows, 3, hs),
-        ga[:, 3 * hs : 4 * hs].T[None],
-        ga[:, 4 * hs : at_ext].reshape(1, rows, 2, hs),
-        gb[None],
-        gc.T[None],
-        ga[:nb_rows, at_ext + REL_AT : at_ext + REL_AT + heads][None],
-        ga[:, at_ext : at_ext + gains.shape[1]].T[None],
-        gx[:, :hs],
-        gx[:, hs : 2 * hs].T,
-        gx[:, 2 * hs],
+        out[None],
+        gin[None],
+        qkv.transpose(1, 0, 2)[None],
+        so[None],
+        kv[None],
+        ff_i[None],
+        ff_o.T[None],
+        rel.transpose(1, 2, 0),
+        gain.transpose(1, 0, 2),
+        cq,
+        co,
+        cg[0],
     )
 
 

time: 365 us -> 338 us (0.926)
  local copies, waits for them, and re-layouts: 37.9 us -> 8.4 us
  Pallas kernels: 317 us -> 325 us
  other arithmetic: 5.09 us -> 0.69 us
    unnamed x23 -> x0, local copies, waits for them, and re-layouts: 12.8 us -> none
    pallas_call x0 -> x2, Pallas kernels: none -> 8.35 us  [the longest x1 4.43 us: run_finish(): pl.pallas_call(functools.partial(finish_kernel, dims, ['oh', 'gh', 'ga',...]
    broadcast_in_dim x8 -> x0, local copies, waits for them, and re-layouts: 6.22 us -> none  [the longest x2 1.53 us: body(): own_seg[:, None]]
    slice x6 -> x0, local copies, waits for them, and re-layouts: 4.52 us -> none  [the longest x1 1.42 us: body(): gx[:, 2 * hs]]
where the time goes in v2:
time: 338 us; the launch traced here: 335 us
  Pallas kernels  325 us (96%)
  local copies, waits for them, and re-layouts  8.4 us (2%)
    pallas_call x1, Pallas kernels, run_kernel(): pl.pallas_call(functools.partial(kernel, dims, names), out_shape=list(out...  317 us

profile of v2, /device:TPU:9, one launch (start us, length us, event | category | flops | bytes accessed | tf_op | source)
XLA Modules:
  0.0 335.4 jit_solution(13645356648278452345)
XLA Ops:
  0.6 0.8 slice.3
  1.4 0.6 pad.8
  2.0 0.7 fusion
  2.7 1.3 copy.28.refs_6_
  4.0 5.7 %gather_fusion = bf16[256,768]{1,0:T(8,128)(2,1)} fusion(bf16[4096,768]{1,0:T(8,128)(2,1)} %param.19, s32[1024]{0:T(1024)S(1)} %pad_clamp_fusion), kind=kCustom, calls=%fused_computation | custom fusion | bytes 787456 | tf_op jit(solution)/shard_map/gather | solution.py:1159
  9.7 3.9 %prep.1 = (bf16[2,128,768]{2,1,0:T(8,128)(2,1)}, bf16[2,128,768]{2,1,0:T(8,128)(2,1)}, bf16[192,1280]{1,0:T(8,128)(2,1)}, bf16[96,512]{1,0:T(8,128)(2,1)}, s32[4...) custom-call(bf16[120,2,768]{2,1,0:T(2,128)(2,1)} %bitcast.34, ...), custom_call_target="tpu_custom_call" | custom-call | tf_op jit(solution)/shard_map/prep/pallas_call | solution.py:1056
  13.7 317.1 %layers.1 = (bf16[2,128,768]{2,1,0:T(8,128)(2,1)}, f32[2,120,768]{2,1,0:T(8,128)}, f32[192,1280]{1,0:T(8,128)}, f32[192,768]{1,0:T(8,128)}, f32[192,768]{1,0:T(8,128)}, /*index=5*/f32[96,512]{1,0:T(8,128)}) custom-call(bf16[2,128,768]{2,1,0:T(8,128)(2,1)} %get-tuple-element.38.refs_0_, bf16[2,128,768]{2,1,0:T(8,128)(2,1)} %get-tuple-element.39.refs_1_, ...), custom_call_target="tpu_custom_call" | custom-call | tf_op jit(solution)/shard_map/layers/pallas_call | solution.py:964
  330.7 4.4 %finish.1 = (bf16[120,2,768]{2,1,0:T(2,128)(2,1)}, f32[120,2,768]{2,1,0:T(2,128)}, f32[3,192,192]{2,1,0:T(8,128)}, f32[192,192]{1,0:T(8,128)}, f32[192,2,192]{2,...) custom-call(bf16[2,128,768]{2,1,0:T(8,128)(2,1)} %get-tuple-element., ...), custom_call_target="tpu_custom_call" | custom-call | tf_op jit(solution)/shard_map/finish/pallas_call | solution.py:1114
  (1 shorter events, 0.0 us)

commit v3 on v2

--- a/solution.py
+++ b/solution.py
@@ -18,7 +18,6 @@
 BF = jnp.bfloat16
 F32 = jnp.float32
 MESH = pl.DeviceIdType.MESH
-CW = 256
 RT = 48
 
 
@@ -46,7 +45,6 @@
     cross_rows = chunk_rows // 2
     n_blk = L // qb_rows
     n_pair = hc // 128
-    n_cw = D // CW
     o = Refs()
     for name, ref in zip(names, refs, strict=True):
         setattr(o, name, ref)
@@ -56,6 +54,8 @@
     enc, dec = p == 0, p == 1
     core = lax.rem(t, 2)
     y = t // 2
+    z = d if nz > 1 else 0
+    skew = (1 - p, d, lax.rem(t + 2, 4))
     sibling = (p, d, t + 1 - 2 * core)
     across = (1 - p, d, t)
     beside = (p, d, lax.rem(t + 2, 4))
@@ -66,11 +66,27 @@
     W = (o.wa, o.wb, o.wc, o.wx)
     RY = (o.ya, o.yb, o.yc, o.yx)
     RZ = (o.za, o.zb, o.zc, o.zx)
-    place = (
-        [(o.oa, o.xmid, chunk_rows, 0, fs), (o.oa, o.xlate, chunk_rows, fs, 6 * hs + EXT - fs)],
-        [(o.ob, o.xlate, 0, 0, fs)],
-        [(o.oc, o.xmid, 0, 0, fs)],
-    )
+    RB, RC, RX, RQ, RK, RG = range(6)
+    REDUCE = {
+        RB: (B, 0, fs),
+        RC: (C, 0, fs),
+        RX: (X, 0, 2 * hs + EXT),
+        RQ: (A, 0, at_kv),
+        RK: (A, at_kv, 2 * hs),
+        RG: (A, at_ext, EXT),
+    }
+    LEAVE = {
+        RB: (o.ob, o.xlate, 0, 0),
+        RC: (o.oc, o.xmid, 0, 0),
+        RQ: (o.oa, o.xmid, chunk_rows, 0),
+        RK: (o.oa, o.xlate, chunk_rows, 0),
+        RG: (o.oa, o.xlate, chunk_rows, 2 * hs),
+    }
+    STAGE = {} if nz == 1 else {
+        A: o.hidden.at[pl.ds(0, chunk_rows), pl.ds(0, 6 * hs + EXT)],
+        B: o.gp.at[pl.ds(0, chunk_rows), pl.ds(0, fs)],
+        C: o.gp.at[pl.ds(0, chunk_rows), pl.ds(fs, fs)],
+    }
     ROWS = ((o.xs, o.xq), (o.cs, o.cq), (o.ms, o.mq))
 
     def chunk(k):
@@ -105,10 +121,10 @@
 
     def ag_each(g, h, act):
         if h == 0:
-            act(d, d + 1 < nz, d > 0, True)
+            act(z, z + 1 < nz, z > 0, True)
         else:
-            act(d - h, d + 1 < nz, False, d - h >= 0)
-            act(d + h, False, d > 0, d + h < nz)
+            act(z - h, z + 1 < nz, False, z - h >= 0)
+            act(z + h, False, z > 0, z + h < nz)
 
     def when(cond, fn):
         if cond is True:
@@ -116,7 +132,64 @@
         elif cond is not False:
             pl.when(cond)(fn)
 
-    def ag_hop(g, h):
+
+    def ag_skew(g):
+        return remote(W[g].at[y, chunk(z)], STAGE[g], o.gd.at[g, 0], o.gd.at[g, 1], skew)
+
+    def ag_relay(g):
+        slot = W[g].at[1 - y, chunk(z)]
+        return remote(STAGE[g], slot, o.gd.at[g, 2], o.gy.at[g, z], across)
+
+    def ag_pass_on(g):
+        ag_skew(g).wait_recv()
+        ag_relay(g).start()
+
+    def ag_aside(g, k, own, wait):
+        act = (lambda c: c.wait_send()) if wait else (lambda c: c.start())
+        if own and g in STAGE:
+            pl.when(enc)(lambda: act(ag_skew(g)))
+            pl.when(dec)(lambda: act(ag_beside(g, k)))
+        elif not own and g == C:
+            pl.when(enc)(lambda: act(ag_beside(g, k)))
+        else:
+            act(ag_beside(g, k))
+
+
+    def ag_also(k, way):
+        slot = W[C].at[1 - y, chunk(k)]
+        return remote(slot, slot, o.ga.at[way, k], o.gb2.at[k], (p, d + (1, -1)[way], t))
+
+    def ag_also_hop(h):
+        if h >= nz or nz == 1:
+            return
+
+        def act(k, right, left, here):
+            def go():
+                slot = W[C].at[1 - y, chunk(k)]
+                if h == 0:
+                    remote(slot, slot, o.gs.at[C, k], o.gy.at[C, k], beside).wait_recv()
+                else:
+                    remote(slot, slot, o.ga.at[0, k], o.gb2.at[k], beside).wait_recv()
+                when(right, lambda: ag_also(k, 0).start())
+                when(left, lambda: ag_also(k, 1).start())
+
+            when(here, go)
+
+        ag_each(C, h, act)
+
+    def ag_also_sent():
+        for h in range(nz):
+
+            def act(k, right, left, here):
+                def go():
+                    when(right, lambda: ag_also(k, 0).wait_send())
+                    when(left, lambda: ag_also(k, 1).wait_send())
+
+                when(here, go)
+
+            ag_each(C, h, act)
+
+    def ag_hop(g, h, aside=True):
         if h >= nz:
             return
 
@@ -127,13 +200,29 @@
                 if nz > 1:
                     when(right, lambda: ag_right(g, k).start())
                     when(left, lambda: ag_left(g, k).start())
-                ag_beside(g, k).start()
+                if aside:
+                    ag_aside(g, k, h == 0, False)
 
             when(here, go)
 
         ag_each(g, h, act)
 
+    def ag_side(g, h):
+        if h >= nz:
+            return
+
+        def act(k, right, left, here):
+            when(here, lambda: ag_aside(g, k, h == 0, False))
+
+        ag_each(g, h, act)
+
     def ag_wait(g):
+        if g == C and nz > 1:
+            pl.when(enc)(lambda: ag_wait_all(g))
+        else:
+            ag_wait_all(g)
+
+    def ag_wait_all(g):
         for k in range(nz):
             slot = W[g].at[1 - y, chunk(k)]
             remote(slot, slot, o.gs.at[g, k], o.gy.at[g, k], beside).wait_recv()
@@ -146,111 +235,134 @@
                     if nz > 1:
                         when(right, lambda: ag_right(g, k).wait_send())
                         when(left, lambda: ag_left(g, k).wait_send())
-                    ag_beside(g, k).wait_send()
+                    ag_aside(g, k, h == 0, True)
 
                 when(here, go)
 
             ag_each(g, h, act)
 
     def own_copy(g):
-        return pltpu.make_async_copy(shard[g], W[g].at[y, chunk(d)], o.oc_sem.at[g])
+        return pltpu.make_async_copy(shard[g], W[g].at[y, chunk(z)], o.oc_sem.at[g])
 
     def cross_part(k, part):
         start = k * chunk_rows + part * cross_rows
         return pl.ds(pl.multiple_of(start, 16), cross_rows)
 
-    cross_own = pltpu.make_async_copy(o.sx, W[X].at[y, cross_part(d, 1)], o.oc_sem.at[X])
+    cross_own = pltpu.make_async_copy(o.sx, W[X].at[y, cross_part(z, 1)], o.oc_sem.at[X])
     cross_in = remote(
-        o.sx, W[X].at[y, cross_part(d, 0)], o.xw.at[0], o.xw.at[1], across
+        o.sx, W[X].at[y, cross_part(z, 0)], o.xw.at[0], o.xw.at[1], across
     )
     cross_out = remote(o.xo, o.xi, o.xw.at[2], o.xw.at[3], across)
 
 
-    def rs_y(g, k):
+    def rs_y(r, k):
+        g, at, width = REDUCE[r]
+        cols = pl.ds(at, width)
         return remote(
-            W[g].at[1 - y, chunk(k)], RY[g].at[chunk(k)], o.rs_s.at[g, k], o.rs_r.at[g, k], beside
+            W[g].at[1 - y, chunk(k), cols],
+            RY[g].at[chunk(k), cols],
+            o.rs_s.at[r, k],
+            o.rs_r.at[r, k],
+            beside,
         )
 
-    def rs_z(g, k):
-        away = lax.rem(d + nz - 1 - k, nz)
+    def rs_z(r, k):
+        g, at, width = REDUCE[r]
+        cols = pl.ds(at, width)
+        away = lax.rem(z + nz - 1 - k, nz)
         return remote(
-            RY[g].at[chunk(k)], RZ[g].at[away], o.rz_s.at[g, k], o.rz_r.at[g, away], (p, k, t)
+            RY[g].at[chunk(k), cols],
+            RZ[g].at[away, :, cols],
+            o.rz_s.at[r, k],
+            o.rz_r.at[r, away],
+            (p, k, t),
         )
 
-    def rs_z_came(g, i):
+    def rs_z_came(r, i):
+        g, at, width = REDUCE[r]
+        cols = pl.ds(at, width)
         remote(
-            RY[g].at[chunk(d)], RZ[g].at[i], o.rz_s.at[g, d], o.rz_r.at[g, i], beside
+            RY[g].at[chunk(z), cols],
+            RZ[g].at[i, :, cols],
+            o.rz_s.at[r, z],
+            o.rz_r.at[r, i],
+            beside,
         ).wait_recv()
 
-    def rs_start(g):
+    def rs_start(r):
         for i in range(nz):
-            rs_y(g, lax.rem(d + 1 + i, nz)).start()
-
-    def rs_mid(g):
+            rs_y(r, lax.rem(z + 1 + i, nz)).start()
+
+    def rs_mid(r, first=0, last=nz):
+        g, at, width = REDUCE[r]
+        cols = slice(at, at + width)
+
+        @pl.loop(min(first, nz), min(last, nz))
+        def _(i):
+            k = lax.rem(z + 1 + i, nz)
+            rs_y(r, k).wait_recv()
+            start = pl.multiple_of(k * chunk_rows, 16)
+
+            @pl.loop(0, chunk_rows // 32)
+            def _(n):
+                rows = pl.ds(pl.multiple_of(start + n * 32, 16), 32)
+                both = W[g][y, rows, cols].astype(F32) + RY[g][rows, cols].astype(F32)
+                RY[g][rows, cols] = both.astype(BF)
+
+            if nz > 1:
+                pl.when(i < nz - 1)(lambda: rs_z(r, k).start())
+
+    def rs_end(r, put):
+        g, at, width = REDUCE[r]
+        cols = slice(at, at + width)
+        for i in range(nz - 1):
+            rs_z_came(r, i)
+        start = pl.multiple_of(z * chunk_rows, 16)
+
+        @pl.loop(0, chunk_rows // 32)
+        def _(n):
+            rows = pl.ds(pl.multiple_of(n * 32, 16), 32)
+            total = RY[g][pl.ds(pl.multiple_of(start + n * 32, 16), 32), cols].astype(F32)
+            for i in range(nz - 1):
+                total = total + RZ[g][i, rows, cols].astype(F32)
+            put(rows, total)
+
+    def rs_sent(r):
         for i in range(nz):
-            k = lax.rem(d + 1 + i, nz)
-            rs_y(g, k).wait_recv()
-            start = pl.multiple_of(k * chunk_rows, 16)
+            k = lax.rem(z + 1 + i, nz)
+            rs_y(r, k).wait_send()
+            if i < nz - 1:
+                rs_z(r, k).wait_send()
+
+    def rs_leave(r):
+        g, at, width = REDUCE[r]
+        out, buffer, first, into = LEAVE[r]
+        return pltpu.make_async_copy(
+            buffer.at[pl.ds(first, chunk_rows), pl.ds(into, width)],
+            out.at[:, pl.ds(at, width)],
+            o.lc.at[r],
+        )
+
+    def rs_out(r):
+        g, at, width = REDUCE[r]
+        out, buffer, first, into = LEAVE[r]
+        if nz == 1:
 
             @pl.loop(0, chunk_rows // 32)
-            def _(r):
-                rows = pl.ds(pl.multiple_of(start + r * 32, 16), 32)
-                both = W[g][y, rows, :].astype(F32) + RY[g][rows, :].astype(F32)
-                RY[g][rows, :] = both.astype(BF)
-
-            if i < nz - 1:
-                rs_z(g, k).start()
-
-    def rs_end(g, put):
-        for i in range(nz - 1):
-            rs_z_came(g, i)
-        start = pl.multiple_of(d * chunk_rows, 16)
-
-        @pl.loop(0, chunk_rows // 32)
-        def _(r):
-            rows = pl.ds(pl.multiple_of(r * 32, 16), 32)
-            total = RY[g][pl.ds(pl.multiple_of(start + r * 32, 16), 32), :].astype(F32)
-            for i in range(nz - 1):
-                total = total + RZ[g][i, rows, :].astype(F32)
-            put(rows, total)
-
-    def rs_sent(g):
-        for i in range(nz):
-            k = lax.rem(d + 1 + i, nz)
-            rs_y(g, k).wait_send()
-            if i < nz - 1:
-                rs_z(g, k).wait_send()
-
-    def rs_copies(g):
-        return [
-            pltpu.make_async_copy(
-                buffer.at[pl.ds(first, chunk_rows), pl.ds(0, width)],
-                out.at[:, pl.ds(at, width)],
-                o.lc.at[g + 3 * i],
-            )
-            for i, (out, buffer, first, at, width) in enumerate(place[g])
-        ]
-
-    def rs_out(g):
-        if nz == 1:
-            start = 0
-
-            @pl.loop(0, chunk_rows // 32)
-            def _(r):
-                rows = pl.ds(pl.multiple_of(r * 32, 16), 32)
-                (o.oa, o.ob, o.oc)[g][rows, :] = RY[g][rows, :]
+            def _(n):
+                rows = pl.ds(pl.multiple_of(n * 32, 16), 32)
+                out[rows, at : at + width] = RY[g][rows, at : at + width]
 
         else:
 
             def put(rows, total):
-                for out, buffer, first, at, width in place[g]:
-                    into = pl.ds(pl.multiple_of(rows.start + first, 16), 32)
-                    buffer[into, :width] = total[:, at : at + width]
-
-            rs_end(g, put)
-            for copy in rs_copies(g):
-                copy.start()
-        rs_sent(g)
+                buffer[pl.ds(pl.multiple_of(rows.start + first, 16), 32), into : into + width] = (
+                    total
+                )
+
+            rs_end(r, put)
+            rs_leave(r).start()
+        rs_sent(r)
 
 
     def rows_sib(i, k, n):
@@ -285,11 +397,18 @@
 
     def rows_join(i, out_ref):
         landing = ROWS[i][1]
-        for k in range(0, 4, 2):
-            value = jnp.concatenate(
-                [landing[k, :held].astype(F32), landing[k + 1, :held].astype(F32)], axis=0
-            )
-            out_ref[k * held : (k + 2) * held, :] = value.astype(out_ref.dtype)
+        wide = 256
+
+        @pl.loop(0, 2)
+        def _(k):
+            @pl.loop(0, D // wide)
+            def _(n):
+                cols = pl.ds(pl.multiple_of(n * wide, 128), wide)
+                value = jnp.concatenate(
+                    [landing[2 * k + j, :held, cols].astype(F32) for j in range(2)], axis=0
+                )
+                rows = pl.ds(pl.multiple_of(2 * k * held, 16), 2 * held)
+                out_ref[rows, cols] = value.astype(out_ref.dtype)
 
 
     def home_copy(i):
@@ -317,20 +436,21 @@
     for g in (A, B, C):
         own_copy(g).start()
     when(dec, cross_own.start)
-    for peer in (sibling, across, beside):
+    for peer in (sibling, across, beside, skew):
         pl.semaphore_signal(barrier, inc=1, device_id=peer, device_id_type=MESH)
     for i in range(1, nz):
         pl.semaphore_signal(
             barrier, inc=1, device_id=(p, lax.rem(d + i, nz), t), device_id_type=MESH
         )
-    pl.semaphore_wait(barrier, 3 + nz - 1)
+    pl.semaphore_wait(barrier, 4 + nz - 1)
     rows_start(0)
     when(enc, lambda: rows_start(2))
     own_copy(A).wait()
     ag_hop(A, 0)
     when(enc, cross_in.start)
     own_copy(B).wait()
-    ag_hop(B, 0)
+    ag_hop(B, 0, False)
+    when(enc, lambda: ag_side(B, 0))
     own_copy(C).wait()
 
     lane = lax.broadcasted_iota(jnp.int32, (1, 128), 1)
@@ -342,49 +462,69 @@
         def _(i):
             fn(pl.ds(pl.multiple_of(i * step, step), step))
 
+    def half_rows(h):
+        return pl.ds(pl.multiple_of(h * half, 16), half)
+
+    def half_loop(h, fn):
+        @pl.loop(0, half // RT)
+        def _(i):
+            fn(pl.ds(pl.multiple_of(h * half + i * RT, 16), RT))
+
+    def halves(fn, ready=None, after=None):
+        @pl.loop(0, 2)
+        def _(i):
+            h = lax.rem(core + i, 2)
+            if ready is not None:
+                ready(i, h)
+            half_loop(h, fn)
+            if after is not None:
+                pl.when(i == 0)(after)
+
+    def normed(v, gain_no):
+        r = lax.rsqrt(jnp.mean(v * v, axis=-1, keepdims=True) + EPSILON)
+        return (v * r * o.g[gain_no : gain_no + 1, :]).astype(BF)
+
     def norm_rows(x_ref, gain_no, out_ref):
         def one(rows):
-            v = x_ref[rows, :].astype(F32)
-            r = lax.rsqrt(jnp.mean(v * v, axis=-1, keepdims=True) + EPSILON)
-            out_ref[rows, :] = (v * r * o.g[gain_no : gain_no + 1, :]).astype(BF)
+            out_ref[rows, :] = normed(x_ref[rows, :].astype(F32), gain_no)
 
         rows_loop(one)
 
-    def exchange(slot, chunk_fn):
-        copies = []
-        for n in range(n_cw):
-            o.exs[slot, n] = chunk_fn(n).astype(BF)
-            copy = remote(
-                o.exs.at[slot, n], o.exr.at[slot, n], o.ss.at[slot, n], o.rs.at[slot, n], sibling
-            )
-            copy.start()
-            copies.append(copy)
-        return copies
-
-    def landed(copies):
-        for copy in copies:
-            copy.wait()
+    def ex_copy(slot, h):
+        rows = half_rows(h)
+        return remote(
+            o.exs.at[slot, rows], o.exr.at[slot, rows], o.ss.at[slot, h], o.rs.at[slot, h], sibling
+        )
+
+    def exchange(slot, fn):
+        @pl.loop(0, 2)
+        def _(i):
+            h = lax.rem(1 - core + i, 2)
+            rows = half_rows(h)
+            o.exs[slot, rows, :] = fn(rows).astype(BF)
+            ex_copy(slot, h).start()
+
+    def arrived(slot):
+        return lambda i, h: ex_copy(slot, h).wait()
 
     def ex_rows(slot, rows):
-        parts = [
-            o.exs[slot, n, rows, :].astype(F32) + o.exr[slot, n, rows, :].astype(F32)
-            for n in range(n_cw)
-        ]
-        return jnp.concatenate(parts, axis=1)
-
-    def residual(slot, base_ref, put):
+        return o.exs[slot, rows, :].astype(F32) + o.exr[slot, rows, :].astype(F32)
+
+    def residual(slot, base_ref, put, after=None):
         def one(rows):
             put(rows, base_ref[rows, :].astype(F32) + ex_rows(slot, rows))
 
-        rows_loop(one)
-
-    def keep(ref):
+        halves(one, arrived(slot), after)
+
+    def keep(ref, gain_no=None, normed_ref=None):
         def put(rows, value):
             ref[rows, :] = value
+            if gain_no is not None:
+                normed_ref[rows, :] = normed(value, gain_no)
 
         return put
 
-    def norm_back(slot, x_ref, gain_no, put):
+    def norm_back(slot, x_ref, gain_no, put, after=None):
         o.dgacc[gain_no] = jnp.zeros((8, D), F32)
 
         def one(rows):
@@ -397,16 +537,31 @@
             put(rows, r * (dhg - n * mu))
             o.dgacc[gain_no] += jnp.sum((dh * n).reshape(RT // 8, 8, D), axis=0)
 
-        rows_loop(one)
+        halves(one, arrived(slot), after)
 
     def split(a):
         return slice(a * hs, (a + 1) * hs)
 
+    def both_shards(fn):
+        @pl.loop(0, 2)
+        def _(a):
+            fn(a)
+
+    def side_first(fn, r):
+        @pl.loop(0, 2)
+        def _(i):
+            fn(lax.rem(1 - y + i, 2))
+            if r is not None:
+                pl.when(i == 0)(lambda: rs_start(r))
+
     def kv_project():
+        def one(a):
+            o.dkv[a] = dot(o.ns[...], W[A][a, :, at_kv:at_ext]).astype(BF)
+
+        both_shards(one)
         for a in range(2):
-            r = dot(o.ns[...], W[A][a, :, at_kv:at_ext]).astype(BF)
-            o.ks[:, split(a)] = r[:, :hs]
-            o.vs[:, split(a)] = r[:, hs:]
+            o.ks[:, split(a)] = o.dkv[a, :, :hs]
+            o.vs[:, split(a)] = o.dkv[a, :, hs:]
 
     def pair_stack(block):
         return jnp.concatenate([block * lo, block * hi], axis=0)
@@ -458,7 +613,7 @@
                     mixed = mixed + dot(probs[-1], o.vp[wrows, cols])
                 mix_ref[rows, cols] = pair_pick(mixed).astype(BF)
 
-    def attn_back(q_ref, mix_ref, mem, own):
+    def attn_back(q_ref, mix_ref, mem, own, hooks=()):
         if mem:
             o.dks[...] = jnp.zeros(o.dks.shape, F32)
             o.dvs[...] = jnp.zeros(o.dvs.shape, F32)
@@ -469,6 +624,8 @@
 
         @pl.loop(0, n_blk)
         def _(b):
+            for i, hook in enumerate(hooks):
+                pl.when(b == i)(hook)
             rows = pl.ds(pl.multiple_of(b * qb_rows, 16), qb_rows)
             wrows = pl.ds(pl.multiple_of(b * qb_rows, 16), win_w)
 
@@ -500,12 +657,10 @@
                 o.dq[rows, cols] = (pair_pick(dq2) * (HD**-0.5)).astype(BF)
 
     def out_project(slot, mix_ref, weight_ref, at):
-        mixed = [mix_ref[:, split(a)] for a in range(2)]
-        return exchange(
+        exchange(
             slot,
-            lambda n: sum(
-                dot_nt(mixed[a], weight_ref[a, n * CW : (n + 1) * CW, at : at + hs])
-                for a in range(2)
+            lambda rows: sum(
+                dot_nt(mix_ref[rows, split(a)], weight_ref[a, :, at : at + hs]) for a in range(2)
             ),
         )
 
@@ -519,8 +674,10 @@
         a = n // 2
         return a, pl.ds(pl.multiple_of((n - 2 * a) * fw, 128), fw)
 
-    def ff_fwd(x_ref):
-        norm_rows(x_ref, 1, o.nc)
+    def shard_cols(a):
+        return slice(a * fs, (a + 1) * fs)
+
+    def ff_fwd():
         ag_wait(B)
 
         @pl.loop(0, 4)
@@ -541,104 +698,127 @@
             rows_loop(one, 32)
 
         ag_wait(C)
-        return exchange(
+        when(dec, lambda: ag_also_hop(3))
+        exchange(
             2,
-            lambda n: sum(
-                dot_nt(o.hidden[:, a * fs : (a + 1) * fs], W[C][a, n * CW : (n + 1) * CW, :])
-                for a in range(2)
-            ),
+            lambda rows: sum(dot_nt(o.hidden[rows, shard_cols(a)], W[C][a]) for a in range(2)),
         )
-
-    def sides():
-        return (1 - y, y)
 
     def side_cols(a, width):
         return pl.ds(pl.multiple_of(a * width, 128), width)
 
-    def ff_back(x_ref):
+    def ff_pre(n):
+        a, half_cols = ff_half(n)
+        cols = pl.ds(pl.multiple_of(n * fw, 128), fw)
+        o.gp[:, cols] = (
+            dot(o.gb[...], W[C][a, :, half_cols]) * o.gp[:, cols].astype(F32)
+        ).astype(BF)
+
+    def ff_out_weights():
+        def one(a):
+            W[C][a] = dot_tn(o.gb[...], o.hidden[:, side_cols(a, fs)]).astype(BF)
+
+        side_first(one, RC)
+
+    def ff_in_weights():
+        def one(a):
+            W[B][a] = dot_tn(o.nc[...], o.gp[:, side_cols(a, fs)]).astype(BF)
+
+        side_first(one, RB)
+
+    def ff_back():
         ag_finish(B)
         ag_finish(C)
+        if nz > 1:
+            when(dec, ag_also_sent)
 
         @pl.loop(0, 4)
         def _(n):
-            a, half_cols = ff_half(n)
-            cols = pl.ds(pl.multiple_of(n * fw, 128), fw)
-            o.gp[:, cols] = (
-                dot(o.gb[...], W[C][a, :, half_cols]) * o.gp[:, cols].astype(F32)
-            ).astype(BF)
-
-        copies = exchange(
-            0,
-            lambda n: sum(
-                dot_nt(o.gp[:, a * fs : (a + 1) * fs], W[B][a, n * CW : (n + 1) * CW, :])
-                for a in range(2)
-            ),
+            ff_pre(n)
+
+        exchange(
+            0, lambda rows: sum(dot_nt(o.gp[rows, shard_cols(a)], W[B][a]) for a in range(2))
         )
-        for i, a in enumerate(sides()):
-            W[C][a] = dot_tn(o.gb[...], o.hidden[:, side_cols(a, fs)]).astype(BF)
-            if i == 0:
-                rs_start(C)
-        landed(copies)
+        ff_out_weights()
 
         def put(rows, dv):
             new = o.gres[rows, :] + dv
             o.gres[rows, :] = new
             o.gb[rows, :] = new.astype(BF)
 
-        norm_back(0, x_ref, 1, put)
-
-    def ff_weights():
-        for i, a in enumerate(sides()):
-            W[B][a] = dot_tn(o.nc[...], o.gp[:, side_cols(a, fs)]).astype(BF)
-            if i == 0:
-                rs_start(B)
-
-    def x_part():
-        return pl.ds(pl.multiple_of(core * half, 16), half)
+        norm_back(0, o.xlate, 1, put)
 
     def x_copy(way):
-        rows = x_part()
+        rows = half_rows(core)
         return remote(
             o.xsend.at[rows], o.xbuf.at[rows], o.xss.at[way, 0], o.xrs.at[way, 0], across
         )
 
-    def x_recv(way):
-        x_copy(way).wait_recv()
-        rows = x_part()
-        copy = remote(
+    def x_pass(way, h):
+        rows = half_rows(h)
+        return remote(
             o.xbuf.at[rows], o.xbuf.at[rows], o.xss.at[way, 1], o.xrs.at[way, 1], sibling
         )
-        copy.start()
-        copy.wait()
+
+    def x_halves(way, fn):
+        x_copy(way).wait_recv()
+        x_pass(way, core).start()
+
+        def ready(i, h):
+            pl.when(i == 1)(lambda: x_pass(way, h).wait_recv())
+
+        halves(fn, ready)
+        x_pass(way, core).wait_send()
+
+    def kv_weights():
+        def one(a):
+            W[A][a, :, at_kv:at_ext] = dot_tn(o.ns[...], o.dkv[a]).astype(BF)
+
+        side_first(one, RK)
 
     def dkv_grads():
         for a in range(2):
             o.dkv[a, :, :hs] = o.dks[:, split(a)].astype(BF)
             o.dkv[a, :, hs:] = o.dvs[:, split(a)].astype(BF)
-        return exchange(
+        exchange(
             2,
-            lambda n: sum(
-                dot_nt(o.dkv[a], W[A][a, n * CW : (n + 1) * CW, at_kv:at_ext]) for a in range(2)
+            lambda rows: sum(
+                dot_nt(o.dkv[a, rows, :], W[A][a, :, at_kv:at_ext]) for a in range(2)
             ),
         )
 
     rows_pass(0)
     when(enc, lambda: rows_pass(2))
-    ag_hop(A, 1)
-    rows_start(1)
-    ag_hop(A, 2)
-    ag_hop(C, 0)
-    rows_pass(1)
-    ag_hop(A, 3)
-    rows_done(0)
-    rows_join(0, o.x)
-
-    @pl.when(dec)
-    def _():
+
+    def first_cross():
         cross_own.wait()
         cross_in.wait_recv()
         ag_hop(X, 0)
 
+    when(dec, first_cross)
+    ag_hop(A, 1)
+    ag_hop(C, 0, False)
+    if STAGE:
+        when(dec, lambda: ag_pass_on(A))
+    ag_side(C, 0)
+    ag_hop(A, 2)
+    ag_hop(B, 1, False)
+    if STAGE:
+        when(dec, lambda: ag_pass_on(B))
+    when(dec, lambda: ag_hop(X, 1))
+    ag_hop(C, 1, False)
+    if STAGE:
+        when(dec, lambda: ag_pass_on(C))
+    ag_hop(A, 3)
+    when(dec, lambda: ag_hop(X, 2))
+    rows_done(0)
+    rows_join(0, o.x)
+    when(dec, lambda: ag_hop(X, 3))
+
+    when(dec, lambda: ag_side(B, 0))
+    ag_side(B, 1)
+    ag_side(C, 1)
+    when(dec, lambda: rows_start(1))
     ag_wait(A)
     o.g[...] = W[A][0, :, at_ext:].astype(F32).T[:8]
     rel_lanes = [dot_tn(W[A][a, :, at_ext:], o.hot[...]) for a in range(2)]
@@ -654,16 +834,20 @@
         ref[:HALO, :] = pad
         ref[HALO + L :, :] = pad
     norm_rows(o.x, 0, o.na)
+
+    def project_own(a):
+        o.dqkv[a] = dot(o.na[...], W[A][a, :, :at_o]).astype(BF)
+
+    both_shards(project_own)
     for a in range(2):
-        r = dot(o.na[...], W[A][a, :, :at_o]).astype(BF)
-        o.q[:, split(a)] = (r[:, :hs] * (HD**-0.5)).astype(BF)
-        o.kp[HALO : HALO + L, split(a)] = r[:, hs : 2 * hs]
-        o.vp[HALO : HALO + L, split(a)] = r[:, 2 * hs :]
-    ag_hop(B, 1)
+        o.q[:, split(a)] = (o.dqkv[a, :, :hs] * (HD**-0.5)).astype(BF)
+        o.kp[HALO : HALO + L, split(a)] = o.dqkv[a, :, hs : 2 * hs]
+        o.vp[HALO : HALO + L, split(a)] = o.dqkv[a, :, 2 * hs :]
+    ag_hop(B, 2)
     hooks = (
-        lambda: ag_hop(C, 1),
-        lambda: ag_hop(B, 2),
         lambda: ag_hop(C, 2),
+        lambda: ag_hop(B, 3),
+        lambda: ag_hop(C, 3),
     )
 
     @pl.when(enc)
@@ -677,99 +861,101 @@
     @pl.when(dec)
     def _():
         attn_fwd(o.q, o.mixa, False, True, True, hooks)
-        ag_hop(X, 1)
-
-    ag_hop(B, 3)
-    copies = out_project(0, o.mixa, W[A], at_o)
-    ag_hop(C, 3)
-    landed(copies)
-    residual(0, o.x, keep(o.xmid))
+        ag_also_hop(0)
+
+    out_project(0, o.mixa, W[A], at_o)
 
     @pl.when(enc)
     def _():
-        landed(ff_fwd(o.xmid))
-
-        def put_out(rows, value):
-            o.xlate[rows, :] = value
-            o.xsend[rows, :] = value.astype(BF)
-
-        residual(2, o.xmid, put_out)
-        x_copy(0).start()
-        home_send(0, o.xlate)
-        o.ho[...] = home_block(o.xlate, t)
-        home_out[0].start()
-        ag_finish(A)
-        rows_done(1)
-        rows_join(1, o.gres)
+        residual(0, o.x, keep(o.xlate, 1, o.nc))
+
+    @pl.when(dec)
+    def _():
+        ag_wait(X)
+        ag_finish(X)
+        if STAGE:
+            ag_relay(A).wait_send()
+            ag_relay(B).wait_send()
+            ag_relay(C).wait_send()
+
+        def whole(a):
+            for k in range(nz):
+                for part in range(2):
+                    at = part * (D // 2) + k * cross_rows
+                    start = k * chunk_rows + part * cross_rows
+                    o.xg[a, at : at + cross_rows, :] = W[X][a, start : start + cross_rows, :]
+
+        both_shards(whole)
+        o.g[3:4, :] = o.xg[0, :, 2 * hs :].astype(F32).T[:1]
+        residual(0, o.x, keep(o.xmid, 3, o.nb))
+        for a in range(2):
+            r = dot(o.nb[...], o.xg[a, :, :hs]).astype(BF)
+            o.qb[:, split(a)] = (r * (HD**-0.5)).astype(BF)
+
+        def one(rows):
+            o.ns[rows, :] = normed(o.xbuf[rows, :].astype(F32), 2)
+
+        x_halves(0, one)
+        kv_project()
+        attn_fwd(o.qb, o.mixb, True, False, False)
+        ag_also_hop(1)
+        out_project(1, o.mixb, o.xg, hs)
+        residual(1, o.xmid, keep(o.xlate, 1, o.nc))
+        ag_also_hop(2)
+
+
+    when(dec, lambda: rows_pass(1))
+    ff_fwd()
+
+    def put_out(rows, value):
+        o.gres[rows, :] = value
+        o.xsend[rows, :] = value.astype(BF)
+
+    residual(2, o.xlate, put_out, lambda: pl.when(enc)(lambda: x_copy(0).start()))
+    when(enc, lambda: rows_start(1))
+    home_send(0, o.gres)
+    o.ho[...] = home_block(o.gres, t)
+    home_out[0].start()
+    ag_finish(A)
+    when(enc, lambda: rows_pass(1))
+    rows_done(1)
+    rows_join(1, o.gres)
+
+    @pl.when(enc)
+    def _():
         x_copy(0).wait_send()
-        x_recv(1)
 
         def one(rows):
             value = o.gres[rows, :] + o.xbuf[rows, :].astype(F32)
             o.gres[rows, :] = value
             o.gb[rows, :] = value.astype(BF)
 
-        rows_loop(one)
-        ff_back(o.xmid)
-        ff_weights()
+        x_halves(1, one)
+
+    when(dec, lambda: rows_join(1, o.gb))
+
+
+    ff_back()
 
     @pl.when(dec)
     def _():
-        ag_hop(X, 2)
-        ag_hop(X, 3)
-        ag_wait(X)
-        ag_finish(X)
-        for a in range(2):
-            for k in range(nz):
-                for part in range(2):
-                    at = part * (D // 2) + k * cross_rows
-                    o.xg[a, at : at + cross_rows, :] = W[X][
-                        a, k * chunk_rows + part * cross_rows :, :
-                    ][:cross_rows]
-        o.g[3:4, :] = o.xg[0, :, 2 * hs :].astype(F32).T[:1]
-        norm_rows(o.xmid, 3, o.nb)
-        for a in range(2):
-            r = dot(o.nb[...], o.xg[a, :, :hs]).astype(BF)
-            o.qb[:, split(a)] = (r * (HD**-0.5)).astype(BF)
-        x_recv(0)
-        norm_rows(o.xbuf, 2, o.ns)
-        kv_project()
-        attn_fwd(o.qb, o.mixb, True, False, False)
-        landed(out_project(1, o.mixb, o.xg, hs))
-        residual(1, o.xmid, keep(o.xlate))
-        landed(ff_fwd(o.xlate))
-        residual(2, o.xlate, keep(o.gres))
-        home_send(0, o.gres)
-        o.ho[...] = home_block(o.gres, t)
-        home_out[0].start()
-        rows_done(1)
-        rows_join(1, o.gres)
-        rows_join(1, o.gb)
-        ff_back(o.xlate)
         mix_grads(o.xg, hs)
         attn_back(o.qb, o.mixb, True, False)
-        copies = dkv_grads()
-        parts = [o.dq[:, split(a)] for a in range(2)]
-        more = exchange(
-            1,
-            lambda n: sum(
-                dot_nt(parts[a], o.xg[a, n * CW : (n + 1) * CW, :hs]) for a in range(2)
-            ),
+        dkv_grads()
+        exchange(
+            1, lambda rows: sum(dot_nt(o.dq[rows, split(a)], o.xg[a, :, :hs]) for a in range(2))
         )
-        ff_weights()
-        landed(copies)
 
         def put_source(rows, dv):
             o.xsend[rows, :] = dv.astype(BF)
 
-        norm_back(2, o.xbuf, 2, put_source)
-        x_copy(1).start()
-        landed(more)
+        norm_back(2, o.xbuf, 2, put_source, lambda: x_copy(1).start())
+        rs_mid(RC, 0, 2)
 
         def put_mid(rows, dv):
             new = o.gres[rows, :] + dv
             o.gres[rows, :] = new
-            o.nc[rows, :] = new.astype(BF)
+            o.xbuf[rows, :] = new.astype(BF)
 
         norm_back(1, o.xmid, 3, put_mid)
         line = jnp.sum(o.dgacc[3], axis=0, keepdims=True)
@@ -777,7 +963,7 @@
         for a in range(2):
             full = jnp.concatenate(
                 [
-                    dot_tn(o.nb[...], parts[a]).astype(BF),
+                    dot_tn(o.nb[...], o.dq[:, split(a)]).astype(BF),
                     dot_tn(o.gb[...], o.mixb[:, split(a)]).astype(BF),
                     tall,
                 ],
@@ -788,42 +974,51 @@
                     at = part * (D // 2) + k * cross_rows
                     to = k * chunk_rows + part * cross_rows
                     W[X][a, to : to + cross_rows, :] = full[at : at + cross_rows]
-        rs_start(X)
-        ag_finish(A)
-        rs_mid(C)
+        rs_start(RX)
         x_copy(1).wait_send()
-        o.gb[...] = o.nc[...]
-
+        o.gb[...] = o.xbuf[...]
+
+    ff_in_weights()
     mix_grads(W[A], at_o)
     for a in range(2):
         W[A][a, :, at_o : at_o + hs] = dot_tn(o.gb[...], o.mixa[:, split(a)]).astype(BF)
+    steps = tuple(functools.partial(rs_mid, RC, i, i + 1) for i in range(3))
 
     @pl.when(enc)
     def _():
-        attn_back(o.q, o.mixa, True, True)
-        landed(dkv_grads())
-
-        def put_source(rows, dv):
-            pass
-
-        norm_back(2, o.nb, 2, put_source)
-        rs_mid(C)
+        attn_back(o.q, o.mixa, True, True, steps)
+        dkv_grads()
 
     @pl.when(dec)
     def _():
         attn_back(o.q, o.mixa, False, True)
-        rs_mid(B)
-
+        rs_mid(RC, 2, 3)
+
+    kv_weights()
+    rs_mid(RC, 3)
     for a in range(2):
         o.dqkv[a, :, :hs] = o.dq[:, split(a)]
         o.dqkv[a, :, hs : 2 * hs] = o.dkp[HALO : HALO + L, split(a)].astype(BF)
         o.dqkv[a, :, 2 * hs :] = o.dvp[HALO : HALO + L, split(a)].astype(BF)
-    copies = exchange(
-        0,
-        lambda n: sum(
-            dot_nt(o.dqkv[a], W[A][a, n * CW : (n + 1) * CW, :at_o]) for a in range(2)
-        ),
+    last_slot = 1 - p
+    exchange(
+        last_slot,
+        lambda rows: sum(dot_nt(o.dqkv[a, rows, :], W[A][a, :, :at_o]) for a in range(2)),
     )
+
+    def own_weights(a):
+        W[A][a, :, :at_o] = dot_tn(o.na[...], o.dqkv[a]).astype(BF)
+
+    side_first(own_weights, RQ)
+
+    @pl.when(enc)
+    def _():
+        def put_source(rows, dv):
+            pass
+
+        norm_back(2, o.nb, 2, put_source)
+        rs_mid(RB, 0, 2)
+
     heads = 2 * n_pair
     acc = jnp.zeros((heads * 8, win_w), F32)
     for k in range(qb_rows // 8):
@@ -835,17 +1030,13 @@
         turned = acc if k == 0 else pltpu.roll(acc, win_w - k, 1)
         diag = diag + jnp.where(sub == k, turned, 0.0)
     lines = jnp.sum(diag.reshape(heads, 8, win_w), axis=1)
-    landed(copies)
 
     def put_in(rows, dv):
         o.gres[rows, :] = o.gres[rows, :] + dv
 
-    norm_back(0, o.x, 0, put_in)
+    norm_back(last_slot, o.x, 0, put_in)
     home_send(1, o.gres)
     home_out[2].start()
-    for i, a in enumerate(sides()):
-        W[A][a, :, :at_o] = dot_tn(o.na[...], o.dqkv[a]).astype(BF)
-        W[A][a, :, at_kv:at_ext] = dot_tn(o.ns[...], o.dkv[a]).astype(BF)
     per = hs // HD
     for a in range(2):
         o.ext[...] = jnp.zeros(o.ext.shape, F32)
@@ -859,30 +1050,30 @@
         low = (whole - high.astype(F32)).astype(BF)
         tall = tall + dot_nt(o.hot[...], high) + dot_nt(o.hot[...], low)
         W[A][a, :, at_ext:] = tall.astype(BF)
-    rs_start(A)
+    rs_start(RG)
     home_copy(0).wait()
     home_out[1].start()
-
-    @pl.when(enc)
-    def _():
-        rs_mid(B)
-
-    rs_out(C)
+    when(enc, lambda: rs_mid(RB, 2))
+    when(dec, lambda: rs_mid(RB))
+    rs_mid(RK)
+    rs_out(RC)
 
     @pl.when(dec)
     def _():
-        rs_mid(X)
-
-    rs_mid(A)
-    rs_out(B)
+        rs_mid(RX)
+
+    rs_mid(RQ)
+    rs_out(RB)
+    rs_mid(RG)
+    rs_out(RK)
 
     @pl.when(dec)
     def _():
         def put(rows, total):
             o.xt[rows, :] = total
 
-        rs_end(X, put)
-        rs_sent(X)
+        rs_end(RX, put)
+        rs_sent(RX)
         o.xo[...] = o.xt[:cross_rows, :]
         cross_out.start()
         o.ox[...] = o.xt[cross_rows:, :].astype(o.ox.dtype)
@@ -897,19 +1088,19 @@
     home_copy(1).wait()
     o.ext[...] = o.hr[1].astype(F32)
     home_out[3].start()
-    rs_out(A)
+    rs_out(RQ)
+    rs_out(RG)
     for copy in home_out:
         copy.wait()
     if nz > 1:
-        for g in (A, B, C):
-            for copy in rs_copies(g):
-                copy.wait()
+        for r in LEAVE:
+            rs_leave(r).wait()
 
 
 def run_kernel(dims, given):
     L, D, hs, fs, nz, qb_rows, win_w = dims
     hc, fc = 2 * hs, 2 * fs
-    n_blk, n_pair, n_cw = L // qb_rows, hc // 128, D // CW
+    n_blk, n_pair = L // qb_rows, hc // 128
     LP = L + 2 * HALO
     LBP = -(-(L // 4) // 16) * 16
     CR = D // nz
@@ -938,7 +1129,7 @@
         dmix=V(LH, BF), dq=V(LH, BF), dqkv=V((2, L, 3 * hs), BF), dkv=V((2, L, 2 * hs), BF),
         dkp=V((LP, hc), F32), dvp=V((LP, hc), F32), dks=V(LH, F32), dvs=V(LH, F32),
         gb=V(LD, BF), xbuf=V(LD, BF), xsend=V(LD, BF),
-        exs=V((3, n_cw, L, CW), BF), exr=V((3, n_cw, L, CW), BF), dgacc=V((4, 8, D), F32),
+        exs=V((3, L, D), BF), exr=V((3, L, D), BF), dgacc=V((4, 8, D), F32),
         g=V((8, D), F32), ext=V((LBP, D), F32), lines=V((EXT, win_w), F32),
         x=V(LD, BF), xq=V((4, LBP, D), BF), cq=V((4, LBP, D), BF), mq=V((4, LBP, D), BF),
         hs=V((2, LBP, D), BF), hr=V((2, LBP, D), BF), ho=V((LBP, D), BF),
@@ -950,11 +1141,13 @@
         scratch["y" + g] = V((D, width), BF)
         scratch["z" + g] = V((nz - 1, CR, width) if nz > 1 else (1, 16, width), BF)
     sem = pltpu.SemaphoreType.DMA
-    scratch.update(ss=sem((3, n_cw)), rs=sem((3, n_cw)), xss=sem((2, 2)), xrs=sem((2, 2)))
-    scratch.update(xw=sem((4,)), oc_sem=sem((4,)), lc=sem((5,)), lh=sem((4,)))
+    scratch.update(ss=sem((3, 2)), rs=sem((3, 2)), gd=sem((3, 3)), ga=sem((2, nz)), gb2=sem((nz,)), xss=sem((2, 2)), xrs=sem((2, 2)))
+    scratch.update(xw=sem((4,)), oc_sem=sem((4,)), lc=sem((6,)), lh=sem((4,)))
     scratch.update(qs=sem((3, 3)), qr=sem((3, 3)), ql=sem((3,)), hx=sem((2,)), hy=sem((2,)))
-    for name in ("gr", "gl", "gs", "gz", "gy", "rs_s", "rs_r", "rz_s", "rz_r"):
+    for name in ("gr", "gl", "gs", "gz", "gy"):
         scratch[name] = sem((4, nz))
+    for name in ("rs_s", "rs_r", "rz_s", "rz_r"):
+        scratch[name] = sem((6, nz))
     spec = pl.BlockSpec(memory_space=pltpu.VMEM)
     far = pl.BlockSpec(memory_space=pl.ANY)
     names = list(given) + list(outs) + list(scratch)

time: 338 us -> 300 us (0.89)
  Pallas kernels: 325 us -> 287 us
    pallas_call x1, Pallas kernels: 317 us -> 279 us  [run_kernel(): pl.pallas_call(functools.partial(kernel, dims, names), out_shape=list(out...]
where the time goes in v3:
time: 300 us; the launch traced here: 297 us
  Pallas kernels  287 us (96%)
  local copies, waits for them, and re-layouts  8.4 us (3%)
    pallas_call x1, Pallas kernels, run_kernel(): pl.pallas_call(functools.partial(kernel, dims, names), out_shape=list(out...  279 us

profile of v3, /device:TPU:9, one launch (start us, length us, event | category | flops | bytes accessed | tf_op | source)
XLA Modules:
  0.0 297.4 jit_solution(5353953195410598188)
XLA Ops:
  0.6 0.8 slice.3
  1.4 0.6 pad.8
  2.0 0.7 fusion
  2.7 1.3 copy.28.refs_6_
  4.0 5.7 %gather_fusion = bf16[256,768]{1,0:T(8,128)(2,1)} fusion(bf16[4096,768]{1,0:T(8,128)(2,1)} %param.19, s32[1024]{0:T(1024)S(1)} %pad_clamp_fusion), kind=kCustom, calls=%fused_computation | custom fusion | bytes 787456 | tf_op jit(solution)/shard_map/gather | solution.py:1352
  9.7 3.9 %prep.1 = (bf16[2,128,768]{2,1,0:T(8,128)(2,1)}, bf16[2,128,768]{2,1,0:T(8,128)(2,1)}, bf16[192,1280]{1,0:T(8,128)(2,1)}, bf16[96,512]{1,0:T(8,128)(2,1)}, s32[4...) custom-call(bf16[120,2,768]{2,1,0:T(2,128)(2,1)} %bitcast.34, ...), custom_call_target="tpu_custom_call" | custom-call | tf_op jit(solution)/shard_map/prep/pallas_call | solution.py:1249
  13.7 279.1 %layers.1 = (bf16[2,128,768]{2,1,0:T(8,128)(2,1)}, f32[2,120,768]{2,1,0:T(8,128)}, f32[192,1280]{1,0:T(8,128)}, f32[192,768]{1,0:T(8,128)}, f32[192,768]{1,0:T(8,128)}, /*index=5*/f32[96,512]{1,0:T(8,128)}) custom-call(bf16[2,128,768]{2,1,0:T(8,128)(2,1)} %get-tuple-element.38.refs_0_, bf16[2,128,768]{2,1,0:T(8,128)(2,1)} %get-tuple-element.39.refs_1_, ...), custom_call_target="tpu_custom_call" | custom-call | tf_op jit(solution)/shard_map/layers/pallas_call | solution.py:1157
  292.8 4.4 %finish.1 = (bf16[120,2,768]{2,1,0:T(2,128)(2,1)}, f32[120,2,768]{2,1,0:T(2,128)}, f32[3,192,192]{2,1,0:T(8,128)}, f32[192,192]{1,0:T(8,128)}, f32[192,2,192]{2,...) custom-call(bf16[2,128,768]{2,1,0:T(8,128)(2,1)} %get-tuple-element., ...), custom_call_target="tpu_custom_call" | custom-call | tf_op jit(solution)/shard_map/finish/pallas_call | solution.py:1307
  (1 shorter events, 0.0 us)

commit v4 on v3

--- a/solution.py
+++ b/solution.py
@@ -11,8 +11,10 @@
 NB = 32
 MEM = 20
 HALO = 48
-EXT = 128
+TILE = 16
+CROSS_AT = 3
 REL_AT = 8
+PIECE = 256
 EPSILON = 1e-06
 NEG = -1000000000.0
 BF = jnp.bfloat16
@@ -66,24 +68,22 @@
     W = (o.wa, o.wb, o.wc, o.wx)
     RY = (o.ya, o.yb, o.yc, o.yx)
     RZ = (o.za, o.zb, o.zc, o.zx)
-    RB, RC, RX, RQ, RK, RG = range(6)
+    RB, RC, RX, RQ, RK = range(5)
     REDUCE = {
         RB: (B, 0, fs),
         RC: (C, 0, fs),
-        RX: (X, 0, 2 * hs + EXT),
+        RX: (X, 0, 2 * hs),
         RQ: (A, 0, at_kv),
         RK: (A, at_kv, 2 * hs),
-        RG: (A, at_ext, EXT),
     }
     LEAVE = {
         RB: (o.ob, o.xlate, 0, 0),
         RC: (o.oc, o.xmid, 0, 0),
         RQ: (o.oa, o.xmid, chunk_rows, 0),
         RK: (o.oa, o.xlate, chunk_rows, 0),
-        RG: (o.oa, o.xlate, chunk_rows, 2 * hs),
     }
     STAGE = {} if nz == 1 else {
-        A: o.hidden.at[pl.ds(0, chunk_rows), pl.ds(0, 6 * hs + EXT)],
+        A: o.hidden.at[pl.ds(0, chunk_rows), pl.ds(0, 6 * hs)],
         B: o.gp.at[pl.ds(0, chunk_rows), pl.ds(0, fs)],
         C: o.gp.at[pl.ds(0, chunk_rows), pl.ds(fs, fs)],
     }
@@ -253,6 +253,180 @@
         o.sx, W[X].at[y, cross_part(z, 0)], o.xw.at[0], o.xw.at[1], across
     )
     cross_out = remote(o.xo, o.xi, o.xw.at[2], o.xw.at[3], across)
+
+
+    nb_each = NB // nz
+    n_rel = hs // HD
+
+    def others(fn):
+        if nz > 1:
+
+            @pl.loop(1, nz)
+            def _(i):
+                fn(lax.rem(z + i, nz))
+
+    def tile_z(a, k, to, sems):
+        slot = o.m.at[a, k]
+        return remote(slot, slot, o.mt.at[sems, to], o.mt.at[sems + 1, k], (p, to, t))
+
+    def tile_beside(k):
+        slot = o.m.at[y, k]
+        return remote(slot, slot, o.mt.at[2, k], o.mt.at[3, k], beside)
+
+    def tile_across():
+        return remote(o.m.at[y, z], o.m.at[2, z], o.mx.at[0], o.mx.at[1], across)
+
+    def tiles_start():
+        o.m[y, z] = o.sm[...]
+
+        @pl.when(enc)
+        def _():
+            o.m[2] = jnp.zeros(o.m.shape[1:], BF)
+
+        others(lambda k: tile_z(y, z, k, 0).start())
+        tile_beside(z).start()
+        when(enc, lambda: tile_across().start())
+
+    def tiles_pass():
+        def one(k):
+            tile_z(y, k, k, 0).wait_recv()
+            tile_beside(k).start()
+
+        others(one)
+
+        @pl.when(dec)
+        def _():
+            tile_across().wait_recv()
+            others(lambda k: tile_z(2, z, k, 4).start())
+
+    def tiles_done():
+        @pl.loop(0, nz)
+        def _(k):
+            slot = o.m.at[1 - y, k]
+            remote(slot, slot, o.mt.at[2, k], o.mt.at[3, k], beside).wait_recv()
+            tile_beside(k).wait_send()
+
+        others(lambda k: tile_z(y, z, k, 0).wait_send())
+        when(enc, lambda: tile_across().wait_send())
+
+        @pl.when(dec)
+        def _():
+            others(lambda k: tile_z(2, k, k, 4).wait_recv())
+            others(lambda k: tile_z(2, z, k, 4).wait_send())
+
+        o.rl[...] = jnp.zeros(o.rl.shape, F32)
+        for k in range(nz):
+            block = o.m[y, k].astype(F32)
+            o.g[:CROSS_AT, k * chunk_rows : (k + 1) * chunk_rows] = block[:CROSS_AT, :chunk_rows]
+            for part in range(2):
+                cross = block if part else o.m[2, k].astype(F32)
+                at = part * (D // 2) + k * cross_rows
+                o.g[CROSS_AT : CROSS_AT + 1, at : at + cross_rows] = cross[
+                    CROSS_AT : CROSS_AT + 1, :cross_rows
+                ]
+            for a in range(2):
+                rel = o.m[a, k].astype(F32)
+                o.rl[a, :n_rel, k * nb_each : (k + 1) * nb_each] = rel[
+                    REL_AT : REL_AT + n_rel, :nb_each
+                ]
+
+    def sums_y():
+        return remote(o.ms1.at[1 - y], o.ms2, o.mx.at[2], o.mx.at[3], beside)
+
+    def sums_z(k):
+        away = lax.rem(z + nz - 1 - k, nz)
+        return remote(o.ms2.at[k], o.ms3.at[away], o.mt.at[6, k], o.mt.at[7, away], (p, k, t))
+
+    def sums_z_came(i):
+        remote(o.ms2.at[z], o.ms3.at[i], o.mt.at[6, z], o.mt.at[7, i], beside).wait_recv()
+
+    def sums_across():
+        return remote(o.mo1, o.mo2, o.mx.at[4], o.mx.at[5], across)
+
+    def sums_start(lines):
+        o.dgl[...] = jnp.zeros(o.dgl.shape, F32)
+        for i in range(4):
+            o.dgl[i : i + 1, :] = jnp.sum(o.dgacc[i], axis=0, keepdims=True)
+        for a in range(2):
+            o.lines[...] = jnp.zeros(o.lines.shape, F32)
+            o.lines[:n_rel, :] = lines[n_rel * a : n_rel * (a + 1), :]
+            whole = o.lines[...]
+            high = whole.astype(BF)
+            low = (whole - high.astype(F32)).astype(BF)
+            o.rl[a] = dot_nt(high, o.hot[...]) + dot_nt(low, o.hot[...])
+            for k in range(nz):
+                o.mf[...] = jnp.zeros(o.mf.shape, F32)
+                o.mf[:CROSS_AT, :chunk_rows] = o.dgl[
+                    :CROSS_AT, k * chunk_rows : (k + 1) * chunk_rows
+                ]
+                for part in range(2):
+                    at = part * (D // 2) + k * cross_rows
+                    row = CROSS_AT + part
+                    o.mf[row : row + 1, :cross_rows] = o.dgl[
+                        CROSS_AT : CROSS_AT + 1, at : at + cross_rows
+                    ]
+                o.mf[REL_AT : REL_AT + n_rel, :nb_each] = o.rl[
+                    a, :n_rel, k * nb_each : (k + 1) * nb_each
+                ]
+                o.ms1[a, k] = o.mf[...].astype(BF)
+        sums_y().start()
+
+    def sums_mid():
+        sums_y().wait()
+        for k in range(nz):
+            both = o.ms1[y, k].astype(F32) + o.ms2[k].astype(F32)
+            o.ms2[k] = both.astype(BF)
+        others(lambda k: sums_z(k).start())
+
+    def sums_end():
+        total = o.ms2[z].astype(F32)
+        for i in range(nz - 1):
+            sums_z_came(i)
+            total = total + o.ms3[i].astype(F32)
+        o.om[...] = total
+        others(lambda k: sums_z(k).wait_send())
+
+        @pl.when(dec)
+        def _():
+            o.mo1[...] = total
+            sums_across().start()
+            o.om[CROSS_AT : CROSS_AT + 1, :] = total[CROSS_AT + 1 : CROSS_AT + 2, :]
+            sums_across().wait_send()
+
+        @pl.when(enc)
+        def _():
+            sums_across().wait_recv()
+            o.om[CROSS_AT : CROSS_AT + 1, :] = o.mo2[CROSS_AT : CROSS_AT + 1, :]
+
+
+    def piece(c, slot):
+        return pltpu.make_async_copy(
+            o.table.at[pl.ds(pl.multiple_of(c * PIECE, PIECE), PIECE)],
+            o.exs.at[slot, pl.ds(0, PIECE)],
+            o.tg.at[slot],
+        )
+
+    def pick_rows():
+        n_piece = o.table.shape[0] // PIECE
+        piece(0, 0).start()
+        rows_done(2)
+        for k in range(4):
+            o.idr[:, k * held : (k + 1) * held] = o.mq[k, 0:1, :held]
+        o.gres[...] = jnp.zeros(o.gres.shape, F32)
+
+        @pl.loop(0, n_piece)
+        def _(c):
+            slot = lax.rem(c, 2)
+            pl.when(c + 1 < n_piece)(lambda: piece(c + 1, 1 - slot).start())
+            at = lax.broadcasted_iota(jnp.int32, (PIECE, L), 0) + c * PIECE
+            hit = jnp.where(at == o.idr[...], 1.0, 0.0).astype(BF)
+            piece(c, slot).wait()
+            o.gres[...] += dot_tn(hit, o.exs[slot, :PIECE, :])
+
+        def one(rows):
+            o.nb[rows, :] = o.gres[rows, :].astype(BF)
+
+        rows_loop(one)
 
 
     def rs_y(r, k):
@@ -443,6 +617,7 @@
             barrier, inc=1, device_id=(p, lax.rem(d + i, nz), t), device_id_type=MESH
         )
     pl.semaphore_wait(barrier, 4 + nz - 1)
+    tiles_start()
     rows_start(0)
     when(enc, lambda: rows_start(2))
     own_copy(A).wait()
@@ -787,6 +962,7 @@
             ),
         )
 
+    tiles_pass()
     rows_pass(0)
     when(enc, lambda: rows_pass(2))
 
@@ -801,6 +977,7 @@
     if STAGE:
         when(dec, lambda: ag_pass_on(A))
     ag_side(C, 0)
+    when(enc, pick_rows)
     ag_hop(A, 2)
     ag_hop(B, 1, False)
     if STAGE:
@@ -820,15 +997,17 @@
     ag_side(C, 1)
     when(dec, lambda: rows_start(1))
     ag_wait(A)
-    o.g[...] = W[A][0, :, at_ext:].astype(F32).T[:8]
-    rel_lanes = [dot_tn(W[A][a, :, at_ext:], o.hot[...]) for a in range(2)]
-    for h in range(2 * n_pair):
-        a = h // (hs // HD)
-        row = REL_AT + h - a * (hs // HD)
-        line = rel_lanes[a][row : row + 1, :]
-        o.tb[h] = pltpu.roll(
-            jnp.broadcast_to(line, (qb_rows, win_w)), 0, 1, stride=1, stride_axis=0
-        )
+    tiles_done()
+    for a in range(2):
+        rel_lines = dot(o.rl[a].astype(BF), o.hot[...])
+        for h in range(n_rel):
+            o.tb[a * n_rel + h] = pltpu.roll(
+                jnp.broadcast_to(rel_lines[h : h + 1, :], (qb_rows, win_w)),
+                0,
+                1,
+                stride=1,
+                stride_axis=0,
+            )
     pad = jnp.zeros((HALO, hc), BF)
     for ref in (o.kp, o.vp):
         ref[:HALO, :] = pad
@@ -852,8 +1031,6 @@
 
     @pl.when(enc)
     def _():
-        rows_done(2)
-        rows_join(2, o.nb)
         norm_rows(o.nb, 2, o.ns)
         kv_project()
         attn_fwd(o.q, o.mixa, True, True, False, hooks)
@@ -886,7 +1063,6 @@
                     o.xg[a, at : at + cross_rows, :] = W[X][a, start : start + cross_rows, :]
 
         both_shards(whole)
-        o.g[3:4, :] = o.xg[0, :, 2 * hs :].astype(F32).T[:1]
         residual(0, o.x, keep(o.xmid, 3, o.nb))
         for a in range(2):
             r = dot(o.nb[...], o.xg[a, :, :hs]).astype(BF)
@@ -923,6 +1099,7 @@
 
     @pl.when(enc)
     def _():
+        o.dgacc[3] = jnp.zeros((8, D), F32)
         x_copy(0).wait_send()
 
         def one(rows):
@@ -958,14 +1135,11 @@
             o.xbuf[rows, :] = new.astype(BF)
 
         norm_back(1, o.xmid, 3, put_mid)
-        line = jnp.sum(o.dgacc[3], axis=0, keepdims=True)
-        tall = jnp.broadcast_to(line, (EXT, D)).T.astype(BF)
         for a in range(2):
             full = jnp.concatenate(
                 [
                     dot_tn(o.nb[...], o.dq[:, split(a)]).astype(BF),
                     dot_tn(o.gb[...], o.mixb[:, split(a)]).astype(BF),
-                    tall,
                 ],
                 axis=1,
             )
@@ -1037,20 +1211,7 @@
     norm_back(last_slot, o.x, 0, put_in)
     home_send(1, o.gres)
     home_out[2].start()
-    per = hs // HD
-    for a in range(2):
-        o.ext[...] = jnp.zeros(o.ext.shape, F32)
-        for k in range(3):
-            o.ext[k : k + 1, :] = jnp.sum(o.dgacc[k], axis=0, keepdims=True)
-        tall = o.ext[...].T
-        o.lines[...] = jnp.zeros((EXT, win_w), F32)
-        o.lines[REL_AT : REL_AT + per, :] = lines[per * a : per * (a + 1), :]
-        whole = o.lines[...]
-        high = whole.astype(BF)
-        low = (whole - high.astype(F32)).astype(BF)
-        tall = tall + dot_nt(o.hot[...], high) + dot_nt(o.hot[...], low)
-        W[A][a, :, at_ext:] = tall.astype(BF)
-    rs_start(RG)
+    sums_start(lines)
     home_copy(0).wait()
     home_out[1].start()
     when(enc, lambda: rs_mid(RB, 2))
@@ -1064,8 +1225,8 @@
 
     rs_mid(RQ)
     rs_out(RB)
-    rs_mid(RG)
     rs_out(RK)
+    sums_mid()
 
     @pl.when(dec)
     def _():
@@ -1089,7 +1250,7 @@
     o.ext[...] = o.hr[1].astype(F32)
     home_out[3].start()
     rs_out(RQ)
-    rs_out(RG)
+    sums_end()
     for copy in home_out:
         copy.wait()
     if nz > 1:
@@ -1104,7 +1265,8 @@
     LP = L + 2 * HALO
     LBP = -(-(L // 4) // 16) * 16
     CR = D // nz
-    widths = dict(a=6 * hs + EXT, b=fs, c=fs, x=2 * hs + EXT)
+    widths = dict(a=6 * hs, b=fs, c=fs, x=2 * hs)
+    MW = -(-CR // 128) * 128
     S = jax.ShapeDtypeStruct
     SUM = F32 if nz > 1 else BF
     outs = dict(
@@ -1114,6 +1276,7 @@
         ob=S((CR, widths["b"]), SUM),
         oc=S((CR, widths["c"]), SUM),
         ox=S((CR // 2, widths["x"]), SUM),
+        om=S((TILE, MW), F32),
     )
     V = pltpu.VMEM
     LD, LH, LF = (L, D), (L, hc), (L, fc)
@@ -1130,8 +1293,12 @@
         dkp=V((LP, hc), F32), dvp=V((LP, hc), F32), dks=V(LH, F32), dvs=V(LH, F32),
         gb=V(LD, BF), xbuf=V(LD, BF), xsend=V(LD, BF),
         exs=V((3, L, D), BF), exr=V((3, L, D), BF), dgacc=V((4, 8, D), F32),
-        g=V((8, D), F32), ext=V((LBP, D), F32), lines=V((EXT, win_w), F32),
-        x=V(LD, BF), xq=V((4, LBP, D), BF), cq=V((4, LBP, D), BF), mq=V((4, LBP, D), BF),
+        g=V((8, D), F32), ext=V((LBP, D), F32), lines=V((TILE, win_w), F32),
+        m=V((3, nz, TILE, MW), BF), ms1=V((2, nz, TILE, MW), BF), ms2=V((nz, TILE, MW), BF),
+        ms3=V((max(nz - 1, 1), TILE, MW), BF), mf=V((TILE, MW), F32), mo1=V((TILE, MW), F32),
+        mo2=V((TILE, MW), F32), dgl=V((8, D), F32), rl=V((2, TILE, 128), F32),
+        idr=V((1, L), jnp.int32),
+        x=V(LD, BF), xq=V((4, LBP, D), BF), cq=V((4, LBP, D), BF), mq=V((4, 8, 128), jnp.int32),
         hs=V((2, LBP, D), BF), hr=V((2, LBP, D), BF), ho=V((LBP, D), BF),
         xg=V((2, D, widths["x"]), BF), xt=V((CR, widths["x"]), F32),
         xo=V((CR // 2, widths["x"]), F32), xi=V((CR // 2, widths["x"]), F32),
@@ -1141,7 +1308,7 @@
         scratch["y" + g] = V((D, width), BF)
         scratch["z" + g] = V((nz - 1, CR, width) if nz > 1 else (1, 16, width), BF)
     sem = pltpu.SemaphoreType.DMA
-    scratch.update(ss=sem((3, 2)), rs=sem((3, 2)), gd=sem((3, 3)), ga=sem((2, nz)), gb2=sem((nz,)), xss=sem((2, 2)), xrs=sem((2, 2)))
+    scratch.update(ss=sem((3, 2)), rs=sem((3, 2)), gd=sem((3, 3)), ga=sem((2, nz)), gb2=sem((nz,)), mt=sem((8, nz)), mx=sem((6,)), tg=sem((2,)), xss=sem((2, 2)), xrs=sem((2, 2)))
     scratch.update(xw=sem((4,)), oc_sem=sem((4,)), lc=sem((6,)), lh=sem((4,)))
     scratch.update(qs=sem((3, 3)), qr=sem((3, 3)), ql=sem((3,)), hx=sem((2,)), hy=sem((2,)))
     for name in ("gr", "gl", "gs", "gz", "gy"):
@@ -1151,7 +1318,7 @@
     spec = pl.BlockSpec(memory_space=pltpu.VMEM)
     far = pl.BlockSpec(memory_space=pl.ANY)
     names = list(given) + list(outs) + list(scratch)
-    FAR = ["sa", "sb", "sc", "sx", "xs", "cs", "ms", "oh", "gh"]
+    FAR = ["sa", "sb", "sc", "sx", "xs", "cs", "ms", "table", "oh", "gh"]
     if nz > 1:
         FAR += ["oa", "ob", "oc"]
     return pl.pallas_call(
@@ -1188,20 +1355,17 @@
         o.kvt[...] = o.kv[...].astype(F32)
         o.sa[:, (4 + i) * hs : (5 + i) * hs] = o.kvt[:, i, :].astype(BF)
     n_gain = o.gain.shape[0]
-    o.ext[...] = jnp.zeros(o.ext.shape, F32)
-    o.ext[:n_gain, :rows] = o.gain[...].astype(F32)
-    tall = o.ext[...].T
-    o.wide[...] = tall
-    nb_rows, heads = o.rel.shape
-    o.wide[:nb_rows, REL_AT : REL_AT + heads] = o.rel[...].astype(F32)
-    o.sa[:, 6 * hs :] = o.wide[:rows, :].astype(BF)
+    heads = o.rel.shape[0]
+    o.mf[...] = jnp.zeros(o.mf.shape, F32)
+    o.mf[:n_gain, : o.gain.shape[1]] = o.gain[...].astype(F32)
+    o.mf[CROSS_AT : CROSS_AT + 1, : o.cg.shape[1]] = o.cg[...].astype(F32)
+    o.mf[REL_AT : REL_AT + heads, : o.rel.shape[1]] = o.rel[...].astype(F32)
+    o.sm[...] = o.mf[...].astype(BF)
     o.sx[:, :hs] = o.cq[...]
     o.sx[:, hs : 2 * hs] = o.cw[...].astype(F32).T.astype(BF)
-    half = o.cg.shape[1]
-    o.ext[...] = jnp.zeros(o.ext.shape, F32)
-    o.ext[:1, :half] = o.cg[...].astype(F32)
-    o.wide[...] = o.ext[...].T
-    o.sx[:, 2 * hs :] = o.wide[:half, :].astype(BF)
+    o.ms[...] = jnp.zeros(o.ms.shape, jnp.int32)
+    for r in range(2):
+        o.ms[r, 0:1, :held] = o.ids[r : r + 1, :]
     own = o.seg[section, pl.ds(y, 1), :]
     first = o.seg[0, pl.ds(y, 1), :]
     o.segq[...] = jnp.broadcast_to(own.astype(F32), (8, L)).T[:, :1].astype(jnp.int32)
@@ -1212,37 +1376,37 @@
     o.line[:, HALO : HALO + L] = own
     for b in range(L // qb_rows):
         o.segw[b] = o.line[:, b * qb_rows : b * qb_rows + win_w]
-    at = lax.broadcasted_iota(jnp.int32, (rows, win_w), 0)
-    for k in range(n_dp):
-        same = (at < nb_rows) & (o.win[...] == at + k * nb_rows)
-        o.hotf[k * rows : (k + 1) * rows, :] = jnp.where(same, 1.0, 0.0)
-    o.hot[...] = o.hotf[...].astype(BF)
+    o.win[...] = jnp.full(o.win.shape, -1, jnp.int32)
+    o.win[:, : 2 * HALO] = o.buckets[:, L - HALO : L + HALO]
+    at = lax.broadcasted_iota(jnp.int32, (128, win_w), 0)
+    o.hot[...] = jnp.where(at == o.win[...], 1.0, 0.0).astype(BF)
 
 
 def run_prep(dims, n_dp, given):
     L, D, hs, fs, nz, qb_rows, win_w = dims
     rows, held = D // n_dp, L // 4
+    MW = -(-(D // nz) // 128) * 128
     LBP = -(-held // 16) * 16
     S = jax.ShapeDtypeStruct
     outs = dict(
         xs=S((2, LBP, D), BF),
         cs=S((2, LBP, D), BF),
-        sa=S((rows, 6 * hs + EXT), BF),
-        sx=S((rows // 2, 2 * hs + EXT), BF),
+        sa=S((rows, 6 * hs), BF),
+        sx=S((rows // 2, 2 * hs), BF),
+        sm=S((TILE, MW), BF),
+        ms=S((2, 8, 128), jnp.int32),
         segq=S((L, 1), jnp.int32),
         segw=S((L // qb_rows, 1, win_w), jnp.int32),
         srcseg=S((1, L), jnp.int32),
-        hot=S((D, win_w), BF),
+        hot=S((128, win_w), BF),
     )
     V = pltpu.VMEM
-    up = -(-rows // 128) * 128
     scratch = dict(
         tmp=V((held, 2, D), F32),
         kvt=V((rows, 2, hs), F32),
-        ext=V((EXT, up), F32),
-        wide=V((up, EXT), F32),
+        mf=V((TILE, MW), F32),
         line=V((1, L + 2 * HALO), jnp.int32),
-        hotf=V((D, win_w), F32),
+        win=V((1, win_w), jnp.int32),
     )
     spec = pl.BlockSpec(memory_space=pltpu.VMEM)
     names = list(given) + list(outs) + list(scratch)
@@ -1273,15 +1437,15 @@
     o.so[...] = o.ga[:, 3 * hs : 4 * hs].T
     for i in range(2):
         o.kv[:, i, :] = o.ga[:, (4 + i) * hs : (5 + i) * hs]
-    ext = o.ga[:, 6 * hs :].T
+    rows = o.ga.shape[0]
     for i in range(o.gain.shape[0]):
-        o.gain[i] = ext[i : i + 1]
+        o.gain[i] = o.gm[i : i + 1, :rows]
     heads, _, nb_rows = o.rel.shape
     for i in range(heads):
-        o.rel[i] = ext[REL_AT + i : REL_AT + i + 1, :nb_rows]
+        o.rel[i] = o.gm[REL_AT + i : REL_AT + i + 1, :nb_rows]
     o.cq[...] = o.gx[:, :hs]
     o.co[...] = o.gx[:, hs : 2 * hs].T
-    o.cg[...] = o.gx[:, 2 * hs :].T[:1]
+    o.cg[...] = o.gm[CROSS_AT : CROSS_AT + 1, : rows // 2]
 
 
 def run_finish(dims, rel_shape, sums):
@@ -1306,10 +1470,10 @@
     spec = pl.BlockSpec(memory_space=pltpu.VMEM)
     return pl.pallas_call(
         functools.partial(
-            finish_kernel, dims, ["oh", "gh", "ga", "gb", "gc", "gx", *outs, "tmp"]
+            finish_kernel, dims, ["oh", "gh", "ga", "gb", "gc", "gx", "gm", *outs, "tmp"]
         ),
         out_shape=list(outs.values()),
-        in_specs=[spec] * 6,
+        in_specs=[spec] * 7,
         out_specs=[spec] * len(outs),
         scratch_shapes=[pltpu.VMEM((held, 2, D), F32)],
         compiler_params=pltpu.CompilerParams(vmem_limit_bytes=60 << 20),
@@ -1347,12 +1511,11 @@
     nz = n_dp if (rows // 2) % 32 == 0 else 1
     dims = (L, D, hs, fs, nz, qb_rows, win_w)
     held = L // nt
-    fill = -(-held // 16) * 16 - held
-    ids = jnp.pad(slot_ids.T, ((0, 0), (0, fill)))
-    ms = memory_table.at[ids].get(mode="promise_in_bounds")
-    window = jnp.pad(
-        buckets[L - HALO : L + HALO], (0, win_w - 2 * HALO), constant_values=-1
-    )
+    gain, rel, cross_g = gains[0], rel_bias[0].T, cross_gain[None]
+    if nz != n_dp:
+        gain = lax.all_gather(gain, "dp", axis=1, tiled=True)
+        rel = lax.all_gather(rel, "dp", axis=1, tiled=True)
+        cross_g = lax.all_gather(cross_g, "dp", axis=1, tiled=True)
     prepared = run_prep(
         dims,
         n_dp,
@@ -1362,30 +1525,44 @@
             qkv=self_qkv[0].transpose(1, 0, 2),
             so=self_out[0],
             kv=source_kv[0],
-            gain=gains[0],
-            rel=rel_bias[0],
+            gain=gain,
+            rel=rel,
             cq=cross_query,
             cw=cross_out,
-            cg=cross_gain[None],
+            cg=cross_g,
             seg=segment_ids,
-            win=window[None],
+            ids=slot_ids.T,
+            buckets=buckets[None],
         ),
     )
-    xs, cs, sa, sx, segq, segw, srcseg, hot = prepared
+    xs, cs, sa, sx, sm, ms, segq, segw, srcseg, hot = prepared
     shards = [sa, ff_in[0], ff_out[0].T, sx]
     if nz != n_dp:
         shards = [lax.all_gather(shard, "dp", axis=0, tiled=True) for shard in shards]
     given = dict(
-        xs=xs, cs=cs, ms=ms, segq=segq, segw=segw, srcseg=srcseg, hot=hot,
+        xs=xs, cs=cs, ms=ms, table=memory_table, sm=sm, segq=segq, segw=segw, srcseg=srcseg, hot=hot,
         sa=shards[0], sb=shards[1], sc=shards[2], sx=shards[3],
     )
-    oh, gh, *sums = run_kernel(dims, given)
+    oh, gh, *sums, gm = run_kernel(dims, given)
     if nz != n_dp:
         sums = [
             lax.psum_scatter(full, "dp", scatter_dimension=0, tiled=True).astype(F32)
             for full in sums
         ]
-    done = run_finish(dims, rel_bias.shape[1:], [oh, gh, *sums])
+
+        def share(first, count, width):
+            mine = lax.psum_scatter(
+                gm[first : first + count, :width], "dp", scatter_dimension=1, tiled=True
+            )
+            below = TILE - first - count
+            return jnp.pad(mine, ((first, below), (0, 128 - mine.shape[1])))
+
+        gm = (
+            share(0, CROSS_AT, D)
+            + share(CROSS_AT, 1, D // 2)
+            + share(REL_AT, rel_bias.shape[2], NB)
+        )
+    done = run_finish(dims, rel_bias.shape[1:], [oh, gh, *sums, gm])
     out, gin, qkv, so, kv, rel, gain, cq, co, cg, ff_i, ff_o = done
     return (
         out[None],

time: 300 us -> 281 us (0.937)
  Pallas kernels: 287 us -> 278 us
  local copies, waits for them, and re-layouts: 8.4 us -> 0 us
    pallas_call x1, Pallas kernels: 279 us -> 270 us  [run_kernel(): pl.pallas_call(functools.partial(kernel, dims, names), out_shape=list(out...]
    gather x1 -> x0, local copies, waits for them, and re-layouts: 5.73 us -> none  [body(): ms = memory_table.at[ids].get(mode='promise_in_bounds')]
where the time goes in v4:
time: 281 us; the launch traced here: 279 us
  Pallas kernels  278 us (99%)
    pallas_call x1, Pallas kernels, run_kernel(): pl.pallas_call(functools.partial(kernel, dims, names), out_shape=list(out...  270 us

profile of v4, /device:TPU:9, one launch (start us, length us, event | category | flops | bytes accessed | tf_op | source)
XLA Modules:
  0.0 279.0 jit_solution(10846404101113072026)
XLA Ops:
  0.6 3.7 %prep.1 = (bf16[2,128,768]{2,1,0:T(8,128)(2,1)}, bf16[2,128,768]{2,1,0:T(8,128)(2,1)}, bf16[192,1152]{1,0:T(8,128)(2,1)}, bf16[96,384]{1,0:T(8,128)(2,1)}, bf16[...) custom-call(bf16[120,2,768]{2,1,0:T(2,128)(2,1)} %bitcast.32, ...), custom_call_target="tpu_custom_call" | custom-call | tf_op jit(solution)/shard_map/prep/pallas_call | solution.py:1413
  4.3 270.1 %layers.1 = (bf16[2,128,768]{2,1,0:T(8,128)(2,1)}, f32[2,120,768]{2,1,0:T(8,128)}, f32[192,1152]{1,0:T(8,128)}, f32[192,768]{1,0:T(8,128)}, f32[192,768]{1,0:T(8...) custom-call(bf16[2,128,768]{2,1,0:T(8,128)(2,1)} %get-tuple-element.41.refs_0_, ...), custom_call_target="tpu_custom_call" | custom-call | tf_op jit(solution)/shard_map/layers/pallas_call | solution.py:1324
  274.5 4.4 %finish.1 = (bf16[120,2,768]{2,1,0:T(2,128)(2,1)}, f32[120,2,768]{2,1,0:T(2,128)}, f32[3,192,192]{2,1,0:T(8,128)}, f32[192,192]{1,0:T(8,128)}, f32[192,2,192]{2,...) custom-call(bf16[2,128,768]{2,1,0:T(8,128)(2,1)} %get-tuple-element., ...), custom_call_target="tpu_custom_call" | custom-call | tf_op jit(solution)/shard_map/finish/pallas_call | solution.py:1471

commit v5 on v4

--- a/solution.py
+++ b/solution.py
@@ -84,7 +84,6 @@
     }
     STAGE = {} if nz == 1 else {
         A: o.hidden.at[pl.ds(0, chunk_rows), pl.ds(0, 6 * hs)],
-        B: o.gp.at[pl.ds(0, chunk_rows), pl.ds(0, fs)],
         C: o.gp.at[pl.ds(0, chunk_rows), pl.ds(fs, fs)],
     }
     ROWS = ((o.xs, o.xq), (o.cs, o.cq), (o.ms, o.mq))
@@ -406,27 +405,32 @@
             o.tg.at[slot],
         )
 
-    def pick_rows():
-        n_piece = o.table.shape[0] // PIECE
-        piece(0, 0).start()
-        rows_done(2)
-        for k in range(4):
-            o.idr[:, k * held : (k + 1) * held] = o.mq[k, 0:1, :held]
-        o.gres[...] = jnp.zeros(o.gres.shape, F32)
+    def pick_rows(part):
+        n_piece = o.table.shape[0] // PIECE // 2
+        first = part * n_piece
+        if part == 0:
+            rows_done(2)
+            for k in range(4):
+                o.idr[:, k * held : (k + 1) * held] = o.mq[k, 0:1, :held]
+            o.gres[...] = jnp.zeros(o.gres.shape, F32)
+        piece(first, 0).start()
 
         @pl.loop(0, n_piece)
-        def _(c):
-            slot = lax.rem(c, 2)
-            pl.when(c + 1 < n_piece)(lambda: piece(c + 1, 1 - slot).start())
+        def _(i):
+            c = first + i
+            slot = lax.rem(i, 2)
+            pl.when(i + 1 < n_piece)(lambda: piece(c + 1, 1 - slot).start())
             at = lax.broadcasted_iota(jnp.int32, (PIECE, L), 0) + c * PIECE
             hit = jnp.where(at == o.idr[...], 1.0, 0.0).astype(BF)
             piece(c, slot).wait()
             o.gres[...] += dot_tn(hit, o.exs[slot, :PIECE, :])
 
-        def one(rows):
-            o.nb[rows, :] = o.gres[rows, :].astype(BF)
-
-        rows_loop(one)
+        if part == 1:
+
+            def one(rows):
+                o.nb[rows, :] = o.gres[rows, :].astype(BF)
+
+            rows_loop(one)
 
 
     def rs_y(r, k):
@@ -440,32 +444,133 @@
             beside,
         )
 
-    def rs_z(r, k):
+    mate = z + 1 - 2 * lax.rem(z, 2)
+    far = 2 - 2 * (z // 2)
+    TAKES = (far + lax.rem(mate, 2), mate, far + lax.rem(z, 2), z)
+    GOES = (mate, mate, far + lax.rem(z, 2), z)
+
+    def by_step(i, values):
+        if nz == 1:
+            return z
+        weights = (
+            (1 - i) * (2 - i) * (3 - i) // 6,
+            i * (2 - i) * (3 - i) // 2,
+            i * (i - 1) * (3 - i) // 2,
+            i * (i - 1) * (i - 2) // 6,
+        )
+        return sum(value * weight for value, weight in zip(values, weights))
+
+    def rs_z(r, i):
         g, at, width = REDUCE[r]
         cols = pl.ds(at, width)
-        away = lax.rem(z + nz - 1 - k, nz)
         return remote(
-            RY[g].at[chunk(k), cols],
-            RZ[g].at[away, :, cols],
-            o.rz_s.at[r, k],
-            o.rz_r.at[r, away],
-            (p, k, t),
+            RY[g].at[chunk(by_step(i, TAKES)), cols],
+            RZ[g].at[i, :, cols],
+            o.rz_s.at[r, i],
+            o.rz_r.at[r, i],
+            (p, by_step(i, GOES), t),
         )
-
-    def rs_z_came(r, i):
-        g, at, width = REDUCE[r]
-        cols = pl.ds(at, width)
-        remote(
-            RY[g].at[chunk(z), cols],
-            RZ[g].at[i, :, cols],
-            o.rz_s.at[r, z],
-            o.rz_r.at[r, i],
-            beside,
-        ).wait_recv()
 
     def rs_start(r):
         for i in range(nz):
-            rs_y(r, lax.rem(z + 1 + i, nz)).start()
+            rs_y(r, by_step(i, TAKES)).start()
+
+
+    kv_cols = slice(at_kv, at_ext)
+    kv_lanes = pl.ds(at_kv, 2 * hs)
+
+    def kv_slot(own, i):
+        return RZ[A].at[i, :, kv_lanes] if own else RY[A].at[chunk(i), kv_lanes]
+
+    def kv_z(own, i):
+        a = y if own else 1 - y
+        return remote(
+            W[A].at[a, chunk(TAKES[i]), kv_lanes],
+            kv_slot(own, i),
+            o.kq.at[own, i],
+            o.kq.at[2 + own, i],
+            (p, GOES[i], t),
+        )
+
+    kv_y = remote(
+        W[A].at[1 - y, chunk(z), kv_lanes],
+        RY[A].at[chunk(nz - 1), kv_lanes],
+        o.kq.at[0, nz - 1],
+        o.kq.at[2, nz - 1],
+        beside,
+    )
+
+    def kv_add(k, terms, put):
+        start = pl.multiple_of(k * chunk_rows, 16)
+
+        @pl.loop(0, chunk_rows // 32)
+        def _(n):
+            rows = pl.ds(pl.multiple_of(start + n * 32, 16), 32)
+            near = pl.ds(pl.multiple_of(n * 32, 16), 32)
+            put(rows, near, sum(term(rows, near).astype(F32) for term in terms))
+
+    def kv_term(own, i):
+        if own:
+            return lambda rows, near: RZ[A][i, near, kv_cols]
+        return lambda rows, near: RY[A][
+            pl.ds(pl.multiple_of(i * chunk_rows + near.start, 16), 32), kv_cols
+        ]
+
+    def kv_mine(own):
+        a = y if own else 1 - y
+        return lambda rows, near: W[A][a, rows, kv_cols]
+
+    def kv_keep(own):
+        a = y if own else 1 - y
+
+        def put(rows, near, value):
+            W[A][a, rows, kv_cols] = value.astype(BF)
+
+        return put
+
+    def kv_start(own):
+        if nz > 1:
+            kv_z(own, 0).start()
+            kv_z(own, 1).start()
+
+    def kv_mid():
+        if nz == 1:
+            rs_mid(RK)
+            return
+        for own in (0, 1):
+            kv_z(own, 0).wait_recv()
+            kv_add(TAKES[2], [kv_mine(own), kv_term(own, 0)], kv_keep(own))
+            kv_z(own, 2).start()
+
+    def kv_cross():
+        if nz == 1:
+            return
+        kv_z(0, 1).wait_recv()
+        kv_z(0, 2).wait_recv()
+        kv_add(z, [kv_mine(0), kv_term(0, 1), kv_term(0, 2)], kv_keep(0))
+        kv_y.start()
+
+    def kv_out():
+        if nz == 1:
+            rs_out(RK)
+            return
+        out, buffer, first, into = LEAVE[RK]
+        kv_z(1, 1).wait_recv()
+        kv_z(1, 2).wait_recv()
+        kv_y.wait_recv()
+
+        def put(rows, near, value):
+            to = pl.ds(pl.multiple_of(near.start + first, 16), 32)
+            buffer[to, into : into + 2 * hs] = value
+
+        kv_add(
+            z, [kv_mine(1), kv_term(1, 1), kv_term(1, 2), kv_term(0, nz - 1)], put
+        )
+        rs_leave(RK).start()
+        for own in (0, 1):
+            for i in range(nz - 1):
+                kv_z(own, i).wait_send()
+        kv_y.wait_send()
 
     def rs_mid(r, first=0, last=nz):
         g, at, width = REDUCE[r]
@@ -473,40 +578,54 @@
 
         @pl.loop(min(first, nz), min(last, nz))
         def _(i):
-            k = lax.rem(z + 1 + i, nz)
+            k = by_step(i, TAKES)
             rs_y(r, k).wait_recv()
             start = pl.multiple_of(k * chunk_rows, 16)
 
-            @pl.loop(0, chunk_rows // 32)
-            def _(n):
-                rows = pl.ds(pl.multiple_of(start + n * 32, 16), 32)
-                both = W[g][y, rows, cols].astype(F32) + RY[g][rows, cols].astype(F32)
-                RY[g][rows, cols] = both.astype(BF)
-
-            if nz > 1:
-                pl.when(i < nz - 1)(lambda: rs_z(r, k).start())
+            def add(more):
+                @pl.loop(0, chunk_rows // 32)
+                def _(n):
+                    rows = pl.ds(pl.multiple_of(start + n * 32, 16), 32)
+                    both = W[g][y, rows, cols].astype(F32) + RY[g][rows, cols].astype(F32)
+                    if more:
+                        near = pl.ds(pl.multiple_of(n * 32, 16), 32)
+                        both = both + RZ[g][0, near, cols].astype(F32)
+                    RY[g][rows, cols] = both.astype(BF)
+
+            if nz == 1:
+                add(False)
+                return
+
+            @pl.when(i == 2)
+            def _():
+                rs_z(r, 0).wait_recv()
+                add(True)
+
+            pl.when(i != 2)(lambda: add(False))
+            pl.when(i < nz - 1)(lambda: rs_z(r, i).start())
 
     def rs_end(r, put):
         g, at, width = REDUCE[r]
         cols = slice(at, at + width)
-        for i in range(nz - 1):
-            rs_z_came(r, i)
+        if nz > 1:
+            rs_z(r, 1).wait_recv()
+            rs_z(r, 2).wait_recv()
         start = pl.multiple_of(z * chunk_rows, 16)
 
         @pl.loop(0, chunk_rows // 32)
         def _(n):
             rows = pl.ds(pl.multiple_of(n * 32, 16), 32)
             total = RY[g][pl.ds(pl.multiple_of(start + n * 32, 16), 32), cols].astype(F32)
-            for i in range(nz - 1):
-                total = total + RZ[g][i, rows, cols].astype(F32)
+            if nz > 1:
+                total = total + RZ[g][1, rows, cols].astype(F32)
+                total = total + RZ[g][2, rows, cols].astype(F32)
             put(rows, total)
 
     def rs_sent(r):
         for i in range(nz):
-            k = lax.rem(z + 1 + i, nz)
-            rs_y(r, k).wait_send()
+            rs_y(r, by_step(i, TAKES)).wait_send()
             if i < nz - 1:
-                rs_z(r, k).wait_send()
+                rs_z(r, i).wait_send()
 
     def rs_leave(r):
         g, at, width = REDUCE[r]
@@ -949,7 +1068,9 @@
         def one(a):
             W[A][a, :, at_kv:at_ext] = dot_tn(o.ns[...], o.dkv[a]).astype(BF)
 
-        side_first(one, RK)
+        side_first(one, RK if nz == 1 else None)
+        kv_start(0)
+        kv_start(1)
 
     def dkv_grads():
         for a in range(2):
@@ -962,8 +1083,6 @@
             ),
         )
 
-    tiles_pass()
-    rows_pass(0)
     when(enc, lambda: rows_pass(2))
 
     def first_cross():
@@ -974,29 +1093,37 @@
     when(dec, first_cross)
     ag_hop(A, 1)
     ag_hop(C, 0, False)
+    tiles_pass()
     if STAGE:
         when(dec, lambda: ag_pass_on(A))
     ag_side(C, 0)
-    when(enc, pick_rows)
+    when(enc, lambda: pick_rows(0))
+    when(enc, lambda: pick_rows(1))
     ag_hop(A, 2)
     ag_hop(B, 1, False)
-    if STAGE:
-        when(dec, lambda: ag_pass_on(B))
+    when(enc, lambda: ag_side(B, 1))
     when(dec, lambda: ag_hop(X, 1))
+    rows_pass(0)
     ag_hop(C, 1, False)
     if STAGE:
         when(dec, lambda: ag_pass_on(C))
     ag_hop(A, 3)
+    ag_side(C, 1)
+    ag_hop(B, 2, False)
+    when(enc, lambda: ag_side(B, 2))
     when(dec, lambda: ag_hop(X, 2))
     rows_done(0)
     rows_join(0, o.x)
-    when(dec, lambda: ag_hop(X, 3))
-
-    when(dec, lambda: ag_side(B, 0))
-    ag_side(B, 1)
-    ag_side(C, 1)
-    when(dec, lambda: rows_start(1))
+
+    @pl.when(dec)
+    def _():
+        ag_hop(X, 3)
+        ag_side(B, 0)
+        ag_side(B, 1)
+        ag_side(B, 2)
+
     ag_wait(A)
+    ag_hop(C, 2)
     tiles_done()
     for a in range(2):
         rel_lines = dot(o.rl[a].astype(BF), o.hot[...])
@@ -1022,12 +1149,7 @@
         o.q[:, split(a)] = (o.dqkv[a, :, :hs] * (HD**-0.5)).astype(BF)
         o.kp[HALO : HALO + L, split(a)] = o.dqkv[a, :, hs : 2 * hs]
         o.vp[HALO : HALO + L, split(a)] = o.dqkv[a, :, 2 * hs :]
-    ag_hop(B, 2)
-    hooks = (
-        lambda: ag_hop(C, 2),
-        lambda: ag_hop(B, 3),
-        lambda: ag_hop(C, 3),
-    )
+    hooks = (lambda: ag_hop(B, 3), lambda: ag_hop(C, 3))
 
     @pl.when(enc)
     def _():
@@ -1037,10 +1159,11 @@
 
     @pl.when(dec)
     def _():
+        ag_also_hop(0)
         attn_fwd(o.q, o.mixa, False, True, True, hooks)
-        ag_also_hop(0)
 
     out_project(0, o.mixa, W[A], at_o)
+    when(dec, lambda: rows_start(1))
 
     @pl.when(enc)
     def _():
@@ -1052,7 +1175,6 @@
         ag_finish(X)
         if STAGE:
             ag_relay(A).wait_send()
-            ag_relay(B).wait_send()
             ag_relay(C).wait_send()
 
         def whole(a):
@@ -1071,16 +1193,15 @@
         def one(rows):
             o.ns[rows, :] = normed(o.xbuf[rows, :].astype(F32), 2)
 
+        ag_also_hop(1)
         x_halves(0, one)
         kv_project()
         attn_fwd(o.qb, o.mixb, True, False, False)
-        ag_also_hop(1)
+        ag_also_hop(2)
         out_project(1, o.mixb, o.xg, hs)
         residual(1, o.xmid, keep(o.xlate, 1, o.nc))
-        ag_also_hop(2)
-
-
-    when(dec, lambda: rows_pass(1))
+
+
     ff_fwd()
 
     def put_out(rows, value):
@@ -1093,7 +1214,7 @@
     o.ho[...] = home_block(o.gres, t)
     home_out[0].start()
     ag_finish(A)
-    when(enc, lambda: rows_pass(1))
+    rows_pass(1)
     rows_done(1)
     rows_join(1, o.gres)
 
@@ -1180,18 +1301,12 @@
         lambda rows: sum(dot_nt(o.dqkv[a, rows, :], W[A][a, :, :at_o]) for a in range(2)),
     )
 
-    def own_weights(a):
-        W[A][a, :, :at_o] = dot_tn(o.na[...], o.dqkv[a]).astype(BF)
-
-    side_first(own_weights, RQ)
-
     @pl.when(enc)
     def _():
         def put_source(rows, dv):
             pass
 
         norm_back(2, o.nb, 2, put_source)
-        rs_mid(RB, 0, 2)
 
     heads = 2 * n_pair
     acc = jnp.zeros((heads * 8, win_w), F32)
@@ -1212,21 +1327,25 @@
     home_send(1, o.gres)
     home_out[2].start()
     sums_start(lines)
+
+    def own_weights(a):
+        W[A][a, :, :at_o] = dot_tn(o.na[...], o.dqkv[a]).astype(BF)
+
+    side_first(own_weights, RQ)
+
     home_copy(0).wait()
     home_out[1].start()
-    when(enc, lambda: rs_mid(RB, 2))
-    when(dec, lambda: rs_mid(RB))
-    rs_mid(RK)
+    kv_mid()
+    rs_mid(RB)
     rs_out(RC)
-
-    @pl.when(dec)
-    def _():
-        rs_mid(RX)
-
-    rs_mid(RQ)
+    kv_cross()
+    sums_mid()
+    when(dec, lambda: rs_mid(RX))
+    rs_mid(RQ, 0, 2)
     rs_out(RB)
-    rs_out(RK)
-    sums_mid()
+    sums_end()
+    rs_mid(RQ, 2)
+    kv_out()
 
     @pl.when(dec)
     def _():
@@ -1250,7 +1369,6 @@
     o.ext[...] = o.hr[1].astype(F32)
     home_out[3].start()
     rs_out(RQ)
-    sums_end()
     for copy in home_out:
         copy.wait()
     if nz > 1:
@@ -1309,7 +1427,7 @@
         scratch["z" + g] = V((nz - 1, CR, width) if nz > 1 else (1, 16, width), BF)
     sem = pltpu.SemaphoreType.DMA
     scratch.update(ss=sem((3, 2)), rs=sem((3, 2)), gd=sem((3, 3)), ga=sem((2, nz)), gb2=sem((nz,)), mt=sem((8, nz)), mx=sem((6,)), tg=sem((2,)), xss=sem((2, 2)), xrs=sem((2, 2)))
-    scratch.update(xw=sem((4,)), oc_sem=sem((4,)), lc=sem((6,)), lh=sem((4,)))
+    scratch.update(xw=sem((4,)), oc_sem=sem((4,)), kq=sem((4, nz)), lc=sem((6,)), lh=sem((4,)))
     scratch.update(qs=sem((3, 3)), qr=sem((3, 3)), ql=sem((3,)), hx=sem((2,)), hy=sem((2,)))
     for name in ("gr", "gl", "gs", "gz", "gy"):
         scratch[name] = sem((4, nz))
@@ -1508,7 +1626,7 @@
     fs = ff_in.shape[2]
     qb_rows, win_w = 160, 256
     rows = D // n_dp
-    nz = n_dp if (rows // 2) % 32 == 0 else 1
+    nz = 4 if n_dp == 4 and (rows // 2) % 32 == 0 else 1
     dims = (L, D, hs, fs, nz, qb_rows, win_w)
     held = L // nt
     gain, rel, cross_g = gains[0], rel_bias[0].T, cross_gain[None]

time: 281 us -> 265 us (0.943)
  Pallas kernels: 278 us -> 260 us
    pallas_call x1, Pallas kernels: 270 us -> 252 us  [run_kernel(): pl.pallas_call(functools.partial(kernel, dims, names), out_shape=list(out...]
where the time goes in v5:
time: 265 us; the launch traced here: 261 us
  Pallas kernels  260 us (98%)
    pallas_call x1, Pallas kernels, run_kernel(): pl.pallas_call(functools.partial(kernel, dims, names), out_shape=list(out...  252 us

profile of v5, /device:TPU:9, one launch (start us, length us, event | category | flops | bytes accessed | tf_op | source)
XLA Modules:
  0.0 260.8 jit_solution(6296396564600249871)
XLA Ops:
  0.6 3.7 %prep.1 = (bf16[2,128,768]{2,1,0:T(8,128)(2,1)}, bf16[2,128,768]{2,1,0:T(8,128)(2,1)}, bf16[192,1152]{1,0:T(8,128)(2,1)}, bf16[96,384]{1,0:T(8,128)(2,1)}, bf16[...) custom-call(bf16[120,2,768]{2,1,0:T(2,128)(2,1)} %bitcast.32, ...), custom_call_target="tpu_custom_call" | custom-call | tf_op jit(solution)/shard_map/prep/pallas_call | solution.py:1531
  4.3 252.0 %layers.1 = (bf16[2,128,768]{2,1,0:T(8,128)(2,1)}, f32[2,120,768]{2,1,0:T(8,128)}, f32[192,1152]{1,0:T(8,128)}, f32[192,768]{1,0:T(8,128)}, f32[192,768]{1,0:T(8...) custom-call(bf16[2,128,768]{2,1,0:T(8,128)(2,1)} %get-tuple-element.41.refs_0_, ...), custom_call_target="tpu_custom_call" | custom-call | tf_op jit(solution)/shard_map/layers/pallas_call | solution.py:1442
  256.3 4.4 %finish.1 = (bf16[120,2,768]{2,1,0:T(2,128)(2,1)}, f32[120,2,768]{2,1,0:T(2,128)}, f32[3,192,192]{2,1,0:T(8,128)}, f32[192,192]{1,0:T(8,128)}, f32[192,2,192]{2,...) custom-call(bf16[2,128,768]{2,1,0:T(8,128)(2,1)} %get-tuple-element., ...), custom_call_target="tpu_custom_call" | custom-call | tf_op jit(solution)/shard_map/finish/pallas_call | solution.py:1589

commit v6 on v5

--- a/solution.py
+++ b/solution.py
@@ -405,32 +405,27 @@
             o.tg.at[slot],
         )
 
-    def pick_rows(part):
-        n_piece = o.table.shape[0] // PIECE // 2
-        first = part * n_piece
-        if part == 0:
-            rows_done(2)
-            for k in range(4):
-                o.idr[:, k * held : (k + 1) * held] = o.mq[k, 0:1, :held]
-            o.gres[...] = jnp.zeros(o.gres.shape, F32)
-        piece(first, 0).start()
+    def pick_rows():
+        n_piece = o.table.shape[0] // PIECE
+        piece(0, 0).start()
+        rows_done(2)
+        for k in range(4):
+            o.idr[:, k * held : (k + 1) * held] = o.mq[k, 0:1, :held]
+        o.gres[...] = jnp.zeros(o.gres.shape, F32)
 
         @pl.loop(0, n_piece)
-        def _(i):
-            c = first + i
-            slot = lax.rem(i, 2)
-            pl.when(i + 1 < n_piece)(lambda: piece(c + 1, 1 - slot).start())
+        def _(c):
+            slot = lax.rem(c, 2)
+            pl.when(c + 1 < n_piece)(lambda: piece(c + 1, 1 - slot).start())
             at = lax.broadcasted_iota(jnp.int32, (PIECE, L), 0) + c * PIECE
             hit = jnp.where(at == o.idr[...], 1.0, 0.0).astype(BF)
             piece(c, slot).wait()
             o.gres[...] += dot_tn(hit, o.exs[slot, :PIECE, :])
 
-        if part == 1:
-
-            def one(rows):
-                o.nb[rows, :] = o.gres[rows, :].astype(BF)
-
-            rows_loop(one)
+        def one(rows):
+            o.nb[rows, :] = o.gres[rows, :].astype(BF)
+
+        rows_loop(one)
 
 
     def rs_y(r, k):
@@ -759,20 +754,23 @@
     def half_rows(h):
         return pl.ds(pl.multiple_of(h * half, 16), half)
 
-    def half_loop(h, fn):
-        @pl.loop(0, half // RT)
-        def _(i):
-            fn(pl.ds(pl.multiple_of(h * half + i * RT, 16), RT))
-
-    def halves(fn, ready=None, after=None):
+    def tile_rows(h, j):
+        return pl.ds(pl.multiple_of(h * half + j * RT, 16), RT)
+
+    def halves(fn, ready=None, before=None, after=None):
         @pl.loop(0, 2)
         def _(i):
             h = lax.rem(core + i, 2)
             if ready is not None:
                 ready(i, h)
-            half_loop(h, fn)
-            if after is not None:
-                pl.when(i == 0)(after)
+
+            @pl.loop(0, half // RT)
+            def _(j):
+                if before is not None:
+                    before(i, h, j)
+                fn(tile_rows(h, j))
+                if after is not None:
+                    pl.when(i == 0)(lambda: after(j))
 
     def normed(v, gain_no):
         r = lax.rsqrt(jnp.mean(v * v, axis=-1, keepdims=True) + EPSILON)
@@ -808,7 +806,7 @@
         def one(rows):
             put(rows, base_ref[rows, :].astype(F32) + ex_rows(slot, rows))
 
-        halves(one, arrived(slot), after)
+        halves(one, arrived(slot), after=after)
 
     def keep(ref, gain_no=None, normed_ref=None):
         def put(rows, value):
@@ -831,7 +829,7 @@
             put(rows, r * (dhg - n * mu))
             o.dgacc[gain_no] += jnp.sum((dh * n).reshape(RT // 8, 8, D), axis=0)
 
-        halves(one, arrived(slot), after)
+        halves(one, arrived(slot), after=after)
 
     def split(a):
         return slice(a * hs, (a + 1) * hs)
@@ -1042,27 +1040,39 @@
 
         norm_back(0, o.xlate, 1, put)
 
-    def x_copy(way):
-        rows = half_rows(core)
+    n_tile = half // RT
+
+    def x_copy(way, j):
+        rows = tile_rows(core, j)
         return remote(
-            o.xsend.at[rows], o.xbuf.at[rows], o.xss.at[way, 0], o.xrs.at[way, 0], across
+            o.xsend.at[rows], o.xbuf.at[rows], o.xss.at[way, 0, j], o.xrs.at[way, 0, j], across
         )
 
-    def x_pass(way, h):
-        rows = half_rows(h)
+    def x_pass(way, h, j):
+        rows = tile_rows(h, j)
         return remote(
-            o.xbuf.at[rows], o.xbuf.at[rows], o.xss.at[way, 1], o.xrs.at[way, 1], sibling
+            o.xbuf.at[rows], o.xbuf.at[rows], o.xss.at[way, 1, j], o.xrs.at[way, 1, j], sibling
         )
 
+    def x_sent(way):
+        @pl.loop(0, n_tile)
+        def _(j):
+            x_copy(way, j).wait_send()
+
     def x_halves(way, fn):
-        x_copy(way).wait_recv()
-        x_pass(way, core).start()
-
-        def ready(i, h):
-            pl.when(i == 1)(lambda: x_pass(way, h).wait_recv())
-
-        halves(fn, ready)
-        x_pass(way, core).wait_send()
+        def before(i, h, j):
+            @pl.when(i == 0)
+            def _():
+                x_copy(way, j).wait_recv()
+                x_pass(way, h, j).start()
+
+            pl.when(i == 1)(lambda: x_pass(way, h, j).wait_recv())
+
+        halves(fn, before=before)
+
+        @pl.loop(0, n_tile)
+        def _(j):
+            x_pass(way, core, j).wait_send()
 
     def kv_weights():
         def one(a):
@@ -1097,8 +1107,7 @@
     if STAGE:
         when(dec, lambda: ag_pass_on(A))
     ag_side(C, 0)
-    when(enc, lambda: pick_rows(0))
-    when(enc, lambda: pick_rows(1))
+    when(enc, pick_rows)
     ag_hop(A, 2)
     ag_hop(B, 1, False)
     when(enc, lambda: ag_side(B, 1))
@@ -1208,7 +1217,7 @@
         o.gres[rows, :] = value
         o.xsend[rows, :] = value.astype(BF)
 
-    residual(2, o.xlate, put_out, lambda: pl.when(enc)(lambda: x_copy(0).start()))
+    residual(2, o.xlate, put_out, lambda j: pl.when(enc)(lambda: x_copy(0, j).start()))
     when(enc, lambda: rows_start(1))
     home_send(0, o.gres)
     o.ho[...] = home_block(o.gres, t)
@@ -1221,7 +1230,7 @@
     @pl.when(enc)
     def _():
         o.dgacc[3] = jnp.zeros((8, D), F32)
-        x_copy(0).wait_send()
+        x_sent(0)
 
         def one(rows):
             value = o.gres[rows, :] + o.xbuf[rows, :].astype(F32)
@@ -1247,7 +1256,7 @@
         def put_source(rows, dv):
             o.xsend[rows, :] = dv.astype(BF)
 
-        norm_back(2, o.xbuf, 2, put_source, lambda: x_copy(1).start())
+        norm_back(2, o.xbuf, 2, put_source, lambda j: x_copy(1, j).start())
         rs_mid(RC, 0, 2)
 
         def put_mid(rows, dv):
@@ -1257,10 +1266,14 @@
 
         norm_back(1, o.xmid, 3, put_mid)
         for a in range(2):
+            o.dqkv[a, :, :hs] = o.dq[:, split(a)]
+            o.dqkv[a, :, hs : 2 * hs] = o.mixb[:, split(a)]
+
+        def cross_weights(a):
             full = jnp.concatenate(
                 [
-                    dot_tn(o.nb[...], o.dq[:, split(a)]).astype(BF),
-                    dot_tn(o.gb[...], o.mixb[:, split(a)]).astype(BF),
+                    dot_tn(o.nb[...], o.dqkv[a, :, :hs]).astype(BF),
+                    dot_tn(o.gb[...], o.dqkv[a, :, hs : 2 * hs]).astype(BF),
                 ],
                 axis=1,
             )
@@ -1269,8 +1282,10 @@
                     at = part * (D // 2) + k * cross_rows
                     to = k * chunk_rows + part * cross_rows
                     W[X][a, to : to + cross_rows, :] = full[at : at + cross_rows]
+
+        both_shards(cross_weights)
         rs_start(RX)
-        x_copy(1).wait_send()
+        x_sent(1)
         o.gb[...] = o.xbuf[...]
 
     ff_in_weights()
@@ -1426,7 +1441,7 @@
         scratch["y" + g] = V((D, width), BF)
         scratch["z" + g] = V((nz - 1, CR, width) if nz > 1 else (1, 16, width), BF)
     sem = pltpu.SemaphoreType.DMA
-    scratch.update(ss=sem((3, 2)), rs=sem((3, 2)), gd=sem((3, 3)), ga=sem((2, nz)), gb2=sem((nz,)), mt=sem((8, nz)), mx=sem((6,)), tg=sem((2,)), xss=sem((2, 2)), xrs=sem((2, 2)))
+    scratch.update(ss=sem((3, 2)), rs=sem((3, 2)), gd=sem((3, 3)), ga=sem((2, nz)), gb2=sem((nz,)), mt=sem((8, nz)), mx=sem((6,)), tg=sem((2,)), xss=sem((2, 2, L // 2 // RT)), xrs=sem((2, 2, L // 2 // RT)))
     scratch.update(xw=sem((4,)), oc_sem=sem((4,)), kq=sem((4, nz)), lc=sem((6,)), lh=sem((4,)))
     scratch.update(qs=sem((3, 3)), qr=sem((3, 3)), ql=sem((3,)), hx=sem((2,)), hy=sem((2,)))
     for name in ("gr", "gl", "gs", "gz", "gy"):

time: 265 us -> 263 us (level)
  no operation moved by 1% of the time
where the time goes in v6:
time: 263 us; the launch traced here: 259 us
  Pallas kernels  258 us (98%)
    pallas_call x1, Pallas kernels, run_kernel(): pl.pallas_call(functools.partial(kernel, dims, names), out_shape=list(out...  250 us

profile of v6, /device:TPU:9, one launch (start us, length us, event | category | flops | bytes accessed | tf_op | source)
XLA Modules:
  0.0 258.8 jit_solution(1519790250685103351)
XLA Ops:
  0.6 3.7 %prep.1 = (bf16[2,128,768]{2,1,0:T(8,128)(2,1)}, bf16[2,128,768]{2,1,0:T(8,128)(2,1)}, bf16[192,1152]{1,0:T(8,128)(2,1)}, bf16[96,384]{1,0:T(8,128)(2,1)}, bf16[...) custom-call(bf16[120,2,768]{2,1,0:T(2,128)(2,1)} %bitcast.32, ...), custom_call_target="tpu_custom_call" | custom-call | tf_op jit(solution)/shard_map/prep/pallas_call | solution.py:1546
  4.3 250.0 %layers.1 = (bf16[2,128,768]{2,1,0:T(8,128)(2,1)}, f32[2,120,768]{2,1,0:T(8,128)}, f32[192,1152]{1,0:T(8,128)}, f32[192,768]{1,0:T(8,128)}, f32[192,768]{1,0:T(8...) custom-call(bf16[2,128,768]{2,1,0:T(8,128)(2,1)} %get-tuple-element.41.refs_0_, ...), custom_call_target="tpu_custom_call" | custom-call | tf_op jit(solution)/shard_map/layers/pallas_call | solution.py:1457
  254.3 4.4 %finish.1 = (bf16[120,2,768]{2,1,0:T(2,128)(2,1)}, f32[120,2,768]{2,1,0:T(2,128)}, f32[3,192,192]{2,1,0:T(8,128)}, f32[192,192]{1,0:T(8,128)}, f32[192,2,192]{2,...) custom-call(bf16[2,128,768]{2,1,0:T(8,128)(2,1)} %get-tuple-element., ...), custom_call_target="tpu_custom_call" | custom-call | tf_op jit(solution)/shard_map/finish/pallas_call | solution.py:1604

commit v7 on v6

--- a/solution.py
+++ b/solution.py
@@ -1350,8 +1350,9 @@
 
     home_copy(0).wait()
     home_out[1].start()
+    rs_mid(RB, 0, 2)
     kv_mid()
-    rs_mid(RB)
+    rs_mid(RB, 2)
     rs_out(RC)
     kv_cross()
     sums_mid()

time: 263 us -> 263 us (level)
  no operation moved by 1% of the time
where the time goes in v7:
time: 263 us; the launch traced here: 259 us
  Pallas kernels  258 us (98%)
    pallas_call x1, Pallas kernels, run_kernel(): pl.pallas_call(functools.partial(kernel, dims, names), out_shape=list(out...  250 us

profile of v7, /device:TPU:9, one launch (start us, length us, event | category | flops | bytes accessed | tf_op | source)
XLA Modules:
  0.0 258.8 jit_solution(9870953286876150156)
XLA Ops:
  0.6 3.7 %prep.1 = (bf16[2,128,768]{2,1,0:T(8,128)(2,1)}, bf16[2,128,768]{2,1,0:T(8,128)(2,1)}, bf16[192,1152]{1,0:T(8,128)(2,1)}, bf16[96,384]{1,0:T(8,128)(2,1)}, bf16[...) custom-call(bf16[120,2,768]{2,1,0:T(2,128)(2,1)} %bitcast.32, ...), custom_call_target="tpu_custom_call" | custom-call | tf_op jit(solution)/shard_map/prep/pallas_call | solution.py:1547
  4.3 249.9 %layers.1 = (bf16[2,128,768]{2,1,0:T(8,128)(2,1)}, f32[2,120,768]{2,1,0:T(8,128)}, f32[192,1152]{1,0:T(8,128)}, f32[192,768]{1,0:T(8,128)}, f32[192,768]{1,0:T(8...) custom-call(bf16[2,128,768]{2,1,0:T(8,128)(2,1)} %get-tuple-element.41.refs_0_, ...), custom_call_target="tpu_custom_call" | custom-call | tf_op jit(solution)/shard_map/layers/pallas_call | solution.py:1458
  254.2 4.4 %finish.1 = (bf16[120,2,768]{2,1,0:T(2,128)(2,1)}, f32[120,2,768]{2,1,0:T(2,128)}, f32[3,192,192]{2,1,0:T(8,128)}, f32[192,192]{1,0:T(8,128)}, f32[192,2,192]{2,...) custom-call(bf16[2,128,768]{2,1,0:T(8,128)(2,1)} %get-tuple-element., ...), custom_call_target="tpu_custom_call" | custom-call | tf_op jit(solution)/shard_map/finish/pallas_call | solution.py:1605
